TPU v7x, 128 devices: a whole 4x4x4 slice. The times are simulated.
128 devices in a mesh: prow: 4 (over z), pcol: 32 (over x, y, core).
Axes of the slice: x: 4, y: 4, z: 4, core: 2. Of those that a mesh axis runs over, the one named last changes fastest.
Arguments:
- right_side: float32 [4, 32, 256, 128], P('prow', 'pcol'), may hold values from -6 to 6
- factor_tiles: bfloat16 [4, 32, 128, 256, 256], P(None, 'pcol', 'prow'), may hold values from -0.03125 to 0.03125
- tile_scales: float32 [4, 32, 128], P(None, 'pcol', 'prow'), may hold values from 0.25 to 4
- tile_pattern: int32 [4, 32, 128], P(None, 'pcol', 'prow'), may hold values from 0 to 1, as said below
- parent: int32 [128], replicated, may hold values from 0 to 128, as said below
- inverses: bfloat16 [2, 4, 32, 256, 256], P(None, 'prow', 'pcol'), may hold values from -3 to 3
Outputs:
- forward: float32 [4, 32, 256, 128], P('prow', 'pcol')
- solution: float32 [4, 32, 256, 128], P('prow', 'pcol')
Inputs may be any that keep to these rules, and one draw needn't show every extreme that they name: A panel of depth d > 0 has as parent a panel of depth d - 1; roots have parent 128; every depth from 0 to 3 occurs. `tile_pattern`: tile_pattern_ij is 1 only where panel i is an ancestor of panel j or panel j an ancestor of panel i in the tree given by parent.
All inputs are finite; a program needn't handle non-finite values.
Results may differ from a plain program's by a relative error of at most 0.0023.
Values may be sent and summed in bfloat16 or wider, within the bound.
No kernel may reach another device: no remote copies, remote signals or barrier semaphores. Data moves between devices by JAX's collectives and lax.ppermute only.
A program may use at most 64 MiB of HBM per device.

v0:
```python
import jax
import jax.numpy as jnp
from jax import lax
from jax.sharding import PartitionSpec as P

DEPTH = 4


def depth_table(parent, levels_count):
    number = parent.shape[0]
    matches = parent[:, None] == jnp.arange(number, dtype=jnp.int32)[None, :]
    depths = jnp.zeros((number,), jnp.int32)
    for repeat in range(levels_count - 1):
        depths = jnp.sum(jnp.where(matches, depths[None, :] + 1, 0), axis=1)
    return depths


def apply_inverse(inverse, vectors):
    return jnp.dot(inverse.astype(jnp.float32), vectors, precision=lax.Precision.HIGHEST)


def refine(target, inverse, weights, panels, solved, prow_at):
    rounded = solved.astype(jnp.bfloat16)[None]
    product = jnp.einsum(
        "aqkl,qlr->aqkr",
        panels,
        lax.all_gather(rounded, "pcol", axis=0, tiled=True),
        preferred_element_type=jnp.float32,
    )
    partial_rows = jnp.sum(weights[:, :, None, None] * product, axis=1)
    summed = lax.psum(partial_rows, "prow")
    own_sum = lax.dynamic_index_in_dim(summed, prow_at, 0, keepdims=False)
    return apply_inverse(inverse, target - own_sum)


def shards(right_side, factor_tiles, tile_scales, tile_pattern, parent, inverses):
    row_count = lax.axis_size("prow")
    col_count = lax.axis_size("pcol")
    prow_at = lax.axis_index("prow")
    pcol_at = lax.axis_index("pcol")
    depths = depth_table(parent, DEPTH)
    depth_rows = lax.dynamic_index_in_dim(
        depths.reshape(row_count, col_count), pcol_at, 1, keepdims=False
    )
    depth_cols = lax.dynamic_slice_in_dim(depths, prow_at * col_count, col_count)
    kept_weight = tile_scales[:, 0] * (tile_pattern[:, 0] == 1).astype(jnp.float32)
    lower_weight = kept_weight * (depth_cols[None, :] > depth_rows[:, None]).astype(jnp.float32)
    upper_weight = kept_weight * (depth_cols[None, :] < depth_rows[:, None]).astype(jnp.float32)
    panels = factor_tiles[:, 0]
    target = right_side[0, 0]
    forward = apply_inverse(inverses[0, 0, 0], target)
    for repeat in range(DEPTH - 1):
        forward = refine(target, inverses[0, 0, 0], lower_weight, panels, forward, prow_at)
    solution = apply_inverse(inverses[1, 0, 0], forward)
    for repeat in range(DEPTH - 1):
        solution = refine(forward, inverses[1, 0, 0], upper_weight, panels, solution, prow_at)
    return (forward[None, None], solution[None, None])


def solution(mesh):
    in_specs = (
        P("prow", "pcol", None, None),
        P(None, "pcol", "prow", None, None),
        P(None, "pcol", "prow"),
        P(None, "pcol", "prow"),
        P(),
        P(None, "prow", "pcol", None, None),
    )
    out_specs = (P("prow", "pcol", None, None), P("prow", "pcol", None, None))
    return jax.shard_map(shards, mesh=mesh, in_specs=in_specs, out_specs=out_specs, check_vma=False)
```

profile of v0, /device:TPU:0, one launch (start us, length us, event | category | flops | bytes accessed | tf_op | source)
XLA Modules:
  0.0 636.0 jit_solution(12399871697980114675)
XLA Ops:
  7.2 1.9 convolution_convert_fusion.5
  9.2 0.8 select_reduce_fusion.2
  10.0 0.8 select_reduce_fusion.1
  10.9 0.8 select_reduce_fusion
  11.7 0.1 reshape.98
  11.8 0.2 dynamic-slice_reduce_fusion
  12.0 0.7 compare_select_fusion
  12.8 0.1 copy.75
  12.9 44.1 %all-gather.13.cloned.1.call-done = bf16[8192,128]{1,0:T(8,128)(2,1)} async-done(((bf16[256,128]{1,0:T(8,128)(2,1)}), bf16[8192,128]{1,0:T(8,128)(2,1)}) %all-gather.13.cloned.1.call-update) | async-done | bytes 2097168 | tf_op jit(solution)/shard_map/all_gather | solution.py:27
  57.0 10.9 %fusion.5 = f32[4,256,128]{1,2,0:T(8,128)} fusion(bf16[32,256,128,1]{2,1,3,0:T(8,128)(2,1)} %bitcast.176, f32[4,32]{0,1:T(8,128)S(1)} %copy.75, bf16[4,1,32,256,256]{4,3,2,1,0:T(8,128)(2,1)} %param.7), kind=kOutput, calls=%fused_computation.11 | convolution fusion | flops 2155741184 | bytes 19399168 | tf_op jit(solution)/shard_map/aqkl,qlr->aqkr/dot_general | solution.py:24
  68.1 42.6 %all-reduce.7.cloned.1.call-done = f32[4,256,128]{1,2,0:T(8,128)} async-done(((f32[4,256,128]{1,2,0:T(8,128)}), f32[4,256,128]{1,2,0:T(8,128)}) %all-reduce.7.cloned.1.call-update) | async-done | bytes 524304 | tf_op jit(solution)/shard_map/psum | solution.py:31
  110.7 0.9 constant_dynamic-slice_fusion.2
  111.6 0.1 copy.78
  111.7 0.9 fusion.17
  112.7 45.8 %all-gather.15.cloned.1.call-done = bf16[8192,128]{0,1:T(8,128)(2,1)} async-done(((bf16[256,128]{0,1:T(8,128)(2,1)}), bf16[8192,128]{0,1:T(8,128)(2,1)}) %all-gather.15.cloned.1.call-update) | async-done | bytes 2097168 | tf_op jit(solution)/shard_map/all_gather | solution.py:27
  158.5 2.2 copy.112
  160.7 10.4 %fusion.4 = f32[4,256,128]{1,2,0:T(8,128)} fusion(f32[4,32]{0,1:T(8,128)S(1)} %copy.75, bf16[32,256,128,1]{1,0,2,3:T(8,128)(2,1)S(1)} %bitcast.172, bf16[4,1,32,256,256]{4,3,2,1,0:T(8,128)(2,1)} %param.7), kind=kOutput, calls=%fused_computation.9 | convolution fusion | flops 2155741184 | bytes 19399168 | tf_op jit(solution)/shard_map/aqkl,qlr->aqkr/dot_general | solution.py:24
  171.2 42.8 %all-reduce.9.cloned.1.call-done = f32[4,256,128]{1,2,0:T(8,128)} async-done(((f32[4,256,128]{1,2,0:T(8,128)}), f32[4,256,128]{1,2,0:T(8,128)}) %all-reduce.9.cloned.1.call-update) | async-done | bytes 524304 | tf_op jit(solution)/shard_map/psum | solution.py:31
  214.0 0.9 constant_dynamic-slice_fusion.1
  214.9 0.1 copy.81
  215.0 0.9 fusion.18
  216.0 45.6 %all-gather.17.cloned.1.call-done = bf16[8192,128]{0,1:T(8,128)(2,1)} async-done(((bf16[256,128]{0,1:T(8,128)(2,1)}), bf16[8192,128]{0,1:T(8,128)(2,1)}) %all-gather.17.cloned.1.call-update) | async-done | bytes 2097168 | tf_op jit(solution)/shard_map/all_gather | solution.py:27
  261.7 2.2 copy.113
  263.9 10.4 %fusion.3 = f32[4,256,128]{1,2,0:T(8,128)} fusion(f32[4,32]{0,1:T(8,128)S(1)} %copy.75, bf16[32,256,128,1]{1,0,2,3:T(8,128)(2,1)S(1)} %bitcast.170, bf16[4,1,32,256,256]{4,3,2,1,0:T(8,128)(2,1)} %param.7), kind=kOutput, calls=%fused_computation.7 | convolution fusion | flops 2155741184 | bytes 19399168 | tf_op jit(solution)/shard_map/aqkl,qlr->aqkr/dot_general | solution.py:24
  274.3 42.8 %all-reduce.11.cloned.1.call-done = f32[4,256,128]{1,2,0:T(8,128)} async-done(((f32[4,256,128]{1,2,0:T(8,128)}), f32[4,256,128]{1,2,0:T(8,128)}) %all-reduce.11.cloned.1.call-update) | async-done | bytes 524304 | tf_op jit(solution)/shard_map/psum | solution.py:31
  317.2 0.9 constant_dynamic-slice_fusion
  318.1 0.1 copy.84
  318.2 0.3 fusion.29
  318.5 0.9 fusion.19
  319.5 0.2 all-reduce.13.cloned.1.call-start
  319.7 0.1 copy.85
  319.8 45.2 %all-gather.19.cloned.1.call-done = bf16[8192,128]{0,1:T(8,128)(2,1)} async-done(((bf16[256,128]{0,1:T(8,128)(2,1)}), bf16[8192,128]{0,1:T(8,128)(2,1)}) %all-gather.19.cloned.1.call-update) | async-done | bytes 2097168 | tf_op jit(solution)/shard_map/all_gather | solution.py:27
  365.0 2.2 copy.114
  367.2 10.4 %fusion.2 = f32[4,256,128]{1,2,0:T(8,128)} fusion(f32[4,32]{0,1:T(8,128)S(1)} %copy.85, bf16[32,256,128,1]{1,0,2,3:T(8,128)(2,1)S(1)} %bitcast.173, bf16[4,1,32,256,256]{4,3,2,1,0:T(8,128)(2,1)} %param.7), kind=kOutput, calls=%fused_computation.5 | convolution fusion | flops 2155741184 | bytes 19399168 | tf_op jit(solution)/shard_map/aqkl,qlr->aqkr/dot_general | solution.py:24
  377.7 42.8 %all-reduce.13.cloned.1.call-done = f32[4,256,128]{1,2,0:T(8,128)} async-done(((f32[4,256,128]{1,2,0:T(8,128)}), f32[4,256,128]{1,2,0:T(8,128)}) %all-reduce.13.cloned.1.call-update) | async-done | bytes 524304 | tf_op jit(solution)/shard_map/psum | solution.py:31
  420.5 1.8 fusion.20
  422.4 45.9 %all-gather.21.cloned.1.call-done = bf16[8192,128]{0,1:T(8,128)(2,1)} async-done(((bf16[256,128]{0,1:T(8,128)(2,1)}), bf16[8192,128]{0,1:T(8,128)(2,1)}) %all-gather.21.cloned.1.call-update) | async-done | bytes 2097168 | tf_op jit(solution)/shard_map/all_gather | solution.py:27
  468.3 2.2 copy.115
  470.5 10.4 %fusion.1 = f32[4,256,128]{1,2,0:T(8,128)} fusion(f32[4,32]{0,1:T(8,128)S(1)} %copy.85, bf16[32,256,128,1]{1,0,2,3:T(8,128)(2,1)S(1)} %bitcast.174, bf16[4,1,32,256,256]{4,3,2,1,0:T(8,128)(2,1)} %param.7), kind=kOutput, calls=%fused_computation.3 | convolution fusion | flops 2155741184 | bytes 19399168 | tf_op jit(solution)/shard_map/aqkl,qlr->aqkr/dot_general | solution.py:24
  481.0 42.8 %all-reduce.15.cloned.1.call-done = f32[4,256,128]{1,2,0:T(8,128)} async-done(((f32[4,256,128]{1,2,0:T(8,128)}), f32[4,256,128]{1,2,0:T(8,128)}) %all-reduce.15.cloned.1.call-update) | async-done | bytes 524304 | tf_op jit(solution)/shard_map/psum | solution.py:31
  523.8 1.8 fusion.21
  525.8 45.9 %all-gather.23.cloned.1.call-done = bf16[8192,128]{0,1:T(8,128)(2,1)} async-done(((bf16[256,128]{0,1:T(8,128)(2,1)}), bf16[8192,128]{0,1:T(8,128)(2,1)}) %all-gather.23.cloned.1.call-update) | async-done | bytes 2097168 | tf_op jit(solution)/shard_map/all_gather | solution.py:27
  571.7 2.2 copy.116
  573.9 10.4 %fusion = f32[4,256,128]{1,2,0:T(8,128)} fusion(f32[4,32]{0,1:T(8,128)S(1)} %copy.85, bf16[32,256,128,1]{1,0,2,3:T(8,128)(2,1)S(1)} %bitcast.171, bf16[4,1,32,256,256]{4,3,2,1,0:T(8,128)(2,1)} %param.7), kind=kOutput, calls=%fused_computation.1 | convolution fusion | flops 2155741184 | bytes 19399168 | tf_op jit(solution)/shard_map/aqkl,qlr->aqkr/dot_general | solution.py:24
  584.3 0.8 copy.92
  585.1 42.1 %all-reduce.17.cloned.1.call-done = f32[4,256,128]{1,2,0:T(8,128)} async-done(((f32[4,256,128]{1,2,0:T(8,128)}), f32[4,256,128]{1,2,0:T(8,128)}) %all-reduce.17.cloned.1.call-update) | async-done | bytes 524304 | tf_op jit(solution)/shard_map/psum | solution.py:31
  627.2 1.2 convolution_bitcast_fusion
  628.4 0.8 copy.93
  (31 shorter events, 0.8 us)
Async XLA Ops:
  7.2 49.9 %all-gather.13.cloned.1.call-start = ((), (), s32[]{:S(2)}) async-start(), calls=%async_computation.6 | async-start | bytes 2162688 | tf_op jit(solution)/shard_map/all_gather | solution.py:27
  9.1 101.6 %all-reduce.7.cloned.1.call-start = ((), (), s32[]{:S(2)}) async-start(), calls=%async_computation | async-start | bytes 1048576 | tf_op jit(solution)/shard_map/psum | solution.py:31
  57.0 54.7 %copy-start = (bf16[2,1,1,256,256]{4,3,2,1,0:T(8,128)(2,1)S(1)}, bf16[2,1,1,256,256]{4,3,2,1,0:T(8,128)(2,1)}, u32[]{:S(2)}) copy-start(bf16[2,1,1,256,256]{4,3,2,1,0:T(8,128)(2,1)} %param.11) | copy-start | bytes 786436
  57.0 54.7 %copy-start.1 = (f32[1,1,256,128]{3,2,1,0:T(8,128)S(1)}, f32[1,1,256,128]{3,2,1,0:T(8,128)}, u32[]{:S(2)}) copy-start(f32[1,1,256,128]{3,2,1,0:T(8,128)} %param.6) | copy-start | bytes 393220
  68.0 90.5 %all-gather.15.cloned.1.call-start = ((), (), s32[]{:S(2)}) async-start(), calls=%async_computation.7 | async-start | bytes 2162688 | tf_op jit(solution)/shard_map/all_gather | solution.py:27
  112.7 101.3 %all-reduce.9.cloned.1.call-start = ((), (), s32[]{:S(2)}) async-start(), calls=%async_computation.1 | async-start | bytes 1048576 | tf_op jit(solution)/shard_map/psum | solution.py:31
  171.1 90.5 %all-gather.17.cloned.1.call-start = ((), (), s32[]{:S(2)}) async-start(), calls=%async_computation.8 | async-start | bytes 2162688 | tf_op jit(solution)/shard_map/all_gather | solution.py:27
  216.0 101.2 %all-reduce.11.cloned.1.call-start = ((), (), s32[]{:S(2)}) async-start(), calls=%async_computation.2 | async-start | bytes 1048576 | tf_op jit(solution)/shard_map/psum | solution.py:31
  274.3 90.7 %all-gather.19.cloned.1.call-start = ((), (), s32[]{:S(2)}) async-start(), calls=%async_computation.9 | async-start | bytes 2162688 | tf_op jit(solution)/shard_map/all_gather | solution.py:27
  319.5 101.1 %all-reduce.13.cloned.1.call-start = ((), (), s32[]{:S(2)}) async-start(), calls=%async_computation.3 | async-start | bytes 1048576 | tf_op jit(solution)/shard_map/psum | solution.py:31
  377.6 90.7 %all-gather.21.cloned.1.call-start = ((), (), s32[]{:S(2)}) async-start(), calls=%async_computation.10 | async-start | bytes 2162688 | tf_op jit(solution)/shard_map/all_gather | solution.py:27
  422.4 101.5 %all-reduce.15.cloned.1.call-start = ((), (), s32[]{:S(2)}) async-start(), calls=%async_computation.4 | async-start | bytes 1048576 | tf_op jit(solution)/shard_map/psum | solution.py:31
  481.0 90.7 %all-gather.23.cloned.1.call-start = ((), (), s32[]{:S(2)}) async-start(), calls=%async_computation.11 | async-start | bytes 2162688 | tf_op jit(solution)/shard_map/all_gather | solution.py:27
  525.7 101.5 %all-reduce.17.cloned.1.call-start = ((), (), s32[]{:S(2)}) async-start(), calls=%async_computation.5 | async-start | bytes 1048576 | tf_op jit(solution)/shard_map/psum | solution.py:31
Sparse Core Ops, SparseCore 0:
  10.8 46.1 all-gather.12
  68.1 42.5 all-reduce.6
  113.5 45.0 all-gather.14
  171.3 42.7 all-reduce.8
  216.6 45.0 all-gather.16
  274.4 42.7 all-reduce.10
  319.9 45.0 all-gather.18
  377.8 42.7 all-reduce.12
  423.3 45.0 all-gather.20
  481.1 42.7 all-reduce.14
  526.6 45.0 all-gather.22
  584.4 42.7 all-reduce.16
where the time goes:
time: 636 us
  waiting for transfers between devices  529 us (83%)
  matrix products  72.9 us (11%)
  local copies, waits for them, and re-layouts  15.9 us (2%)
  between operations  14.4 us (2%)
    all_gather x6, waiting for transfers between devices, refine(): lax.all_gather(rounded, 'pcol', axis=0, tiled=True)  273 us
    psum x6, waiting for transfers between devices, refine(): summed = lax.psum(partial_rows, 'prow')  256 us
    dot_general x6, matrix products, refine(): jnp.einsum('aqkl,qlr->aqkr', panels, lax.all_gather(rounded, 'pcol', axis...  63.1 us
  transfers between devices with their start and end apart: 12, of which 12 were waited for; matrix products, arithmetic and copies ran while one was open for 1% of the time, Pallas kernels for 0%

commit v1 on v0

v1 whole, which is shorter than its diff:
```python
import functools
import jax
import jax.numpy as jnp
from jax import lax
from jax.experimental import pallas as pl
from jax.experimental.pallas import tpu as pltpu
from jax.sharding import PartitionSpec as P

DEPTH = 4
B = 256
R = 128
SLOTS = 8
SHIFTS = (0, 1, 3, 2)
ANY = pl.BlockSpec(memory_space=pl.ANY)
SMEM = pl.BlockSpec(memory_space=pltpu.SMEM)
VMEM = pl.BlockSpec(memory_space=pltpu.VMEM)


def y_pairs(k):
    return [(i, (i & 25) | ((((i >> 1) + k) & 3) << 1)) for i in range(32)]


def x_pairs(k):
    return [(i, (i & 7) | ((((i >> 3) + k) & 3) << 3)) for i in range(32)]


def z_pairs(k):
    return [(i, (i + k) & 3) for i in range(4)]


CORE_PAIRS = [(i, i ^ 1) for i in range(32)]


def depth_table(parent, levels_count):
    number = parent.shape[0]
    matches = parent[:, None] == jnp.arange(number, dtype=jnp.int32)[None, :]
    depths = jnp.zeros((number,), jnp.int32)
    for repeat in range(levels_count - 1):
        depths = jnp.sum(jnp.where(matches, depths[None, :] + 1, 0), axis=1)
    return depths


def work_lists(depth_rows, depth_cols, pattern):
    row_depth = depth_rows[:, None]
    col_depth = depth_cols[None, :]
    step = jnp.where(col_depth > row_depth, 3 - col_depth, jnp.where(col_depth < row_depth, 3 + col_depth, 6))
    step = jnp.where(pattern == 1, step, 6).reshape(-1)
    number = jnp.arange(128, dtype=jnp.int32)
    before = (step[None, :] < step[:, None]) | ((step[None, :] == step[:, None]) & (number[None, :] < number[:, None]))
    place = jnp.sum(before.astype(jnp.int32), axis=1)
    order = jnp.sum(jnp.where(place[None, :] == number[:, None], number[None, :], 0), axis=1)
    starts = jnp.sum((step[None, :] < jnp.arange(8, dtype=jnp.int32)[:, None]).astype(jnp.int32), axis=1)
    return order, starts


def tile_kernel(step, order, starts, scales, place, *refs):
    pieces = refs[:8]
    tiles = refs[8]
    outs = refs[9:13]
    acc, tile_buf, panel_buf, tile_sem, panel_sem = refs[13:]
    first, last = starts[step], starts[step + 1]
    prow_at, pcol_at = place[0], place[1]

    def copies(n, slot, act):
        code = order[n]
        row, col = code // 32, code % 32
        act(pltpu.make_async_copy(tiles.at[row, col], tile_buf.at[slot], tile_sem.at[slot]))
        other = (col ^ pcol_at) & 1
        x_back = ((pcol_at >> 3) - (col >> 3)) & 3
        y_back = (((pcol_at >> 1) & 3) - ((col >> 1) & 3)) & 3
        y_slot = jnp.where(y_back == 2, 3, jnp.where(y_back == 3, 2, y_back))
        return other, x_back, y_slot

    def start(n, slot):
        other, x_back, y_slot = copies(n, slot, lambda c: c.start())
        for e in range(2):
            for k in range(4):
                @pl.when((other == e) & (x_back == SHIFTS[k]))
                def _():
                    pltpu.make_async_copy(pieces[e * 4 + k].at[y_slot], panel_buf.at[slot], panel_sem.at[slot]).start()

    for n in range(SLOTS):
        @pl.when(first + n < last)
        def _():
            start(first + n, n)

    acc[...] = jnp.zeros_like(acc)

    def body(n, carry):
        slot = (n - first) % SLOTS
        code = order[n]
        pltpu.make_async_copy(tiles.at[0, 0], tile_buf.at[slot], tile_sem.at[slot]).wait()
        pltpu.make_async_copy(pieces[0].at[0], panel_buf.at[slot], panel_sem.at[slot]).wait()
        product = jnp.dot(tile_buf[slot], panel_buf[slot], preferred_element_type=jnp.float32)
        row = code // 32
        acc[row] = acc[row] + scales[code] * product

        @pl.when(n + SLOTS < last)
        def _():
            start(n + SLOTS, slot)
        return carry

    lax.fori_loop(first, last, body, 0)
    outs[0][...] = acc[prow_at]
    for k in range(1, 4):
        outs[k][...] = acc[(prow_at + SHIFTS[k]) & 3].astype(jnp.bfloat16)


def tile_products(step, order, starts, scales, place, pieces, tiles):
    return pl.pallas_call(
        functools.partial(tile_kernel, step),
        out_shape=[jax.ShapeDtypeStruct((B, R), jnp.float32)] + [jax.ShapeDtypeStruct((B, R), jnp.bfloat16)] * 3,
        in_specs=[SMEM] * 4 + [ANY] * 9,
        out_specs=[VMEM] * 4,
        scratch_shapes=[
            pltpu.VMEM((4, B, R), jnp.float32),
            pltpu.VMEM((SLOTS, B, B), jnp.bfloat16),
            pltpu.VMEM((SLOTS, B, R), jnp.bfloat16),
            pltpu.SemaphoreType.DMA((SLOTS,)),
            pltpu.SemaphoreType.DMA((SLOTS,)),
        ],
        compiler_params=pltpu.CompilerParams(vmem_limit_bytes=50 * 2**20),
        cost_estimate=pl.CostEstimate(flops=2 * 4 * B * B * R, bytes_accessed=4 * (B * B + B * R) * 2, transcendentals=0),
        name="tile_products",
    )(order, starts, scales, place, *pieces, tiles)


def apply_inverse(inverse, vectors):
    high = vectors.astype(jnp.bfloat16)
    low = (vectors - high.astype(jnp.float32)).astype(jnp.bfloat16)
    return jnp.dot(inverse, high, preferred_element_type=jnp.float32) + jnp.dot(inverse, low, preferred_element_type=jnp.float32)


def first_kernel(target, inverse, solved, rounded):
    value = apply_inverse(inverse[...], target[...])
    solved[...] = value
    rounded[...] = value.astype(jnp.bfloat16)


def first_solve(target, inverse):
    return pl.pallas_call(
        first_kernel,
        out_shape=[jax.ShapeDtypeStruct((B, R), jnp.float32), jax.ShapeDtypeStruct((B, R), jnp.bfloat16)],
        in_specs=[VMEM] * 2,
        out_specs=[VMEM] * 2,
        cost_estimate=pl.CostEstimate(flops=4 * B * B * R, bytes_accessed=B * R * 12, transcendentals=0),
        name="first_solve",
    )(target, inverse)


def next_kernel(target, inverse, total, own, one, two, three, new_total, solved, rounded):
    summed = total[...] + own[...] + (one[...].astype(jnp.float32) + two[...].astype(jnp.float32) + three[...].astype(jnp.float32))
    new_total[...] = summed
    value = apply_inverse(inverse[...], target[...] - summed)
    solved[...] = value
    rounded[...] = value.astype(jnp.bfloat16)


def next_solve(target, inverse, total, parts):
    return pl.pallas_call(
        next_kernel,
        out_shape=[jax.ShapeDtypeStruct((B, R), jnp.float32)] * 2 + [jax.ShapeDtypeStruct((B, R), jnp.bfloat16)],
        in_specs=[VMEM] * 7,
        out_specs=[VMEM] * 3,
        cost_estimate=pl.CostEstimate(flops=4 * B * B * R, bytes_accessed=B * R * 20, transcendentals=0),
        name="next_solve",
    )(target, inverse, total, *parts)


def gather_panels(panel):
    along_y = [panel] + [lax.ppermute(panel, "pcol", y_pairs(k)) for k in SHIFTS[1:]]
    stacked = jnp.stack(along_y)
    along_x = [stacked] + [lax.ppermute(stacked, "pcol", x_pairs(k)) for k in SHIFTS[1:]]
    return along_x + [lax.ppermute(piece, "pcol", CORE_PAIRS) for piece in along_x]


def shards(right_side, factor_tiles, tile_scales, tile_pattern, parent, inverses):
    prow_at = lax.axis_index("prow")
    pcol_at = lax.axis_index("pcol")
    depths = depth_table(parent, DEPTH)
    depth_rows = lax.dynamic_index_in_dim(depths.reshape(4, 32), pcol_at, 1, keepdims=False)
    depth_cols = lax.dynamic_slice_in_dim(depths, prow_at * 32, 32)
    order, starts = work_lists(depth_rows, depth_cols, tile_pattern[:, 0])
    scales = tile_scales.reshape(-1)
    place = jnp.stack([prow_at, pcol_at]).astype(jnp.int32)
    tiles = factor_tiles[:, 0]

    def sweep(target, inverse, first_step):
        solved, rounded = first_solve(target, inverse)
        total = jnp.zeros_like(target)
        for step in range(first_step, first_step + DEPTH - 1):
            pieces = gather_panels(rounded)
            parts = tile_products(step, order, starts, scales, place, pieces, tiles)
            received = [parts[0]] + [lax.ppermute(parts[k], "prow", z_pairs(SHIFTS[k])) for k in (1, 2, 3)]
            total, solved, rounded = next_solve(target, inverse, total, received)
        return solved

    forward = sweep(right_side[0, 0], inverses[0, 0, 0], 0)
    solution = sweep(forward, inverses[1, 0, 0], 3)
    return (forward[None, None], solution[None, None])


def solution(mesh):
    in_specs = (
        P("prow", "pcol", None, None),
        P(None, "pcol", "prow", None, None),
        P(None, "pcol", "prow"),
        P(None, "pcol", "prow"),
        P(),
        P(None, "prow", "pcol", None, None),
    )
    out_specs = (P("prow", "pcol", None, None), P("prow", "pcol", None, None))
    return jax.shard_map(shards, mesh=mesh, in_specs=in_specs, out_specs=out_specs, check_vma=False)
```

time: 636 us -> 237 us (0.37)
  waiting for transfers between devices: 529 us -> 122 us
  matrix products: 72.9 us -> 0 us
  starting transfers between devices: 0.68 us -> 69.3 us
  Pallas kernels: 0 us -> 23.1 us
  between operations: 14.4 us -> 0.98 us
  other arithmetic: 3.27 us -> 10.4 us
    all_gather x6 -> x0, waiting for transfers between devices: 273 us -> none  [refine(): lax.all_gather(rounded, 'pcol', axis=0, tiled=True)]
    psum x6 -> x0, waiting for transfers between devices: 256 us -> none  [refine(): summed = lax.psum(partial_rows, 'prow')]
    ppermute x0 -> x78, waiting for transfers between devices: none -> 122 us  [the longest x18 55.2 us: gather_panels(): lax.ppermute(stacked, 'pcol', x_pairs(k))]
    dot_general x14 -> x0, matrix products: 72.9 us -> none  [the longest x6 63.1 us: refine(): jnp.einsum('aqkl,qlr->aqkr', panels, lax.all_gather(rounded, 'pcol', axis...]
    ppermute x0 -> x78, starting transfers between devices: none -> 69.3 us  [the longest x18 24.1 us: gather_panels(): lax.ppermute(stacked, 'pcol', x_pairs(k))]
    pallas_call x0 -> x14, Pallas kernels: none -> 23.1 us  [the longest x6 12.4 us: next_solve(): pl.pallas_call(next_kernel, out_shape=[jax.ShapeDtypeStruct((B, R), jnp.f...]
  transfers between devices with their start and end apart: 12 -> 78, of which waited for: 12 -> 54; matrix products, arithmetic and copies ran while one was open for 1% -> 3% of each run, Pallas kernels for 0% -> 0%
where the time goes in v1:
time: 237 us; the launch traced here: 236 us
  waiting for transfers between devices  122 us (51%)
  starting transfers between devices  69.3 us (29%)
  Pallas kernels  23.1 us (10%)
  local copies, waits for them, and re-layouts  10.4 us (4%)
  other arithmetic  10.4 us (4%)
    ppermute x18, waiting for transfers between devices, gather_panels(): lax.ppermute(stacked, 'pcol', x_pairs(k))  55.2 us
    ppermute x18, waiting for transfers between devices, sweep(): lax.ppermute(parts[k], 'prow', z_pairs(SHIFTS[k]))  32.7 us
    ppermute x18, waiting for transfers between devices, gather_panels(): lax.ppermute(panel, 'pcol', y_pairs(k))  26.8 us
    ppermute x18, starting transfers between devices, gather_panels(): lax.ppermute(stacked, 'pcol', x_pairs(k))  24.1 us
    ppermute x18, starting transfers between devices, sweep(): lax.ppermute(parts[k], 'prow', z_pairs(SHIFTS[k]))  23 us
    ppermute x18, starting transfers between devices, gather_panels(): lax.ppermute(panel, 'pcol', y_pairs(k))  21.1 us
    pallas_call x6, Pallas kernels, next_solve(): pl.pallas_call(next_kernel, out_shape=[jax.ShapeDtypeStruct((B, R), jnp.f...  12.4 us
    unnamed x49, local copies, waits for them, and re-layouts  7.5 us
  transfers between devices with their start and end apart: 78, of which 54 were waited for; matrix products, arithmetic and copies ran while one was open for 3% of the time, Pallas kernels for 0%

profile of v1, /device:TPU:0, one launch (start us, length us, event | category | flops | bytes accessed | tf_op | source)
XLA Modules:
  0.0 236.5 jit_solution(4556333811917391124)
XLA Ops:
  4.2 3.3 %collective-permute-start.2 = (bf16[256,128]{1,0:T(8,128)(2,1)}, bf16[256,128]{1,0:T(8,128)(2,1)S(1)}, u32[]{:S(2)}, u32[]{:S(2)}) collective-permute-start(bf16[256,128]{1,0:T(8,128)(2,1)} %get-tuple-element.38), channel_id=1, source_target_pairs={{0,4},{1,5},{2,6},{3,7},{4,0},{5,1},{6,2},{7,3},{8,12},{9,13},{10,... | collective-permute-start | bytes 196616 | tf_op jit(solution)/shard_map/ppermute | solution.py:171
  15.1 3.1 %collective-permute-start.5 = (bf16[4,256,128]{2,1,0:T(8,128)(2,1)S(1)}, bf16[4,256,128]{2,1,0:T(8,128)(2,1)S(1)}, u32[]{:S(2)}, u32[]{:S(2)}) collective-permute-start(bf16[4,256,128]{2,1,0:T(8,128)(2,1)S(1)} %pad_maximum_fusion.refs_0_), channel_id=1, source_target_pairs={{0,16},{1,17},{2,18},{3,19},{4,20},{5,21},{6,22},{7,23},{8,24},{9,... | collective-permute-start | bytes 786440 | tf_op jit(solution)/shard_map/ppermute | solution.py:173
  20.4 5.5 %collective-permute-done.5.refs_3_ = bf16[4,256,128]{2,1,0:T(8,128)(2,1)S(1)} collective-permute-done((bf16[4,256,128]{2,1,0:T(8,128)(2,1)S(1)}, bf16[4,256,128]{2,1,0:T(8,128)(2,1)S(1)}, u32[]{:S(2)}, u32[]{:S(2)}) %collective-permute-start.5) | collective-permute-done | bytes 262176 | tf_op jit(solution)/shard_map/ppermute | solution.py:173
  25.9 2.8 %collective-permute-done.4.refs_2_ = bf16[4,256,128]{2,1,0:T(8,128)(2,1)S(1)} collective-permute-done((bf16[4,256,128]{2,1,0:T(8,128)(2,1)S(1)}, bf16[4,256,128]{2,1,0:T(8,128)(2,1)S(1)}, u32[]{:S(2)}, u32[]{:S(2)}) %collective-permute-start.4) | collective-permute-done | bytes 262176 | tf_op jit(solution)/shard_map/ppermute | solution.py:173
  35.0 2.1 collective-permute-start.11
  39.9 3.6 %collective-permute-done.12.three = bf16[256,128]{1,0:T(8,128)(2,1)S(1)} collective-permute-done((bf16[256,128]{1,0:T(8,128)(2,1)S(1)}, bf16[256,128]{1,0:T(8,128)(2,1)S(1)}, u32[]{:S(2)}, u32[]{:S(2)}) %collective-permute-start.12) | collective-permute-done | bytes 65568 | tf_op jit(solution)/shard_map/ppermute | solution.py:194
  44.2 2.1 next_solve.6
  46.3 2.3 collective-permute-start.15
  53.5 2.3 collective-permute-done.13
  58.3 2.6 %collective-permute-start.17 = (bf16[4,256,128]{2,1,0:T(8,128)(2,1)S(1)}, bf16[4,256,128]{2,1,0:T(8,128)(2,1)S(1)}, u32[]{:S(2)}, u32[]{:S(2)}) collective-permute-start(bf16[4,256,128]{2,1,0:T(8,128)(2,1)S(1)} %pad_maximum_fusion.1.refs_0_), channel_id=1, source_target_pairs={{0,24},{1,25},{2,26},{3,27},{4,28},{5,29},{6,30},{7,31},{8,0},{9,1... | collective-permute-start | bytes 786440 | tf_op jit(solution)/shard_map/ppermute | solution.py:173
  60.9 6.5 %collective-permute-done.18.refs_3_ = bf16[4,256,128]{2,1,0:T(8,128)(2,1)S(1)} collective-permute-done((bf16[4,256,128]{2,1,0:T(8,128)(2,1)S(1)}, bf16[4,256,128]{2,1,0:T(8,128)(2,1)S(1)}, u32[]{:S(2)}, u32[]{:S(2)}) %collective-permute-start.18) | collective-permute-done | bytes 262176 | tf_op jit(solution)/shard_map/ppermute | solution.py:173
  73.9 2.7 %collective-permute-start.24 = (bf16[256,128]{1,0:T(8,128)(2,1)S(1)}, bf16[256,128]{1,0:T(8,128)(2,1)S(1)}, u32[]{:S(2)}, u32[]{:S(2)}) collective-permute-start(bf16[256,128]{1,0:T(8,128)(2,1)S(1)} %get-tuple-element.47), channel_id=1, source_target_pairs={{0,96},{32,0},{64,32},{96,64},{1,97},{33,1},{65,33},{97,65},{2,98}... | collective-permute-start | bytes 196616 | tf_op jit(solution)/shard_map/ppermute | solution.py:194
  79.4 3.0 %collective-permute-done.25.three = bf16[256,128]{1,0:T(8,128)(2,1)S(1)} collective-permute-done((bf16[256,128]{1,0:T(8,128)(2,1)S(1)}, bf16[256,128]{1,0:T(8,128)(2,1)S(1)}, u32[]{:S(2)}, u32[]{:S(2)}) %collective-permute-start.25) | collective-permute-done | bytes 65568 | tf_op jit(solution)/shard_map/ppermute | solution.py:194
  83.0 2.1 next_solve.7
  85.1 2.7 %collective-permute-start.28 = (bf16[256,128]{1,0:T(8,128)(2,1)}, bf16[256,128]{1,0:T(8,128)(2,1)S(1)}, u32[]{:S(2)}, u32[]{:S(2)}) collective-permute-start(bf16[256,128]{1,0:T(8,128)(2,1)} %get-tuple-element.50), channel_id=1, source_target_pairs={{0,4},{1,5},{2,6},{3,7},{4,0},{5,1},{6,2},{7,3},{8,12},{9,13},{10,... | collective-permute-start | bytes 196616 | tf_op jit(solution)/shard_map/ppermute | solution.py:171
  92.2 2.5 %collective-permute-done.26 = bf16[256,128]{1,0:T(8,128)(2,1)S(1)} collective-permute-done((bf16[256,128]{1,0:T(8,128)(2,1)}, bf16[256,128]{1,0:T(8,128)(2,1)S(1)}, u32[]{:S(2)}, u32[]{:S(2)}) %collective-permute-start.26) | collective-permute-done | bytes 65568 | tf_op jit(solution)/shard_map/ppermute | solution.py:171
  95.7 2.7 %collective-permute-start.30 = (bf16[4,256,128]{2,1,0:T(8,128)(2,1)S(1)}, bf16[4,256,128]{2,1,0:T(8,128)(2,1)S(1)}, u32[]{:S(2)}, u32[]{:S(2)}) collective-permute-start(bf16[4,256,128]{2,1,0:T(8,128)(2,1)S(1)} %pad_maximum_fusion.2.refs_0_), channel_id=1, source_target_pairs={{0,24},{1,25},{2,26},{3,27},{4,28},{5,29},{6,30},{7,31},{8,0},{9,1... | collective-permute-start | bytes 786440 | tf_op jit(solution)/shard_map/ppermute | solution.py:173
  98.4 8.0 %collective-permute-done.31.refs_3_ = bf16[4,256,128]{2,1,0:T(8,128)(2,1)S(1)} collective-permute-done((bf16[4,256,128]{2,1,0:T(8,128)(2,1)S(1)}, bf16[4,256,128]{2,1,0:T(8,128)(2,1)S(1)}, u32[]{:S(2)}, u32[]{:S(2)}) %collective-permute-start.31) | collective-permute-done | bytes 262176 | tf_op jit(solution)/shard_map/ppermute | solution.py:173
  106.9 2.5 %collective-permute-done.29.refs_1_ = bf16[4,256,128]{2,1,0:T(8,128)(2,1)S(1)} collective-permute-done((bf16[4,256,128]{2,1,0:T(8,128)(2,1)S(1)}, bf16[4,256,128]{2,1,0:T(8,128)(2,1)S(1)}, u32[]{:S(2)}, u32[]{:S(2)}) %collective-permute-start.29) | collective-permute-done | bytes 262176 | tf_op jit(solution)/shard_map/ppermute | solution.py:173
  112.4 3.2 %collective-permute-start.37 = (bf16[256,128]{1,0:T(8,128)(2,1)S(1)}, bf16[256,128]{1,0:T(8,128)(2,1)S(1)}, u32[]{:S(2)}, u32[]{:S(2)}) collective-permute-start(bf16[256,128]{1,0:T(8,128)(2,1)S(1)} %get-tuple-element.53), channel_id=1, source_target_pairs={{0,96},{32,0},{64,32},{96,64},{1,97},{33,1},{65,33},{97,65},{2,98}... | collective-permute-start | bytes 196616 | tf_op jit(solution)/shard_map/ppermute | solution.py:194
  115.7 2.2 collective-permute-done.36.one
  118.5 3.0 %collective-permute-done.38.three = bf16[256,128]{1,0:T(8,128)(2,1)S(1)} collective-permute-done((bf16[256,128]{1,0:T(8,128)(2,1)S(1)}, bf16[256,128]{1,0:T(8,128)(2,1)S(1)}, u32[]{:S(2)}, u32[]{:S(2)}) %collective-permute-start.38) | collective-permute-done | bytes 65568 | tf_op jit(solution)/shard_map/ppermute | solution.py:194
  122.0 2.1 next_solve.8
  128.6 3.3 %collective-permute-done.41 = bf16[256,128]{1,0:T(8,128)(2,1)S(1)} collective-permute-done((bf16[256,128]{1,0:T(8,128)(2,1)}, bf16[256,128]{1,0:T(8,128)(2,1)S(1)}, u32[]{:S(2)}, u32[]{:S(2)}) %collective-permute-start.41) | collective-permute-done | bytes 65568 | tf_op jit(solution)/shard_map/ppermute | solution.py:171
  131.9 2.3 collective-permute-done.39
  136.0 2.3 collective-permute-start.43
  138.3 6.2 %collective-permute-done.44.refs_3_ = bf16[4,256,128]{2,1,0:T(8,128)(2,1)S(1)} collective-permute-done((bf16[4,256,128]{2,1,0:T(8,128)(2,1)S(1)}, bf16[4,256,128]{2,1,0:T(8,128)(2,1)S(1)}, u32[]{:S(2)}, u32[]{:S(2)}) %collective-permute-start.44) | collective-permute-done | bytes 262176 | tf_op jit(solution)/shard_map/ppermute | solution.py:173
  145.8 2.3 collective-permute-done.42.refs_1_
  152.1 3.2 %collective-permute-start.50 = (bf16[256,128]{1,0:T(8,128)(2,1)S(1)}, bf16[256,128]{1,0:T(8,128)(2,1)S(1)}, u32[]{:S(2)}, u32[]{:S(2)}) collective-permute-start(bf16[256,128]{1,0:T(8,128)(2,1)S(1)} %get-tuple-element.59), channel_id=1, source_target_pairs={{0,96},{32,0},{64,32},{96,64},{1,97},{33,1},{65,33},{97,65},{2,98}... | collective-permute-start | bytes 196616 | tf_op jit(solution)/shard_map/ppermute | solution.py:194
  155.4 2.2 collective-permute-done.49.one
  157.6 3.5 %collective-permute-done.51.three = bf16[256,128]{1,0:T(8,128)(2,1)S(1)} collective-permute-done((bf16[256,128]{1,0:T(8,128)(2,1)S(1)}, bf16[256,128]{1,0:T(8,128)(2,1)S(1)}, u32[]{:S(2)}, u32[]{:S(2)}) %collective-permute-start.51) | collective-permute-done | bytes 65568 | tf_op jit(solution)/shard_map/ppermute | solution.py:194
  161.8 2.1 next_solve.9
  165.9 4.0 %collective-permute-done.54 = bf16[256,128]{1,0:T(8,128)(2,1)S(1)} collective-permute-done((bf16[256,128]{1,0:T(8,128)(2,1)}, bf16[256,128]{1,0:T(8,128)(2,1)S(1)}, u32[]{:S(2)}, u32[]{:S(2)}) %collective-permute-start.54) | collective-permute-done | bytes 65568 | tf_op jit(solution)/shard_map/ppermute | solution.py:171
  172.2 2.4 %collective-permute-start.57 = (bf16[4,256,128]{2,1,0:T(8,128)(2,1)S(1)}, bf16[4,256,128]{2,1,0:T(8,128)(2,1)S(1)}, u32[]{:S(2)}, u32[]{:S(2)}) collective-permute-start(bf16[4,256,128]{2,1,0:T(8,128)(2,1)S(1)} %pad_maximum_fusion.4.refs_0_), channel_id=1, source_target_pairs={{0,16},{1,17},{2,18},{3,19},{4,20},{5,21},{6,22},{7,23},{8,24},{9,... | collective-permute-start | bytes 786440 | tf_op jit(solution)/shard_map/ppermute | solution.py:173
  176.6 5.0 %collective-permute-done.57.refs_3_ = bf16[4,256,128]{2,1,0:T(8,128)(2,1)S(1)} collective-permute-done((bf16[4,256,128]{2,1,0:T(8,128)(2,1)S(1)}, bf16[4,256,128]{2,1,0:T(8,128)(2,1)S(1)}, u32[]{:S(2)}, u32[]{:S(2)}) %collective-permute-start.57) | collective-permute-done | bytes 262176 | tf_op jit(solution)/shard_map/ppermute | solution.py:173
  181.6 2.3 collective-permute-done.56.refs_2_
  189.4 2.9 %collective-permute-start.63 = (bf16[256,128]{1,0:T(8,128)(2,1)S(1)}, bf16[256,128]{1,0:T(8,128)(2,1)S(1)}, u32[]{:S(2)}, u32[]{:S(2)}) collective-permute-start(bf16[256,128]{1,0:T(8,128)(2,1)S(1)} %get-tuple-element.65), channel_id=1, source_target_pairs={{0,96},{32,0},{64,32},{96,64},{1,97},{33,1},{65,33},{97,65},{2,98}... | collective-permute-start | bytes 196616 | tf_op jit(solution)/shard_map/ppermute | solution.py:194
  192.3 2.2 collective-permute-done.62.one
  195.0 3.0 %collective-permute-done.64.three = bf16[256,128]{1,0:T(8,128)(2,1)S(1)} collective-permute-done((bf16[256,128]{1,0:T(8,128)(2,1)S(1)}, bf16[256,128]{1,0:T(8,128)(2,1)S(1)}, u32[]{:S(2)}, u32[]{:S(2)}) %collective-permute-start.64) | collective-permute-done | bytes 65568 | tf_op jit(solution)/shard_map/ppermute | solution.py:194
  198.7 2.1 next_solve.10
  202.8 4.0 %collective-permute-done.67 = bf16[256,128]{1,0:T(8,128)(2,1)S(1)} collective-permute-done((bf16[256,128]{1,0:T(8,128)(2,1)}, bf16[256,128]{1,0:T(8,128)(2,1)S(1)}, u32[]{:S(2)}, u32[]{:S(2)}) %collective-permute-start.67) | collective-permute-done | bytes 65568 | tf_op jit(solution)/shard_map/ppermute | solution.py:171
  208.7 2.1 collective-permute-start.70
  212.8 5.3 %collective-permute-done.70.refs_3_ = bf16[4,256,128]{2,1,0:T(8,128)(2,1)S(1)} collective-permute-done((bf16[4,256,128]{2,1,0:T(8,128)(2,1)S(1)}, bf16[4,256,128]{2,1,0:T(8,128)(2,1)S(1)}, u32[]{:S(2)}, u32[]{:S(2)}) %collective-permute-start.70) | collective-permute-done | bytes 262176 | tf_op jit(solution)/shard_map/ppermute | solution.py:173
  218.1 3.0 %collective-permute-done.69.refs_2_ = bf16[4,256,128]{2,1,0:T(8,128)(2,1)S(1)} collective-permute-done((bf16[4,256,128]{2,1,0:T(8,128)(2,1)S(1)}, bf16[4,256,128]{2,1,0:T(8,128)(2,1)S(1)}, u32[]{:S(2)}, u32[]{:S(2)}) %collective-permute-start.69) | collective-permute-done | bytes 262176 | tf_op jit(solution)/shard_map/ppermute | solution.py:173
  224.6 3.1 %collective-permute-start.76 = (bf16[256,128]{1,0:T(8,128)(2,1)S(1)}, bf16[256,128]{1,0:T(8,128)(2,1)S(1)}, u32[]{:S(2)}, u32[]{:S(2)}) collective-permute-start(bf16[256,128]{1,0:T(8,128)(2,1)S(1)} %get-tuple-element.71), channel_id=1, source_target_pairs={{0,96},{32,0},{64,32},{96,64},{1,97},{33,1},{65,33},{97,65},{2,98}... | collective-permute-start | bytes 196616 | tf_op jit(solution)/shard_map/ppermute | solution.py:194
  228.3 2.2 collective-permute-done.75.one
  231.5 2.3 collective-permute-done.77.three
  234.4 2.1 next_solve.11
  (199 shorter events, 87.6 us)
Async XLA Ops:
  4.2 9.1 %collective-permute-start.2 = (bf16[256,128]{1,0:T(8,128)(2,1)}, bf16[256,128]{1,0:T(8,128)(2,1)S(1)}, u32[]{:S(2)}, u32[]{:S(2)}) collective-permute-start(bf16[256,128]{1,0:T(8,128)(2,1)} %get-tuple-element.38), channel_id=1, source_target_pairs={{0,4},{1,5},{2,6},{3,7},{4,0},{5,1},{6,2},{7,3},{8,12},{9,13},{10,... | collective-permute-start | bytes 196616 | tf_op jit(solution)/shard_map/ppermute | solution.py:171
  7.4 5.9 %collective-permute-start.1 = (bf16[256,128]{1,0:T(8,128)(2,1)}, bf16[256,128]{1,0:T(8,128)(2,1)S(1)}, u32[]{:S(2)}, u32[]{:S(2)}) collective-permute-start(bf16[256,128]{1,0:T(8,128)(2,1)} %get-tuple-element.38), channel_id=1, source_target_pairs={{0,6},{1,7},{2,0},{3,1},{4,2},{5,3},{6,4},{7,5},{8,14},{9,15},{10,... | collective-permute-start | bytes 196616 | tf_op jit(solution)/shard_map/ppermute | solution.py:171
  8.5 5.7 %collective-permute-start = (bf16[256,128]{1,0:T(8,128)(2,1)}, bf16[256,128]{1,0:T(8,128)(2,1)S(1)}, u32[]{:S(2)}, u32[]{:S(2)}) collective-permute-start(bf16[256,128]{1,0:T(8,128)(2,1)} %get-tuple-element.38), channel_id=1, source_target_pairs={{0,2},{1,3},{2,4},{3,5},{4,6},{5,7},{6,0},{7,1},{8,10},{9,11},{10,... | collective-permute-start | bytes 196616 | tf_op jit(solution)/shard_map/ppermute | solution.py:171
  15.1 10.8 %collective-permute-start.5 = (bf16[4,256,128]{2,1,0:T(8,128)(2,1)S(1)}, bf16[4,256,128]{2,1,0:T(8,128)(2,1)S(1)}, u32[]{:S(2)}, u32[]{:S(2)}) collective-permute-start(bf16[4,256,128]{2,1,0:T(8,128)(2,1)S(1)} %pad_maximum_fusion.refs_0_), channel_id=1, source_target_pairs={{0,16},{1,17},{2,18},{3,19},{4,20},{5,21},{6,22},{7,23},{8,24},{9,... | collective-permute-start | bytes 786440 | tf_op jit(solution)/shard_map/ppermute | solution.py:173
  18.2 10.6 %collective-permute-start.4 = (bf16[4,256,128]{2,1,0:T(8,128)(2,1)S(1)}, bf16[4,256,128]{2,1,0:T(8,128)(2,1)S(1)}, u32[]{:S(2)}, u32[]{:S(2)}) collective-permute-start(bf16[4,256,128]{2,1,0:T(8,128)(2,1)S(1)} %pad_maximum_fusion.refs_0_), channel_id=1, source_target_pairs={{0,24},{1,25},{2,26},{3,27},{4,28},{5,29},{6,30},{7,31},{8,0},{9,1... | collective-permute-start | bytes 786440 | tf_op jit(solution)/shard_map/ppermute | solution.py:173
  19.3 9.6 %collective-permute-start.3 = (bf16[4,256,128]{2,1,0:T(8,128)(2,1)S(1)}, bf16[4,256,128]{2,1,0:T(8,128)(2,1)S(1)}, u32[]{:S(2)}, u32[]{:S(2)}) collective-permute-start(bf16[4,256,128]{2,1,0:T(8,128)(2,1)S(1)} %pad_maximum_fusion.refs_0_), channel_id=1, source_target_pairs={{0,8},{1,9},{2,10},{3,11},{4,12},{5,13},{6,14},{7,15},{8,16},{9,17... | collective-permute-start | bytes 786440 | tf_op jit(solution)/shard_map/ppermute | solution.py:173
  20.3 11.2 %collective-permute-start.6 = (bf16[4,256,128]{2,1,0:T(8,128)(2,1)S(1)}, bf16[4,256,128]{2,1,0:T(8,128)(2,1)S(1)}, u32[]{:S(2)}, u32[]{:S(2)}) collective-permute-start(bf16[4,256,128]{2,1,0:T(8,128)(2,1)S(1)} %pad_maximum_fusion.refs_0_), channel_id=1, source_target_pairs={{0,1},{1,0},{2,3},{3,2},{4,5},{5,4},{6,7},{7,6},{8,9},{9,8},{10,11... | collective-permute-start | bytes 786440 | tf_op jit(solution)/shard_map/ppermute | solution.py:174
  33.1 6.6 %collective-permute-start.10 = (bf16[256,128]{1,0:T(8,128)(2,1)S(1)}, bf16[256,128]{1,0:T(8,128)(2,1)S(1)}, u32[]{:S(2)}, u32[]{:S(2)}) collective-permute-start(bf16[256,128]{1,0:T(8,128)(2,1)S(1)} %get-tuple-element.40), channel_id=1, source_target_pairs={{0,32},{32,64},{64,96},{96,0},{1,33},{33,65},{65,97},{97,1},{2,34}... | collective-permute-start | bytes 196616 | tf_op jit(solution)/shard_map/ppermute | solution.py:194
  37.2 6.4 %collective-permute-start.12 = (bf16[256,128]{1,0:T(8,128)(2,1)S(1)}, bf16[256,128]{1,0:T(8,128)(2,1)S(1)}, u32[]{:S(2)}, u32[]{:S(2)}) collective-permute-start(bf16[256,128]{1,0:T(8,128)(2,1)S(1)} %get-tuple-element.42), channel_id=1, source_target_pairs={{0,64},{32,96},{64,0},{96,32},{1,65},{33,97},{65,1},{97,33},{2,66}... | collective-permute-start | bytes 196616 | tf_op jit(solution)/shard_map/ppermute | solution.py:194
  46.3 6.2 %collective-permute-start.15 = (bf16[256,128]{1,0:T(8,128)(2,1)}, bf16[256,128]{1,0:T(8,128)(2,1)S(1)}, u32[]{:S(2)}, u32[]{:S(2)}) collective-permute-start(bf16[256,128]{1,0:T(8,128)(2,1)} %get-tuple-element.44), channel_id=1, source_target_pairs={{0,4},{1,5},{2,6},{3,7},{4,0},{5,1},{6,2},{7,3},{8,12},{9,13},{10,... | collective-permute-start | bytes 196616 | tf_op jit(solution)/shard_map/ppermute | solution.py:171
  50.0 5.7 %collective-permute-start.13 = (bf16[256,128]{1,0:T(8,128)(2,1)}, bf16[256,128]{1,0:T(8,128)(2,1)S(1)}, u32[]{:S(2)}, u32[]{:S(2)}) collective-permute-start(bf16[256,128]{1,0:T(8,128)(2,1)} %get-tuple-element.44), channel_id=1, source_target_pairs={{0,2},{1,3},{2,4},{3,5},{4,6},{5,7},{6,0},{7,1},{8,10},{9,11},{10,... | collective-permute-start | bytes 196616 | tf_op jit(solution)/shard_map/ppermute | solution.py:171
  56.6 10.8 %collective-permute-start.18 = (bf16[4,256,128]{2,1,0:T(8,128)(2,1)S(1)}, bf16[4,256,128]{2,1,0:T(8,128)(2,1)S(1)}, u32[]{:S(2)}, u32[]{:S(2)}) collective-permute-start(bf16[4,256,128]{2,1,0:T(8,128)(2,1)S(1)} %pad_maximum_fusion.1.refs_0_), channel_id=1, source_target_pairs={{0,16},{1,17},{2,18},{3,19},{4,20},{5,21},{6,22},{7,23},{8,24},{9,... | collective-permute-start | bytes 786440 | tf_op jit(solution)/shard_map/ppermute | solution.py:173
  58.3 10.5 %collective-permute-start.17 = (bf16[4,256,128]{2,1,0:T(8,128)(2,1)S(1)}, bf16[4,256,128]{2,1,0:T(8,128)(2,1)S(1)}, u32[]{:S(2)}, u32[]{:S(2)}) collective-permute-start(bf16[4,256,128]{2,1,0:T(8,128)(2,1)S(1)} %pad_maximum_fusion.1.refs_0_), channel_id=1, source_target_pairs={{0,24},{1,25},{2,26},{3,27},{4,28},{5,29},{6,30},{7,31},{8,0},{9,1... | collective-permute-start | bytes 786440 | tf_op jit(solution)/shard_map/ppermute | solution.py:173
  60.9 9.4 %collective-permute-start.16 = (bf16[4,256,128]{2,1,0:T(8,128)(2,1)S(1)}, bf16[4,256,128]{2,1,0:T(8,128)(2,1)S(1)}, u32[]{:S(2)}, u32[]{:S(2)}) collective-permute-start(bf16[4,256,128]{2,1,0:T(8,128)(2,1)S(1)} %pad_maximum_fusion.1.refs_0_), channel_id=1, source_target_pairs={{0,8},{1,9},{2,10},{3,11},{4,12},{5,13},{6,14},{7,15},{8,16},{9,17... | collective-permute-start | bytes 786440 | tf_op jit(solution)/shard_map/ppermute | solution.py:173
  60.9 9.4 %collective-permute-start.19 = (bf16[4,256,128]{2,1,0:T(8,128)(2,1)S(1)}, bf16[4,256,128]{2,1,0:T(8,128)(2,1)S(1)}, u32[]{:S(2)}, u32[]{:S(2)}) collective-permute-start(bf16[4,256,128]{2,1,0:T(8,128)(2,1)S(1)} %pad_maximum_fusion.1.refs_0_), channel_id=1, source_target_pairs={{0,1},{1,0},{2,3},{3,2},{4,5},{5,4},{6,7},{7,6},{8,9},{9,8},{10,11... | collective-permute-start | bytes 786440 | tf_op jit(solution)/shard_map/ppermute | solution.py:174
  76.6 5.8 %collective-permute-start.25 = (bf16[256,128]{1,0:T(8,128)(2,1)S(1)}, bf16[256,128]{1,0:T(8,128)(2,1)S(1)}, u32[]{:S(2)}, u32[]{:S(2)}) collective-permute-start(bf16[256,128]{1,0:T(8,128)(2,1)S(1)} %get-tuple-element.48), channel_id=1, source_target_pairs={{0,64},{32,96},{64,0},{96,32},{1,65},{33,97},{65,1},{97,33},{2,66}... | collective-permute-start | bytes 196616 | tf_op jit(solution)/shard_map/ppermute | solution.py:194
  85.1 6.0 %collective-permute-start.28 = (bf16[256,128]{1,0:T(8,128)(2,1)}, bf16[256,128]{1,0:T(8,128)(2,1)S(1)}, u32[]{:S(2)}, u32[]{:S(2)}) collective-permute-start(bf16[256,128]{1,0:T(8,128)(2,1)} %get-tuple-element.50), channel_id=1, source_target_pairs={{0,4},{1,5},{2,6},{3,7},{4,0},{5,1},{6,2},{7,3},{8,12},{9,13},{10,... | collective-permute-start | bytes 196616 | tf_op jit(solution)/shard_map/ppermute | solution.py:171
  89.0 5.7 %collective-permute-start.26 = (bf16[256,128]{1,0:T(8,128)(2,1)}, bf16[256,128]{1,0:T(8,128)(2,1)S(1)}, u32[]{:S(2)}, u32[]{:S(2)}) collective-permute-start(bf16[256,128]{1,0:T(8,128)(2,1)} %get-tuple-element.50), channel_id=1, source_target_pairs={{0,2},{1,3},{2,4},{3,5},{4,6},{5,7},{6,0},{7,1},{8,10},{9,11},{10,... | collective-permute-start | bytes 196616 | tf_op jit(solution)/shard_map/ppermute | solution.py:171
  95.6 10.8 %collective-permute-start.31 = (bf16[4,256,128]{2,1,0:T(8,128)(2,1)S(1)}, bf16[4,256,128]{2,1,0:T(8,128)(2,1)S(1)}, u32[]{:S(2)}, u32[]{:S(2)}) collective-permute-start(bf16[4,256,128]{2,1,0:T(8,128)(2,1)S(1)} %pad_maximum_fusion.2.refs_0_), channel_id=1, source_target_pairs={{0,16},{1,17},{2,18},{3,19},{4,20},{5,21},{6,22},{7,23},{8,24},{9,... | collective-permute-start | bytes 786440 | tf_op jit(solution)/shard_map/ppermute | solution.py:173
  95.7 11.1 %collective-permute-start.30 = (bf16[4,256,128]{2,1,0:T(8,128)(2,1)S(1)}, bf16[4,256,128]{2,1,0:T(8,128)(2,1)S(1)}, u32[]{:S(2)}, u32[]{:S(2)}) collective-permute-start(bf16[4,256,128]{2,1,0:T(8,128)(2,1)S(1)} %pad_maximum_fusion.2.refs_0_), channel_id=1, source_target_pairs={{0,24},{1,25},{2,26},{3,27},{4,28},{5,29},{6,30},{7,31},{8,0},{9,1... | collective-permute-start | bytes 786440 | tf_op jit(solution)/shard_map/ppermute | solution.py:173
  98.4 11.0 %collective-permute-start.29 = (bf16[4,256,128]{2,1,0:T(8,128)(2,1)S(1)}, bf16[4,256,128]{2,1,0:T(8,128)(2,1)S(1)}, u32[]{:S(2)}, u32[]{:S(2)}) collective-permute-start(bf16[4,256,128]{2,1,0:T(8,128)(2,1)S(1)} %pad_maximum_fusion.2.refs_0_), channel_id=1, source_target_pairs={{0,8},{1,9},{2,10},{3,11},{4,12},{5,13},{6,14},{7,15},{8,16},{9,17... | collective-permute-start | bytes 786440 | tf_op jit(solution)/shard_map/ppermute | solution.py:173
  98.4 11.0 %collective-permute-start.32 = (bf16[4,256,128]{2,1,0:T(8,128)(2,1)S(1)}, bf16[4,256,128]{2,1,0:T(8,128)(2,1)S(1)}, u32[]{:S(2)}, u32[]{:S(2)}) collective-permute-start(bf16[4,256,128]{2,1,0:T(8,128)(2,1)S(1)} %pad_maximum_fusion.2.refs_0_), channel_id=1, source_target_pairs={{0,1},{1,0},{2,3},{3,2},{4,5},{5,4},{6,7},{7,6},{8,9},{9,8},{10,11... | collective-permute-start | bytes 786440 | tf_op jit(solution)/shard_map/ppermute | solution.py:174
  112.4 6.0 %collective-permute-start.37 = (bf16[256,128]{1,0:T(8,128)(2,1)S(1)}, bf16[256,128]{1,0:T(8,128)(2,1)S(1)}, u32[]{:S(2)}, u32[]{:S(2)}) collective-permute-start(bf16[256,128]{1,0:T(8,128)(2,1)S(1)} %get-tuple-element.53), channel_id=1, source_target_pairs={{0,96},{32,0},{64,32},{96,64},{1,97},{33,1},{65,33},{97,65},{2,98}... | collective-permute-start | bytes 196616 | tf_op jit(solution)/shard_map/ppermute | solution.py:194
  115.7 5.8 %collective-permute-start.38 = (bf16[256,128]{1,0:T(8,128)(2,1)S(1)}, bf16[256,128]{1,0:T(8,128)(2,1)S(1)}, u32[]{:S(2)}, u32[]{:S(2)}) collective-permute-start(bf16[256,128]{1,0:T(8,128)(2,1)S(1)} %get-tuple-element.54), channel_id=1, source_target_pairs={{0,64},{32,96},{64,0},{96,32},{1,65},{33,97},{65,1},{97,33},{2,66}... | collective-permute-start | bytes 196616 | tf_op jit(solution)/shard_map/ppermute | solution.py:194
  125.9 6.0 %collective-permute-start.41 = (bf16[256,128]{1,0:T(8,128)(2,1)}, bf16[256,128]{1,0:T(8,128)(2,1)S(1)}, u32[]{:S(2)}, u32[]{:S(2)}) collective-permute-start(bf16[256,128]{1,0:T(8,128)(2,1)} %get-tuple-element.56), channel_id=1, source_target_pairs={{0,4},{1,5},{2,6},{3,7},{4,0},{5,1},{6,2},{7,3},{8,12},{9,13},{10,... | collective-permute-start | bytes 196616 | tf_op jit(solution)/shard_map/ppermute | solution.py:171
  128.5 5.7 %collective-permute-start.39 = (bf16[256,128]{1,0:T(8,128)(2,1)}, bf16[256,128]{1,0:T(8,128)(2,1)S(1)}, u32[]{:S(2)}, u32[]{:S(2)}) collective-permute-start(bf16[256,128]{1,0:T(8,128)(2,1)} %get-tuple-element.56), channel_id=1, source_target_pairs={{0,2},{1,3},{2,4},{3,5},{4,6},{5,7},{6,0},{7,1},{8,10},{9,11},{10,... | collective-permute-start | bytes 196616 | tf_op jit(solution)/shard_map/ppermute | solution.py:171
  135.1 9.4 %collective-permute-start.44 = (bf16[4,256,128]{2,1,0:T(8,128)(2,1)S(1)}, bf16[4,256,128]{2,1,0:T(8,128)(2,1)S(1)}, u32[]{:S(2)}, u32[]{:S(2)}) collective-permute-start(bf16[4,256,128]{2,1,0:T(8,128)(2,1)S(1)} %pad_maximum_fusion.3.refs_0_), channel_id=1, source_target_pairs={{0,16},{1,17},{2,18},{3,19},{4,20},{5,21},{6,22},{7,23},{8,24},{9,... | collective-permute-start | bytes 786440 | tf_op jit(solution)/shard_map/ppermute | solution.py:173
  136.0 9.8 %collective-permute-start.43 = (bf16[4,256,128]{2,1,0:T(8,128)(2,1)S(1)}, bf16[4,256,128]{2,1,0:T(8,128)(2,1)S(1)}, u32[]{:S(2)}, u32[]{:S(2)}) collective-permute-start(bf16[4,256,128]{2,1,0:T(8,128)(2,1)S(1)} %pad_maximum_fusion.3.refs_0_), channel_id=1, source_target_pairs={{0,24},{1,25},{2,26},{3,27},{4,28},{5,29},{6,30},{7,31},{8,0},{9,1... | collective-permute-start | bytes 786440 | tf_op jit(solution)/shard_map/ppermute | solution.py:173
  138.3 9.8 %collective-permute-start.42 = (bf16[4,256,128]{2,1,0:T(8,128)(2,1)S(1)}, bf16[4,256,128]{2,1,0:T(8,128)(2,1)S(1)}, u32[]{:S(2)}, u32[]{:S(2)}) collective-permute-start(bf16[4,256,128]{2,1,0:T(8,128)(2,1)S(1)} %pad_maximum_fusion.3.refs_0_), channel_id=1, source_target_pairs={{0,8},{1,9},{2,10},{3,11},{4,12},{5,13},{6,14},{7,15},{8,16},{9,17... | collective-permute-start | bytes 786440 | tf_op jit(solution)/shard_map/ppermute | solution.py:173
  138.3 9.8 %collective-permute-start.45 = (bf16[4,256,128]{2,1,0:T(8,128)(2,1)S(1)}, bf16[4,256,128]{2,1,0:T(8,128)(2,1)S(1)}, u32[]{:S(2)}, u32[]{:S(2)}) collective-permute-start(bf16[4,256,128]{2,1,0:T(8,128)(2,1)S(1)} %pad_maximum_fusion.3.refs_0_), channel_id=1, source_target_pairs={{0,1},{1,0},{2,3},{3,2},{4,5},{5,4},{6,7},{7,6},{8,9},{9,8},{10,11... | collective-permute-start | bytes 786440 | tf_op jit(solution)/shard_map/ppermute | solution.py:174
  155.4 5.8 %collective-permute-start.51 = (bf16[256,128]{1,0:T(8,128)(2,1)S(1)}, bf16[256,128]{1,0:T(8,128)(2,1)S(1)}, u32[]{:S(2)}, u32[]{:S(2)}) collective-permute-start(bf16[256,128]{1,0:T(8,128)(2,1)S(1)} %get-tuple-element.60), channel_id=1, source_target_pairs={{0,64},{32,96},{64,0},{96,32},{1,65},{33,97},{65,1},{97,33},{2,66}... | collective-permute-start | bytes 196616 | tf_op jit(solution)/shard_map/ppermute | solution.py:194
  163.8 6.0 %collective-permute-start.54 = (bf16[256,128]{1,0:T(8,128)(2,1)}, bf16[256,128]{1,0:T(8,128)(2,1)S(1)}, u32[]{:S(2)}, u32[]{:S(2)}) collective-permute-start(bf16[256,128]{1,0:T(8,128)(2,1)} %get-tuple-element.62), channel_id=1, source_target_pairs={{0,4},{1,5},{2,6},{3,7},{4,0},{5,1},{6,2},{7,3},{8,12},{9,13},{10,... | collective-permute-start | bytes 196616 | tf_op jit(solution)/shard_map/ppermute | solution.py:171
  163.8 6.0 %collective-permute-start.53 = (bf16[256,128]{1,0:T(8,128)(2,1)}, bf16[256,128]{1,0:T(8,128)(2,1)S(1)}, u32[]{:S(2)}, u32[]{:S(2)}) collective-permute-start(bf16[256,128]{1,0:T(8,128)(2,1)} %get-tuple-element.62), channel_id=1, source_target_pairs={{0,6},{1,7},{2,0},{3,1},{4,2},{5,3},{6,4},{7,5},{8,14},{9,15},{10,... | collective-permute-start | bytes 196616 | tf_op jit(solution)/shard_map/ppermute | solution.py:171
  165.6 5.7 %collective-permute-start.52 = (bf16[256,128]{1,0:T(8,128)(2,1)}, bf16[256,128]{1,0:T(8,128)(2,1)S(1)}, u32[]{:S(2)}, u32[]{:S(2)}) collective-permute-start(bf16[256,128]{1,0:T(8,128)(2,1)} %get-tuple-element.62), channel_id=1, source_target_pairs={{0,2},{1,3},{2,4},{3,5},{4,6},{5,7},{6,0},{7,1},{8,10},{9,11},{10,... | collective-permute-start | bytes 196616 | tf_op jit(solution)/shard_map/ppermute | solution.py:171
  172.2 9.4 %collective-permute-start.57 = (bf16[4,256,128]{2,1,0:T(8,128)(2,1)S(1)}, bf16[4,256,128]{2,1,0:T(8,128)(2,1)S(1)}, u32[]{:S(2)}, u32[]{:S(2)}) collective-permute-start(bf16[4,256,128]{2,1,0:T(8,128)(2,1)S(1)} %pad_maximum_fusion.4.refs_0_), channel_id=1, source_target_pairs={{0,16},{1,17},{2,18},{3,19},{4,20},{5,21},{6,22},{7,23},{8,24},{9,... | collective-permute-start | bytes 786440 | tf_op jit(solution)/shard_map/ppermute | solution.py:173
  174.6 9.3 %collective-permute-start.56 = (bf16[4,256,128]{2,1,0:T(8,128)(2,1)S(1)}, bf16[4,256,128]{2,1,0:T(8,128)(2,1)S(1)}, u32[]{:S(2)}, u32[]{:S(2)}) collective-permute-start(bf16[4,256,128]{2,1,0:T(8,128)(2,1)S(1)} %pad_maximum_fusion.4.refs_0_), channel_id=1, source_target_pairs={{0,24},{1,25},{2,26},{3,27},{4,28},{5,29},{6,30},{7,31},{8,0},{9,1... | collective-permute-start | bytes 786440 | tf_op jit(solution)/shard_map/ppermute | solution.py:173
  176.2 8.8 %collective-permute-start.55 = (bf16[4,256,128]{2,1,0:T(8,128)(2,1)S(1)}, bf16[4,256,128]{2,1,0:T(8,128)(2,1)S(1)}, u32[]{:S(2)}, u32[]{:S(2)}) collective-permute-start(bf16[4,256,128]{2,1,0:T(8,128)(2,1)S(1)} %pad_maximum_fusion.4.refs_0_), channel_id=1, source_target_pairs={{0,8},{1,9},{2,10},{3,11},{4,12},{5,13},{6,14},{7,15},{8,16},{9,17... | collective-permute-start | bytes 786440 | tf_op jit(solution)/shard_map/ppermute | solution.py:173
  176.6 8.5 %collective-permute-start.58 = (bf16[4,256,128]{2,1,0:T(8,128)(2,1)S(1)}, bf16[4,256,128]{2,1,0:T(8,128)(2,1)S(1)}, u32[]{:S(2)}, u32[]{:S(2)}) collective-permute-start(bf16[4,256,128]{2,1,0:T(8,128)(2,1)S(1)} %pad_maximum_fusion.4.refs_0_), channel_id=1, source_target_pairs={{0,1},{1,0},{2,3},{3,2},{4,5},{5,4},{6,7},{7,6},{8,9},{9,8},{10,11... | collective-permute-start | bytes 786440 | tf_op jit(solution)/shard_map/ppermute | solution.py:174
  192.3 5.8 %collective-permute-start.64 = (bf16[256,128]{1,0:T(8,128)(2,1)S(1)}, bf16[256,128]{1,0:T(8,128)(2,1)S(1)}, u32[]{:S(2)}, u32[]{:S(2)}) collective-permute-start(bf16[256,128]{1,0:T(8,128)(2,1)S(1)} %get-tuple-element.66), channel_id=1, source_target_pairs={{0,64},{32,96},{64,0},{96,32},{1,65},{33,97},{65,1},{97,33},{2,66}... | collective-permute-start | bytes 196616 | tf_op jit(solution)/shard_map/ppermute | solution.py:194
  200.8 6.0 %collective-permute-start.67 = (bf16[256,128]{1,0:T(8,128)(2,1)}, bf16[256,128]{1,0:T(8,128)(2,1)S(1)}, u32[]{:S(2)}, u32[]{:S(2)}) collective-permute-start(bf16[256,128]{1,0:T(8,128)(2,1)} %get-tuple-element.68), channel_id=1, source_target_pairs={{0,4},{1,5},{2,6},{3,7},{4,0},{5,1},{6,2},{7,3},{8,12},{9,13},{10,... | collective-permute-start | bytes 196616 | tf_op jit(solution)/shard_map/ppermute | solution.py:171
  200.8 6.0 %collective-permute-start.66 = (bf16[256,128]{1,0:T(8,128)(2,1)}, bf16[256,128]{1,0:T(8,128)(2,1)S(1)}, u32[]{:S(2)}, u32[]{:S(2)}) collective-permute-start(bf16[256,128]{1,0:T(8,128)(2,1)} %get-tuple-element.68), channel_id=1, source_target_pairs={{0,6},{1,7},{2,0},{3,1},{4,2},{5,3},{6,4},{7,5},{8,14},{9,15},{10,... | collective-permute-start | bytes 196616 | tf_op jit(solution)/shard_map/ppermute | solution.py:171
  208.7 9.4 %collective-permute-start.70 = (bf16[4,256,128]{2,1,0:T(8,128)(2,1)S(1)}, bf16[4,256,128]{2,1,0:T(8,128)(2,1)S(1)}, u32[]{:S(2)}, u32[]{:S(2)}) collective-permute-start(bf16[4,256,128]{2,1,0:T(8,128)(2,1)S(1)} %pad_maximum_fusion.5.refs_0_), channel_id=1, source_target_pairs={{0,16},{1,17},{2,18},{3,19},{4,20},{5,21},{6,22},{7,23},{8,24},{9,... | collective-permute-start | bytes 786440 | tf_op jit(solution)/shard_map/ppermute | solution.py:173
  210.8 10.3 %collective-permute-start.69 = (bf16[4,256,128]{2,1,0:T(8,128)(2,1)S(1)}, bf16[4,256,128]{2,1,0:T(8,128)(2,1)S(1)}, u32[]{:S(2)}, u32[]{:S(2)}) collective-permute-start(bf16[4,256,128]{2,1,0:T(8,128)(2,1)S(1)} %pad_maximum_fusion.5.refs_0_), channel_id=1, source_target_pairs={{0,24},{1,25},{2,26},{3,27},{4,28},{5,29},{6,30},{7,31},{8,0},{9,1... | collective-permute-start | bytes 786440 | tf_op jit(solution)/shard_map/ppermute | solution.py:173
  212.4 8.7 %collective-permute-start.68 = (bf16[4,256,128]{2,1,0:T(8,128)(2,1)S(1)}, bf16[4,256,128]{2,1,0:T(8,128)(2,1)S(1)}, u32[]{:S(2)}, u32[]{:S(2)}) collective-permute-start(bf16[4,256,128]{2,1,0:T(8,128)(2,1)S(1)} %pad_maximum_fusion.5.refs_0_), channel_id=1, source_target_pairs={{0,8},{1,9},{2,10},{3,11},{4,12},{5,13},{6,14},{7,15},{8,16},{9,17... | collective-permute-start | bytes 786440 | tf_op jit(solution)/shard_map/ppermute | solution.py:173
  212.8 8.8 %collective-permute-start.71 = (bf16[4,256,128]{2,1,0:T(8,128)(2,1)S(1)}, bf16[4,256,128]{2,1,0:T(8,128)(2,1)S(1)}, u32[]{:S(2)}, u32[]{:S(2)}) collective-permute-start(bf16[4,256,128]{2,1,0:T(8,128)(2,1)S(1)} %pad_maximum_fusion.5.refs_0_), channel_id=1, source_target_pairs={{0,1},{1,0},{2,3},{3,2},{4,5},{5,4},{6,7},{7,6},{8,9},{9,8},{10,11... | collective-permute-start | bytes 786440 | tf_op jit(solution)/shard_map/ppermute | solution.py:174
  224.5 6.0 %collective-permute-start.75 = (bf16[256,128]{1,0:T(8,128)(2,1)S(1)}, bf16[256,128]{1,0:T(8,128)(2,1)S(1)}, u32[]{:S(2)}, u32[]{:S(2)}) collective-permute-start(bf16[256,128]{1,0:T(8,128)(2,1)S(1)} %get-tuple-element.70), channel_id=1, source_target_pairs={{0,32},{32,64},{64,96},{96,0},{1,33},{33,65},{65,97},{97,1},{2,34}... | collective-permute-start | bytes 196616 | tf_op jit(solution)/shard_map/ppermute | solution.py:194
  224.6 6.9 %collective-permute-start.76 = (bf16[256,128]{1,0:T(8,128)(2,1)S(1)}, bf16[256,128]{1,0:T(8,128)(2,1)S(1)}, u32[]{:S(2)}, u32[]{:S(2)}) collective-permute-start(bf16[256,128]{1,0:T(8,128)(2,1)S(1)} %get-tuple-element.71), channel_id=1, source_target_pairs={{0,96},{32,0},{64,32},{96,64},{1,97},{33,1},{65,33},{97,65},{2,98}... | collective-permute-start | bytes 196616 | tf_op jit(solution)/shard_map/ppermute | solution.py:194
  227.7 6.1 %collective-permute-start.77 = (bf16[256,128]{1,0:T(8,128)(2,1)S(1)}, bf16[256,128]{1,0:T(8,128)(2,1)S(1)}, u32[]{:S(2)}, u32[]{:S(2)}) collective-permute-start(bf16[256,128]{1,0:T(8,128)(2,1)S(1)} %get-tuple-element.72), channel_id=1, source_target_pairs={{0,64},{32,96},{64,0},{96,32},{1,65},{33,97},{65,1},{97,33},{2,66}... | collective-permute-start | bytes 196616 | tf_op jit(solution)/shard_map/ppermute | solution.py:194
  (54 other events, 157.9 us)

commit v2 on v0

v2 whole, which is shorter than its diff:
```python
import functools
import jax
import jax.numpy as jnp
from jax import lax
from jax.experimental import pallas as pl
from jax.experimental.pallas import tpu as pltpu
from jax.sharding import PartitionSpec as P

DEPTH = 4
B = 256
R = 128
SLOTS = 8
SHIFTS = (0, 1, 3, 2)
ANY = pl.BlockSpec(memory_space=pl.ANY)
SMEM = pl.BlockSpec(memory_space=pltpu.SMEM)
VMEM = pl.BlockSpec(memory_space=pltpu.VMEM)
HBM = pl.BlockSpec(memory_space=pltpu.HBM)
LIMIT = 50 * 2**20
READY = 24


def near_pairs(k):
    return [(i, shifted(i, k, 1 if i & 1 == 0 else 3)) for i in range(32)]


def far_pairs(k):
    return [(i, shifted(i, k, 3 if i & 1 == 0 else 1)) for i in range(32)]


def shifted(i, k, bit):
    return (i & ~(3 << bit)) | ((((i >> bit) + k) & 3) << bit)


def z_pairs(k):
    return [(i, (i + k) & 3) for i in range(4)]


CORE_PAIRS = [(i, i ^ 1) for i in range(32)]


def plan_kernel(place, parent, pattern, out):
    prow_at, pcol_at = place[0], place[1]
    down = lax.broadcasted_iota(jnp.int32, (128, 128), 0)
    across = lax.broadcasted_iota(jnp.int32, (128, 128), 1)

    def column(row):
        return jnp.broadcast_to(row, (128, 128)).T

    def total(values):
        return jnp.sum(values, axis=0, keepdims=True)

    matches = parent[...] == down
    depths = jnp.zeros((1, 128), jnp.int32)
    for repeat in range(DEPTH - 1):
        depths = total(jnp.where(matches, column(depths) + 1, 0))
    depth_column = column(depths)
    row_depth = total(jnp.where(down == (across & 96) + pcol_at, depth_column, 0))
    col_depth = total(jnp.where(down == (across & 31) + prow_at * 32, depth_column, 0))
    spread = (lax.broadcasted_iota(jnp.int32, (32, 128), 1) & 31) == lax.broadcasted_iota(jnp.int32, (32, 128), 0)
    kept = jnp.zeros((1, 128), jnp.float32)
    for row in range(4):
        ones = (jnp.broadcast_to(pattern[row], (8, 32)) == 1).astype(jnp.float32)
        wide = jnp.dot(ones, spread.astype(jnp.float32), preferred_element_type=jnp.float32)[:1]
        kept = jnp.where(across[:1] >> 5 == row, wide, kept)
    step = jnp.where(col_depth > row_depth, 3 - col_depth, jnp.where(col_depth < row_depth, 3 + col_depth, 6))
    step = jnp.where(kept > 0.5, step, 6)
    steps = column(step)
    before = (steps < step) | ((steps == step) & (down < across))
    places = total(before.astype(jnp.int32))
    out[0:1] = total(jnp.where(column(places) == across, down, 0))
    out[1:2] = total((steps < across).astype(jnp.int32))


def make_plan(place, parent, pattern):
    return pl.pallas_call(
        plan_kernel,
        out_shape=jax.ShapeDtypeStruct((2, 128), jnp.int32),
        in_specs=[SMEM, VMEM, VMEM],
        out_specs=VMEM,
        compiler_params=pltpu.CompilerParams(vmem_limit_bytes=LIMIT),
        cost_estimate=pl.CostEstimate(flops=2**22, bytes_accessed=2**12, transcendentals=0),
        name="make_plan",
    )(place, parent, pattern)


def ready_kernel(plan, tiles, out, sems):
    count = jnp.minimum(plan[1, 6], READY)
    for act in (lambda copy: copy.start(), lambda copy: copy.wait()):
        for n in range(READY):
            @pl.when(n < count)
            def _():
                code = plan[0, n]
                act(pltpu.make_async_copy(tiles.at[code >> 5, code & 31], out.at[n], sems.at[n]))


def ready_tiles(plan, tiles):
    return pl.pallas_call(
        ready_kernel,
        out_shape=jax.ShapeDtypeStruct((READY, B, B), jnp.bfloat16),
        in_specs=[SMEM, ANY],
        out_specs=ANY,
        scratch_shapes=[pltpu.SemaphoreType.DMA((READY,))],
        compiler_params=pltpu.CompilerParams(vmem_limit_bytes=LIMIT),
        cost_estimate=pl.CostEstimate(flops=0, bytes_accessed=2 * READY * B * B * 2, transcendentals=0),
        name="ready_tiles",
    )(plan, tiles)


def fetch(sources, buffers, sems):
    fetched = [pltpu.make_async_copy(src, buf, sems.at[n]) for n, (src, buf) in enumerate(zip(sources, buffers))]
    for copy in fetched:
        copy.start()
    return fetched


def panel_place(pcol_at, col):
    x_back = ((pcol_at >> 3) - (col >> 3)) & 3
    y_back = ((pcol_at >> 1) - (col >> 1)) & 3
    far = jnp.where((col & 1) == 0, x_back, y_back)
    near = jnp.where((col & 1) == 0, y_back, x_back)
    near_slot = jnp.where(near == 2, 3, jnp.where(near == 3, 2, near))
    return (col ^ pcol_at) & 1, far, near_slot


def start_panel(pieces, pcol_at, col, buffer, sem):
    other, far, near_slot = panel_place(pcol_at, col)
    for e in range(2):
        for k in range(4):
            @pl.when((other == e) & (far == SHIFTS[k]))
            def _():
                pltpu.make_async_copy(pieces[e * 4 + k].at[near_slot], buffer, sem).start()


def tile_kernel(step, plan, scales, place, *refs):
    pieces, tiles, ready, refs = refs[:8], refs[8], refs[9], refs[10:]
    before, refs = (refs[0], refs[1:]) if step % 3 > 0 else (None, refs)
    outs, refs = refs[:4], refs[4:]
    after, refs = (refs[0], refs[1:]) if step % 3 < 2 else (None, refs)
    acc, tile_buf, panel_buf, tile_sem, panel_sem, before_sem = refs
    first, last = plan[1, step], plan[1, step + 1]
    prow_at, pcol_at = place[0], place[1]

    def start(n, slot):
        code = plan[0, n]
        row, col = code >> 5, code & 31

        @pl.when(n < READY)
        def _():
            pltpu.make_async_copy(ready.at[n], tile_buf.at[slot], tile_sem.at[slot]).start()

        @pl.when(n >= READY)
        def _():
            pltpu.make_async_copy(tiles.at[row, col], tile_buf.at[slot], tile_sem.at[slot]).start()

        start_panel(pieces, pcol_at, col, panel_buf.at[slot], panel_sem.at[slot])

    if step % 3 > 0:
        previous = pltpu.make_async_copy(before, acc, before_sem)
        previous.start()
    for n in range(SLOTS):
        @pl.when(first + n < last)
        def _():
            start(first + n, n)

    if step % 3 > 0:
        previous.wait()
    else:
        acc[...] = jnp.zeros_like(acc)

    def body(n, carry):
        slot = (n - first) % SLOTS
        code = plan[0, n]
        pltpu.make_async_copy(tiles.at[0, 0], tile_buf.at[slot], tile_sem.at[slot]).wait()
        pltpu.make_async_copy(pieces[0].at[0], panel_buf.at[slot], panel_sem.at[slot]).wait()
        product = jnp.dot(tile_buf[slot], panel_buf[slot], preferred_element_type=jnp.float32)
        row = code >> 5
        acc[row] = acc[row] + scales[row, 0, code & 31] * product

        @pl.when(n + SLOTS < last)
        def _():
            start(n + SLOTS, slot)
        return carry

    lax.fori_loop(first, last, body, 0)
    if after is not None:
        after[...] = acc[...]
    outs[0][...] = acc[prow_at]
    for k in range(1, 4):
        outs[k][...] = acc[(prow_at + SHIFTS[k]) & 3].astype(jnp.bfloat16)


def tile_products(step, plan, scales, place, pieces, tiles, ready, before):
    out_shape = [jax.ShapeDtypeStruct((B, R), jnp.float32)] + [jax.ShapeDtypeStruct((B, R), jnp.bfloat16)] * 3
    if step % 3 < 2:
        out_shape = out_shape + [jax.ShapeDtypeStruct((4, B, R), jnp.float32)]
    return pl.pallas_call(
        functools.partial(tile_kernel, step),
        out_shape=out_shape,
        in_specs=[SMEM] * 3 + [ANY] * (10 + len(before)),
        out_specs=[VMEM] * len(out_shape),
        scratch_shapes=[
            pltpu.VMEM((4, B, R), jnp.float32),
            pltpu.VMEM((SLOTS, B, B), jnp.bfloat16),
            pltpu.VMEM((SLOTS, B, R), jnp.bfloat16),
            pltpu.SemaphoreType.DMA((SLOTS,)),
            pltpu.SemaphoreType.DMA((SLOTS,)),
            pltpu.SemaphoreType.DMA,
        ],
        compiler_params=pltpu.CompilerParams(vmem_limit_bytes=LIMIT),
        cost_estimate=pl.CostEstimate(flops=2 * 4 * B * B * R, bytes_accessed=4 * (B * B + B * R) * 2, transcendentals=0),
        name="tile_products",
    )(plan, scales, place, *pieces, tiles, ready, *before)


def split(vectors):
    high = vectors.astype(jnp.bfloat16)
    return high, (vectors - high.astype(jnp.float32)).astype(jnp.bfloat16)


def apply_split(inverse, high, low):
    return jnp.dot(inverse, high, preferred_element_type=jnp.float32) + jnp.dot(inverse, low, preferred_element_type=jnp.float32)


def solve_kernel(uses, summed, keep, send, target, inverses, *refs):
    sums, refs = refs[:summed], refs[summed:]
    rounded, refs = (refs[0], refs[1:]) if send else (None, refs)
    solved, refs = (refs[0], refs[1:]) if keep else (None, refs)
    buffers, inverse_buf, sems = refs[:-2], refs[-2], refs[-1]
    inverse_copies = fetch([inverses.at[n] for n in uses], [inverse_buf.at[n] for n in range(len(uses))], sems.at[pl.ds(5, 2)])
    for copy in fetch((target,) + sums, buffers, sems):
        copy.wait()
    value = buffers[0][...]
    if sums:
        received = buffers[2][...].astype(jnp.float32) + buffers[3][...].astype(jnp.float32) + buffers[4][...].astype(jnp.float32)
        value = value - (buffers[1][...] + received)
    for n, use in enumerate(uses):
        inverse_copies[n].wait()
        value = apply_split(inverse_buf[n], *split(value))
        if n == 0 and solved is not None:
            solved[...] = value
    if rounded is not None:
        rounded[...] = value.astype(jnp.bfloat16)


def solve(uses, target, inverses, sums, keep=False, send=True):
    out_shape = []
    if send:
        out_shape.append(jax.ShapeDtypeStruct((B, R), jnp.bfloat16))
    if keep:
        out_shape.append(jax.ShapeDtypeStruct((B, R), jnp.float32))
    buffers = [pltpu.VMEM((B, R), jnp.float32)]
    if sums:
        buffers = buffers + [pltpu.VMEM((B, R), jnp.float32)] + [pltpu.VMEM((B, R), jnp.bfloat16)] * 3
    return pl.pallas_call(
        functools.partial(solve_kernel, uses, len(sums), keep, send),
        out_shape=out_shape,
        in_specs=[ANY] * (2 + len(sums)),
        out_specs=[VMEM] * len(out_shape),
        scratch_shapes=buffers + [pltpu.VMEM((len(uses), B, B), jnp.bfloat16), pltpu.SemaphoreType.DMA((7,))],
        compiler_params=pltpu.CompilerParams(vmem_limit_bytes=LIMIT),
        cost_estimate=pl.CostEstimate(flops=4 * B * B * R, bytes_accessed=B * R * 20, transcendentals=0),
        name="solve",
    )(target, inverses, *sums)


def stack_kernel(ready, *refs):
    panels, out, sems = refs[:4], refs[4], refs[5]
    for copy in fetch(panels, [out.at[k] for k in range(4)], sems):
        copy.wait()


def stack_after(ready, panels):
    return pl.pallas_call(
        stack_kernel,
        out_shape=jax.ShapeDtypeStruct((4, B, R), jnp.bfloat16),
        in_specs=[ANY] * 5,
        out_specs=ANY,
        scratch_shapes=[pltpu.SemaphoreType.DMA((4,))],
        compiler_params=pltpu.CompilerParams(vmem_limit_bytes=LIMIT),
        name="stack_after",
    )(ready, *panels)


def gather_panels(panel, ready=None):
    near = [panel] + [lax.ppermute(panel, "pcol", near_pairs(k)) for k in SHIFTS[1:]]
    near = jnp.stack(near) if ready is None else stack_after(ready, near)
    far = [near] + [lax.ppermute(near, "pcol", far_pairs(k)) for k in SHIFTS[1:]]
    return far + [lax.ppermute(piece, "pcol", CORE_PAIRS) for piece in far]


def across_rows(values):
    return [lax.ppermute(value, "prow", z_pairs(k)) for value, k in zip(values, SHIFTS[1:])]


def shards(right_side, factor_tiles, tile_scales, tile_pattern, parent, inverses):
    place = jnp.stack([lax.axis_index("prow"), lax.axis_index("pcol")]).astype(jnp.int32)
    tiles = factor_tiles[:, 0]
    inverse_pair = inverses[:, 0, 0]

    target = right_side[0, 0]
    (rounded,) = solve((0,), target, inverse_pair, ())
    plan = make_plan(place, parent.reshape(1, 128), tile_pattern)
    ready = ready_tiles(plan, tiles)
    before = ()
    for step in range(6):
        pieces = gather_panels(rounded, ready if step == 0 else None)
        parts = tile_products(step, plan, tile_scales, place, pieces, tiles, ready, before)
        before = tuple(parts[4:])
        sums = (parts[0], *across_rows(parts[1:4]))
        if step == 2:
            rounded, forward = solve((0, 1), target, inverse_pair, sums, keep=True)
            target = forward
        elif step == 5:
            (solved,) = solve((1,), target, inverse_pair, sums, keep=True, send=False)
        else:
            (rounded,) = solve((step // 3,), target, inverse_pair, sums)
    return (forward[None, None], solved[None, None])


def solution(mesh):
    in_specs = (
        P("prow", "pcol", None, None),
        P(None, "pcol", "prow", None, None),
        P(None, "pcol", "prow"),
        P(None, "pcol", "prow"),
        P(),
        P(None, "prow", "pcol", None, None),
    )
    out_specs = (P("prow", "pcol", None, None), P("prow", "pcol", None, None))
    return jax.shard_map(shards, mesh=mesh, in_specs=in_specs, out_specs=out_specs, check_vma=False)
```

time: 636 us -> 204 us (0.32)
  waiting for transfers between devices: 529 us -> 105 us
  starting transfers between devices: 0.68 us -> 75.2 us
  matrix products: 72.9 us -> 0 us
  Pallas kernels: 0 us -> 17.9 us
  between operations: 14.4 us -> 1.13 us
  local copies, waits for them, and re-layouts: 15.9 us -> 3.22 us
    all_gather x6 -> x0, waiting for transfers between devices: 273 us -> none  [refine(): lax.all_gather(rounded, 'pcol', axis=0, tiled=True)]
    psum x6 -> x0, waiting for transfers between devices: 256 us -> none  [refine(): summed = lax.psum(partial_rows, 'prow')]
    ppermute x0 -> x78, waiting for transfers between devices: none -> 105 us  [the longest x18 41.1 us: gather_panels(): lax.ppermute(near, 'pcol', far_pairs(k))]
    ppermute x0 -> x78, starting transfers between devices: none -> 75.2 us  [the longest x18 28.3 us: gather_panels(): lax.ppermute(near, 'pcol', far_pairs(k))]
    dot_general x14 -> x0, matrix products: 72.9 us -> none  [the longest x6 63.1 us: refine(): jnp.einsum('aqkl,qlr->aqkr', panels, lax.all_gather(rounded, 'pcol', axis...]
    pallas_call x0 -> x16, Pallas kernels: none -> 17.9 us  [the longest x7 8.39 us: solve(): pl.pallas_call(functools.partial(solve_kernel, uses, len(sums), keep, sen...]
    unnamed x11 -> x18, local copies, waits for them, and re-layouts: 12.4 us -> 3.22 us
  transfers between devices with their start and end apart: 12 -> 78, of which waited for: 12 -> 58; matrix products, arithmetic and copies ran while one was open for 1% -> 0% of each run, Pallas kernels for 0% -> 1%
where the time goes in v2:
time: 204 us; the launch traced here: 202 us
  waiting for transfers between devices  105 us (51%)
  starting transfers between devices  75.2 us (37%)
  Pallas kernels  17.9 us (9%)
  local copies, waits for them, and re-layouts  3.22 us (2%)
    ppermute x18, waiting for transfers between devices, gather_panels(): lax.ppermute(near, 'pcol', far_pairs(k))  41.1 us
    ppermute x18, waiting for transfers between devices, across_rows(): lax.ppermute(value, 'prow', z_pairs(k))  31.9 us
    ppermute x18, starting transfers between devices, gather_panels(): lax.ppermute(near, 'pcol', far_pairs(k))  28.3 us
    ppermute x18, starting transfers between devices, across_rows(): lax.ppermute(value, 'prow', z_pairs(k))  23.2 us
    ppermute x18, waiting for transfers between devices, gather_panels(): lax.ppermute(panel, 'pcol', near_pairs(k))  22.9 us
    ppermute x18, starting transfers between devices, gather_panels(): lax.ppermute(panel, 'pcol', near_pairs(k))  22.5 us
    ppermute x24, waiting for transfers between devices, gather_panels(): return far + [lax.ppermute(piece, 'pcol', CORE_PAIRS) for piece in far]  8.77 us
    pallas_call x7, Pallas kernels, solve(): pl.pallas_call(functools.partial(solve_kernel, uses, len(sums), keep, sen...  8.39 us
  transfers between devices with their start and end apart: 78, of which 58 were waited for; matrix products, arithmetic and copies ran while one was open for 0% of the time, Pallas kernels for 1%

profile of v2, /device:TPU:0, one launch (start us, length us, event | category | flops | bytes accessed | tf_op | source)
XLA Modules:
  0.0 202.4 jit_solution(13028187384070084218)
XLA Ops:
  3.1 3.4 %collective-permute-start.2 = (bf16[256,128]{1,0:T(8,128)(2,1)S(1)}, bf16[256,128]{1,0:T(8,128)(2,1)S(1)}, u32[]{:S(2)}, u32[]{:S(2)}) collective-permute-start(bf16[256,128]{1,0:T(8,128)(2,1)S(1)} %solve.7.refs_0_), channel_id=1, source_target_pairs={{0,4},{1,17},{2,6},{3,19},{4,0},{5,21},{6,2},{7,23},{8,12},{9,25},... | collective-permute-start | bytes 196616 | tf_op jit(solution)/shard_map/ppermute | solution.py:285
  13.3 3.2 %collective-permute-start.5 = (bf16[4,256,128]{2,1,0:T(8,128)(2,1)S(1)}, bf16[4,256,128]{2,1,0:T(8,128)(2,1)S(1)}, u32[]{:S(2)}, u32[]{:S(2)}) collective-permute-start(bf16[4,256,128]{2,1,0:T(8,128)(2,1)S(1)} %stack_after.1.refs_0_), channel_id=1, source_target_pairs={{0,16},{1,5},{2,18},{3,7},{4,20},{5,1},{6,22},{7,3},{8,24},{9,13},... | collective-permute-start | bytes 786440 | tf_op jit(solution)/shard_map/ppermute | solution.py:287
  18.5 2.8 %collective-permute-done.5.refs_3_ = bf16[4,256,128]{2,1,0:T(8,128)(2,1)S(1)} collective-permute-done((bf16[4,256,128]{2,1,0:T(8,128)(2,1)S(1)}, bf16[4,256,128]{2,1,0:T(8,128)(2,1)S(1)}, u32[]{:S(2)}, u32[]{:S(2)}) %collective-permute-start.5) | collective-permute-done | bytes 262176 | tf_op jit(solution)/shard_map/ppermute | solution.py:287
  21.3 2.9 %collective-permute-done.4.refs_2_ = bf16[4,256,128]{2,1,0:T(8,128)(2,1)S(1)} collective-permute-done((bf16[4,256,128]{2,1,0:T(8,128)(2,1)S(1)}, bf16[4,256,128]{2,1,0:T(8,128)(2,1)S(1)}, u32[]{:S(2)}, u32[]{:S(2)}) %collective-permute-start.4) | collective-permute-done | bytes 262176 | tf_op jit(solution)/shard_map/ppermute | solution.py:287
  26.7 1.9 tile_products.6
  29.6 2.3 %collective-permute-start.11 = (bf16[256,128]{1,0:T(8,128)(2,1)S(1)}, bf16[256,128]{1,0:T(8,128)(2,1)S(1)}, u32[]{:S(2)}, u32[]{:S(2)}) collective-permute-start(bf16[256,128]{1,0:T(8,128)(2,1)S(1)} %get-tuple-element.34), channel_id=1, source_target_pairs={{0,96},{32,0},{64,32},{96,64},{1,97},{33,1},{65,33},{97,65},{2,98}... | collective-permute-start | bytes 196616 | tf_op jit(solution)/shard_map/ppermute | solution.py:292
  31.9 1.8 collective-permute-start.12
  34.5 3.8 %collective-permute-done.12.refs_3_ = bf16[256,128]{1,0:T(8,128)(2,1)S(1)} collective-permute-done((bf16[256,128]{1,0:T(8,128)(2,1)S(1)}, bf16[256,128]{1,0:T(8,128)(2,1)S(1)}, u32[]{:S(2)}, u32[]{:S(2)}) %collective-permute-start.12) | collective-permute-done | bytes 65568 | tf_op jit(solution)/shard_map/ppermute | solution.py:292
  40.0 3.0 %collective-permute-start.14 = (bf16[256,128]{1,0:T(8,128)(2,1)S(1)}, bf16[256,128]{1,0:T(8,128)(2,1)S(1)}, u32[]{:S(2)}, u32[]{:S(2)}) collective-permute-start(bf16[256,128]{1,0:T(8,128)(2,1)S(1)} %solve.8), channel_id=1, source_target_pairs={{0,6},{1,25},{2,0},{3,27},{4,2},{5,29},{6,4},{7,31},{8,14},{9,1},{... | collective-permute-start | bytes 196616 | tf_op jit(solution)/shard_map/ppermute | solution.py:285
  43.4 1.9 collective-permute-done.15
  46.3 2.1 %collective-permute-done.13 = bf16[256,128]{1,0:T(8,128)(2,1)S(1)} collective-permute-done((bf16[256,128]{1,0:T(8,128)(2,1)S(1)}, bf16[256,128]{1,0:T(8,128)(2,1)S(1)}, u32[]{:S(2)}, u32[]{:S(2)}) %collective-permute-start.13) | collective-permute-done | bytes 65568 | tf_op jit(solution)/shard_map/ppermute | solution.py:285
  48.5 5.2 %collective-permute-start.18 = (bf16[4,256,128]{2,1,0:T(8,128)(2,1)S(1)}, bf16[4,256,128]{2,1,0:T(8,128)(2,1)S(1)}, u32[]{:S(2)}, u32[]{:S(2)}) collective-permute-start(bf16[4,256,128]{2,1,0:T(8,128)(2,1)S(1)} %pad_maximum_fusion.refs_0_), channel_id=1, source_target_pairs={{0,16},{1,5},{2,18},{3,7},{4,20},{5,1},{6,22},{7,3},{8,24},{9,13},... | collective-permute-start | bytes 786440 | tf_op jit(solution)/shard_map/ppermute | solution.py:287
  53.6 2.0 collective-permute-start.16
  55.7 2.3 %collective-permute-done.18.refs_3_ = bf16[4,256,128]{2,1,0:T(8,128)(2,1)S(1)} collective-permute-done((bf16[4,256,128]{2,1,0:T(8,128)(2,1)S(1)}, bf16[4,256,128]{2,1,0:T(8,128)(2,1)S(1)}, u32[]{:S(2)}, u32[]{:S(2)}) %collective-permute-start.18) | collective-permute-done | bytes 262176 | tf_op jit(solution)/shard_map/ppermute | solution.py:287
  58.0 3.6 %collective-permute-done.17.refs_2_ = bf16[4,256,128]{2,1,0:T(8,128)(2,1)S(1)} collective-permute-done((bf16[4,256,128]{2,1,0:T(8,128)(2,1)S(1)}, bf16[4,256,128]{2,1,0:T(8,128)(2,1)S(1)}, u32[]{:S(2)}, u32[]{:S(2)}) %collective-permute-start.17) | collective-permute-done | bytes 262176 | tf_op jit(solution)/shard_map/ppermute | solution.py:287
  64.5 3.2 %collective-permute-start.24 = (bf16[256,128]{1,0:T(8,128)(2,1)S(1)}, bf16[256,128]{1,0:T(8,128)(2,1)S(1)}, u32[]{:S(2)}, u32[]{:S(2)}) collective-permute-start(bf16[256,128]{1,0:T(8,128)(2,1)S(1)} %get-tuple-element.39), channel_id=1, source_target_pairs={{0,96},{32,0},{64,32},{96,64},{1,97},{33,1},{65,33},{97,65},{2,98}... | collective-permute-start | bytes 196616 | tf_op jit(solution)/shard_map/ppermute | solution.py:292
  68.5 2.1 %collective-permute-done.23.refs_1_ = bf16[256,128]{1,0:T(8,128)(2,1)S(1)} collective-permute-done((bf16[256,128]{1,0:T(8,128)(2,1)S(1)}, bf16[256,128]{1,0:T(8,128)(2,1)S(1)}, u32[]{:S(2)}, u32[]{:S(2)}) %collective-permute-start.23) | collective-permute-done | bytes 65568 | tf_op jit(solution)/shard_map/ppermute | solution.py:292
  70.6 3.0 %collective-permute-done.25.refs_3_ = bf16[256,128]{1,0:T(8,128)(2,1)S(1)} collective-permute-done((bf16[256,128]{1,0:T(8,128)(2,1)S(1)}, bf16[256,128]{1,0:T(8,128)(2,1)S(1)}, u32[]{:S(2)}, u32[]{:S(2)}) %collective-permute-start.25) | collective-permute-done | bytes 65568 | tf_op jit(solution)/shard_map/ppermute | solution.py:292
  77.9 2.7 %collective-permute-done.28 = bf16[256,128]{1,0:T(8,128)(2,1)S(1)} collective-permute-done((bf16[256,128]{1,0:T(8,128)(2,1)S(1)}, bf16[256,128]{1,0:T(8,128)(2,1)S(1)}, u32[]{:S(2)}, u32[]{:S(2)}) %collective-permute-start.28) | collective-permute-done | bytes 65568 | tf_op jit(solution)/shard_map/ppermute | solution.py:285
  82.0 1.9 collective-permute-start.31
  85.9 4.1 %collective-permute-done.31.refs_3_ = bf16[4,256,128]{2,1,0:T(8,128)(2,1)S(1)} collective-permute-done((bf16[4,256,128]{2,1,0:T(8,128)(2,1)S(1)}, bf16[4,256,128]{2,1,0:T(8,128)(2,1)S(1)}, u32[]{:S(2)}, u32[]{:S(2)}) %collective-permute-start.31) | collective-permute-done | bytes 262176 | tf_op jit(solution)/shard_map/ppermute | solution.py:287
  90.0 2.4 %collective-permute-done.30.refs_2_ = bf16[4,256,128]{2,1,0:T(8,128)(2,1)S(1)} collective-permute-done((bf16[4,256,128]{2,1,0:T(8,128)(2,1)S(1)}, bf16[4,256,128]{2,1,0:T(8,128)(2,1)S(1)}, u32[]{:S(2)}, u32[]{:S(2)}) %collective-permute-start.30) | collective-permute-done | bytes 262176 | tf_op jit(solution)/shard_map/ppermute | solution.py:287
  95.3 3.2 %collective-permute-start.37 = (bf16[256,128]{1,0:T(8,128)(2,1)S(1)}, bf16[256,128]{1,0:T(8,128)(2,1)S(1)}, u32[]{:S(2)}, u32[]{:S(2)}) collective-permute-start(bf16[256,128]{1,0:T(8,128)(2,1)S(1)} %get-tuple-element.44), channel_id=1, source_target_pairs={{0,96},{32,0},{64,32},{96,64},{1,97},{33,1},{65,33},{97,65},{2,98}... | collective-permute-start | bytes 196616 | tf_op jit(solution)/shard_map/ppermute | solution.py:292
  98.5 2.2 %collective-permute-done.36.refs_1_ = bf16[256,128]{1,0:T(8,128)(2,1)S(1)} collective-permute-done((bf16[256,128]{1,0:T(8,128)(2,1)S(1)}, bf16[256,128]{1,0:T(8,128)(2,1)S(1)}, u32[]{:S(2)}, u32[]{:S(2)}) %collective-permute-start.36) | collective-permute-done | bytes 65568 | tf_op jit(solution)/shard_map/ppermute | solution.py:292
  101.3 3.0 %collective-permute-done.38.refs_3_ = bf16[256,128]{1,0:T(8,128)(2,1)S(1)} collective-permute-done((bf16[256,128]{1,0:T(8,128)(2,1)S(1)}, bf16[256,128]{1,0:T(8,128)(2,1)S(1)}, u32[]{:S(2)}, u32[]{:S(2)}) %collective-permute-start.38) | collective-permute-done | bytes 65568 | tf_op jit(solution)/shard_map/ppermute | solution.py:292
  104.3 1.9 solve.10
  106.2 2.1 %collective-permute-start.41 = (bf16[256,128]{1,0:T(8,128)(2,1)S(1)}, bf16[256,128]{1,0:T(8,128)(2,1)S(1)}, u32[]{:S(2)}, u32[]{:S(2)}) collective-permute-start(bf16[256,128]{1,0:T(8,128)(2,1)S(1)} %get-tuple-element.47), channel_id=1, source_target_pairs={{0,4},{1,17},{2,6},{3,19},{4,0},{5,21},{6,2},{7,23},{8,12},{9,25},... | collective-permute-start | bytes 196616 | tf_op jit(solution)/shard_map/ppermute | solution.py:285
  110.3 1.8 collective-permute-done.41
  112.5 2.4 %collective-permute-done.39 = bf16[256,128]{1,0:T(8,128)(2,1)S(1)} collective-permute-done((bf16[256,128]{1,0:T(8,128)(2,1)S(1)}, bf16[256,128]{1,0:T(8,128)(2,1)S(1)}, u32[]{:S(2)}, u32[]{:S(2)}) %collective-permute-start.39) | collective-permute-done | bytes 65568 | tf_op jit(solution)/shard_map/ppermute | solution.py:285
  116.5 2.3 %collective-permute-start.43 = (bf16[4,256,128]{2,1,0:T(8,128)(2,1)S(1)}, bf16[4,256,128]{2,1,0:T(8,128)(2,1)S(1)}, u32[]{:S(2)}, u32[]{:S(2)}) collective-permute-start(bf16[4,256,128]{2,1,0:T(8,128)(2,1)S(1)} %pad_maximum_fusion.2.refs_0_), channel_id=1, source_target_pairs={{0,24},{1,7},{2,26},{3,1},{4,28},{5,3},{6,30},{7,5},{8,0},{9,15},{... | collective-permute-start | bytes 786440 | tf_op jit(solution)/shard_map/ppermute | solution.py:287
  118.8 4.1 %collective-permute-done.44.refs_3_ = bf16[4,256,128]{2,1,0:T(8,128)(2,1)S(1)} collective-permute-done((bf16[4,256,128]{2,1,0:T(8,128)(2,1)S(1)}, bf16[4,256,128]{2,1,0:T(8,128)(2,1)S(1)}, u32[]{:S(2)}, u32[]{:S(2)}) %collective-permute-start.44) | collective-permute-done | bytes 262176 | tf_op jit(solution)/shard_map/ppermute | solution.py:287
  122.9 2.6 %collective-permute-done.43.refs_2_ = bf16[4,256,128]{2,1,0:T(8,128)(2,1)S(1)} collective-permute-done((bf16[4,256,128]{2,1,0:T(8,128)(2,1)S(1)}, bf16[4,256,128]{2,1,0:T(8,128)(2,1)S(1)}, u32[]{:S(2)}, u32[]{:S(2)}) %collective-permute-start.43) | collective-permute-done | bytes 262176 | tf_op jit(solution)/shard_map/ppermute | solution.py:287
  129.0 3.2 %collective-permute-start.50 = (bf16[256,128]{1,0:T(8,128)(2,1)S(1)}, bf16[256,128]{1,0:T(8,128)(2,1)S(1)}, u32[]{:S(2)}, u32[]{:S(2)}) collective-permute-start(bf16[256,128]{1,0:T(8,128)(2,1)S(1)} %get-tuple-element.50), channel_id=1, source_target_pairs={{0,96},{32,0},{64,32},{96,64},{1,97},{33,1},{65,33},{97,65},{2,98}... | collective-permute-start | bytes 196616 | tf_op jit(solution)/shard_map/ppermute | solution.py:292
  134.4 3.5 %collective-permute-done.51.refs_3_ = bf16[256,128]{1,0:T(8,128)(2,1)S(1)} collective-permute-done((bf16[256,128]{1,0:T(8,128)(2,1)S(1)}, bf16[256,128]{1,0:T(8,128)(2,1)S(1)}, u32[]{:S(2)}, u32[]{:S(2)}) %collective-permute-start.51) | collective-permute-done | bytes 65568 | tf_op jit(solution)/shard_map/ppermute | solution.py:292
  141.2 3.6 %collective-permute-done.54 = bf16[256,128]{1,0:T(8,128)(2,1)S(1)} collective-permute-done((bf16[256,128]{1,0:T(8,128)(2,1)S(1)}, bf16[256,128]{1,0:T(8,128)(2,1)S(1)}, u32[]{:S(2)}, u32[]{:S(2)}) %collective-permute-start.54) | collective-permute-done | bytes 65568 | tf_op jit(solution)/shard_map/ppermute | solution.py:285
  146.4 1.7 collective-permute-start.57
  150.2 4.2 %collective-permute-done.57.refs_3_ = bf16[4,256,128]{2,1,0:T(8,128)(2,1)S(1)} collective-permute-done((bf16[4,256,128]{2,1,0:T(8,128)(2,1)S(1)}, bf16[4,256,128]{2,1,0:T(8,128)(2,1)S(1)}, u32[]{:S(2)}, u32[]{:S(2)}) %collective-permute-start.57) | collective-permute-done | bytes 262176 | tf_op jit(solution)/shard_map/ppermute | solution.py:287
  154.3 2.8 %collective-permute-done.56.refs_2_ = bf16[4,256,128]{2,1,0:T(8,128)(2,1)S(1)} collective-permute-done((bf16[4,256,128]{2,1,0:T(8,128)(2,1)S(1)}, bf16[4,256,128]{2,1,0:T(8,128)(2,1)S(1)}, u32[]{:S(2)}, u32[]{:S(2)}) %collective-permute-start.56) | collective-permute-done | bytes 262176 | tf_op jit(solution)/shard_map/ppermute | solution.py:287
  160.6 2.6 %collective-permute-start.63 = (bf16[256,128]{1,0:T(8,128)(2,1)S(1)}, bf16[256,128]{1,0:T(8,128)(2,1)S(1)}, u32[]{:S(2)}, u32[]{:S(2)}) collective-permute-start(bf16[256,128]{1,0:T(8,128)(2,1)S(1)} %get-tuple-element.55), channel_id=1, source_target_pairs={{0,96},{32,0},{64,32},{96,64},{1,97},{33,1},{65,33},{97,65},{2,98}... | collective-permute-start | bytes 196616 | tf_op jit(solution)/shard_map/ppermute | solution.py:292
  163.6 1.9 collective-permute-done.62.refs_1_
  166.1 3.0 %collective-permute-done.64.refs_3_ = bf16[256,128]{1,0:T(8,128)(2,1)S(1)} collective-permute-done((bf16[256,128]{1,0:T(8,128)(2,1)S(1)}, bf16[256,128]{1,0:T(8,128)(2,1)S(1)}, u32[]{:S(2)}, u32[]{:S(2)}) %collective-permute-start.64) | collective-permute-done | bytes 65568 | tf_op jit(solution)/shard_map/ppermute | solution.py:292
  173.8 2.2 %collective-permute-done.67 = bf16[256,128]{1,0:T(8,128)(2,1)S(1)} collective-permute-done((bf16[256,128]{1,0:T(8,128)(2,1)S(1)}, bf16[256,128]{1,0:T(8,128)(2,1)S(1)}, u32[]{:S(2)}, u32[]{:S(2)}) %collective-permute-start.67) | collective-permute-done | bytes 65568 | tf_op jit(solution)/shard_map/ppermute | solution.py:285
  177.6 2.4 %collective-permute-start.70 = (bf16[4,256,128]{2,1,0:T(8,128)(2,1)S(1)}, bf16[4,256,128]{2,1,0:T(8,128)(2,1)S(1)}, u32[]{:S(2)}, u32[]{:S(2)}) collective-permute-start(bf16[4,256,128]{2,1,0:T(8,128)(2,1)S(1)} %pad_maximum_fusion.4.refs_0_), channel_id=1, source_target_pairs={{0,16},{1,5},{2,18},{3,7},{4,20},{5,1},{6,22},{7,3},{8,24},{9,13},... | collective-permute-start | bytes 786440 | tf_op jit(solution)/shard_map/ppermute | solution.py:287
  182.0 3.5 %collective-permute-done.70.refs_3_ = bf16[4,256,128]{2,1,0:T(8,128)(2,1)S(1)} collective-permute-done((bf16[4,256,128]{2,1,0:T(8,128)(2,1)S(1)}, bf16[4,256,128]{2,1,0:T(8,128)(2,1)S(1)}, u32[]{:S(2)}, u32[]{:S(2)}) %collective-permute-start.70) | collective-permute-done | bytes 262176 | tf_op jit(solution)/shard_map/ppermute | solution.py:287
  185.6 2.8 %collective-permute-done.69.refs_2_ = bf16[4,256,128]{2,1,0:T(8,128)(2,1)S(1)} collective-permute-done((bf16[4,256,128]{2,1,0:T(8,128)(2,1)S(1)}, bf16[4,256,128]{2,1,0:T(8,128)(2,1)S(1)}, u32[]{:S(2)}, u32[]{:S(2)}) %collective-permute-start.69) | collective-permute-done | bytes 262176 | tf_op jit(solution)/shard_map/ppermute | solution.py:287
  191.6 3.2 %collective-permute-start.76 = (bf16[256,128]{1,0:T(8,128)(2,1)S(1)}, bf16[256,128]{1,0:T(8,128)(2,1)S(1)}, u32[]{:S(2)}, u32[]{:S(2)}) collective-permute-start(bf16[256,128]{1,0:T(8,128)(2,1)S(1)} %get-tuple-element.60), channel_id=1, source_target_pairs={{0,96},{32,0},{64,32},{96,64},{1,97},{33,1},{65,33},{97,65},{2,98}... | collective-permute-start | bytes 196616 | tf_op jit(solution)/shard_map/ppermute | solution.py:292
  194.8 2.2 %collective-permute-done.75.refs_1_ = bf16[256,128]{1,0:T(8,128)(2,1)S(1)} collective-permute-done((bf16[256,128]{1,0:T(8,128)(2,1)S(1)}, bf16[256,128]{1,0:T(8,128)(2,1)S(1)}, u32[]{:S(2)}, u32[]{:S(2)}) %collective-permute-start.75) | collective-permute-done | bytes 65568 | tf_op jit(solution)/shard_map/ppermute | solution.py:292
  197.6 3.0 %collective-permute-done.77.refs_3_ = bf16[256,128]{1,0:T(8,128)(2,1)S(1)} collective-permute-done((bf16[256,128]{1,0:T(8,128)(2,1)S(1)}, bf16[256,128]{1,0:T(8,128)(2,1)S(1)}, u32[]{:S(2)}, u32[]{:S(2)}) %collective-permute-start.77) | collective-permute-done | bytes 65568 | tf_op jit(solution)/shard_map/ppermute | solution.py:292
  (148 shorter events, 68.4 us)
Async XLA Ops:
  3.1 9.6 %collective-permute-start.2 = (bf16[256,128]{1,0:T(8,128)(2,1)S(1)}, bf16[256,128]{1,0:T(8,128)(2,1)S(1)}, u32[]{:S(2)}, u32[]{:S(2)}) collective-permute-start(bf16[256,128]{1,0:T(8,128)(2,1)S(1)} %solve.7.refs_0_), channel_id=1, source_target_pairs={{0,4},{1,17},{2,6},{3,19},{4,0},{5,21},{6,2},{7,23},{8,12},{9,25},... | collective-permute-start | bytes 196616 | tf_op jit(solution)/shard_map/ppermute | solution.py:285
  6.5 6.3 %collective-permute-start.1 = (bf16[256,128]{1,0:T(8,128)(2,1)S(1)}, bf16[256,128]{1,0:T(8,128)(2,1)S(1)}, u32[]{:S(2)}, u32[]{:S(2)}) collective-permute-start(bf16[256,128]{1,0:T(8,128)(2,1)S(1)} %solve.7.refs_0_), channel_id=1, source_target_pairs={{0,6},{1,25},{2,0},{3,27},{4,2},{5,29},{6,4},{7,31},{8,14},{9,1},{... | collective-permute-start | bytes 196616 | tf_op jit(solution)/shard_map/ppermute | solution.py:285
  13.3 8.0 %collective-permute-start.5 = (bf16[4,256,128]{2,1,0:T(8,128)(2,1)S(1)}, bf16[4,256,128]{2,1,0:T(8,128)(2,1)S(1)}, u32[]{:S(2)}, u32[]{:S(2)}) collective-permute-start(bf16[4,256,128]{2,1,0:T(8,128)(2,1)S(1)} %stack_after.1.refs_0_), channel_id=1, source_target_pairs={{0,16},{1,5},{2,18},{3,7},{4,20},{5,1},{6,22},{7,3},{8,24},{9,13},... | collective-permute-start | bytes 786440 | tf_op jit(solution)/shard_map/ppermute | solution.py:287
  16.5 7.7 %collective-permute-start.4 = (bf16[4,256,128]{2,1,0:T(8,128)(2,1)S(1)}, bf16[4,256,128]{2,1,0:T(8,128)(2,1)S(1)}, u32[]{:S(2)}, u32[]{:S(2)}) collective-permute-start(bf16[4,256,128]{2,1,0:T(8,128)(2,1)S(1)} %stack_after.1.refs_0_), channel_id=1, source_target_pairs={{0,24},{1,7},{2,26},{3,1},{4,28},{5,3},{6,30},{7,5},{8,0},{9,15},{... | collective-permute-start | bytes 786440 | tf_op jit(solution)/shard_map/ppermute | solution.py:287
  17.6 7.6 %collective-permute-start.3 = (bf16[4,256,128]{2,1,0:T(8,128)(2,1)S(1)}, bf16[4,256,128]{2,1,0:T(8,128)(2,1)S(1)}, u32[]{:S(2)}, u32[]{:S(2)}) collective-permute-start(bf16[4,256,128]{2,1,0:T(8,128)(2,1)S(1)} %stack_after.1.refs_0_), channel_id=1, source_target_pairs={{0,8},{1,3},{2,10},{3,5},{4,12},{5,7},{6,14},{7,1},{8,16},{9,11},{... | collective-permute-start | bytes 786440 | tf_op jit(solution)/shard_map/ppermute | solution.py:287
  18.5 6.6 %collective-permute-start.6 = (bf16[4,256,128]{2,1,0:T(8,128)(2,1)S(1)}, bf16[4,256,128]{2,1,0:T(8,128)(2,1)S(1)}, u32[]{:S(2)}, u32[]{:S(2)}) collective-permute-start(bf16[4,256,128]{2,1,0:T(8,128)(2,1)S(1)} %stack_after.1.refs_0_), channel_id=1, source_target_pairs={{0,1},{1,0},{2,3},{3,2},{4,5},{5,4},{6,7},{7,6},{8,9},{9,8},{10,11... | collective-permute-start | bytes 786440 | tf_op jit(solution)/shard_map/ppermute | solution.py:288
  28.6 5.9 %collective-permute-start.10 = (bf16[256,128]{1,0:T(8,128)(2,1)S(1)}, bf16[256,128]{1,0:T(8,128)(2,1)S(1)}, u32[]{:S(2)}, u32[]{:S(2)}) collective-permute-start(bf16[256,128]{1,0:T(8,128)(2,1)S(1)} %get-tuple-element.33), channel_id=1, source_target_pairs={{0,32},{32,64},{64,96},{96,0},{1,33},{33,65},{65,97},{97,1},{2,34}... | collective-permute-start | bytes 196616 | tf_op jit(solution)/shard_map/ppermute | solution.py:292
  31.9 6.4 %collective-permute-start.12 = (bf16[256,128]{1,0:T(8,128)(2,1)S(1)}, bf16[256,128]{1,0:T(8,128)(2,1)S(1)}, u32[]{:S(2)}, u32[]{:S(2)}) collective-permute-start(bf16[256,128]{1,0:T(8,128)(2,1)S(1)} %get-tuple-element.35), channel_id=1, source_target_pairs={{0,64},{32,96},{64,0},{96,32},{1,65},{33,97},{65,1},{97,33},{2,66}... | collective-permute-start | bytes 196616 | tf_op jit(solution)/shard_map/ppermute | solution.py:292
  39.4 5.8 %collective-permute-start.15 = (bf16[256,128]{1,0:T(8,128)(2,1)S(1)}, bf16[256,128]{1,0:T(8,128)(2,1)S(1)}, u32[]{:S(2)}, u32[]{:S(2)}) collective-permute-start(bf16[256,128]{1,0:T(8,128)(2,1)S(1)} %solve.8), channel_id=1, source_target_pairs={{0,4},{1,17},{2,6},{3,19},{4,0},{5,21},{6,2},{7,23},{8,12},{9,25},... | collective-permute-start | bytes 196616 | tf_op jit(solution)/shard_map/ppermute | solution.py:285
  40.0 6.4 %collective-permute-start.14 = (bf16[256,128]{1,0:T(8,128)(2,1)S(1)}, bf16[256,128]{1,0:T(8,128)(2,1)S(1)}, u32[]{:S(2)}, u32[]{:S(2)}) collective-permute-start(bf16[256,128]{1,0:T(8,128)(2,1)S(1)} %solve.8), channel_id=1, source_target_pairs={{0,6},{1,25},{2,0},{3,27},{4,2},{5,29},{6,4},{7,31},{8,14},{9,1},{... | collective-permute-start | bytes 196616 | tf_op jit(solution)/shard_map/ppermute | solution.py:285
  48.5 9.5 %collective-permute-start.18 = (bf16[4,256,128]{2,1,0:T(8,128)(2,1)S(1)}, bf16[4,256,128]{2,1,0:T(8,128)(2,1)S(1)}, u32[]{:S(2)}, u32[]{:S(2)}) collective-permute-start(bf16[4,256,128]{2,1,0:T(8,128)(2,1)S(1)} %pad_maximum_fusion.refs_0_), channel_id=1, source_target_pairs={{0,16},{1,5},{2,18},{3,7},{4,20},{5,1},{6,22},{7,3},{8,24},{9,13},... | collective-permute-start | bytes 786440 | tf_op jit(solution)/shard_map/ppermute | solution.py:287
  53.6 8.0 %collective-permute-start.17 = (bf16[4,256,128]{2,1,0:T(8,128)(2,1)S(1)}, bf16[4,256,128]{2,1,0:T(8,128)(2,1)S(1)}, u32[]{:S(2)}, u32[]{:S(2)}) collective-permute-start(bf16[4,256,128]{2,1,0:T(8,128)(2,1)S(1)} %pad_maximum_fusion.refs_0_), channel_id=1, source_target_pairs={{0,24},{1,7},{2,26},{3,1},{4,28},{5,3},{6,30},{7,5},{8,0},{9,15},{... | collective-permute-start | bytes 786440 | tf_op jit(solution)/shard_map/ppermute | solution.py:287
  53.6 8.0 %collective-permute-start.16 = (bf16[4,256,128]{2,1,0:T(8,128)(2,1)S(1)}, bf16[4,256,128]{2,1,0:T(8,128)(2,1)S(1)}, u32[]{:S(2)}, u32[]{:S(2)}) collective-permute-start(bf16[4,256,128]{2,1,0:T(8,128)(2,1)S(1)} %pad_maximum_fusion.refs_0_), channel_id=1, source_target_pairs={{0,8},{1,3},{2,10},{3,5},{4,12},{5,7},{6,14},{7,1},{8,16},{9,11},{... | collective-permute-start | bytes 786440 | tf_op jit(solution)/shard_map/ppermute | solution.py:287
  55.7 6.5 %collective-permute-start.19 = (bf16[4,256,128]{2,1,0:T(8,128)(2,1)S(1)}, bf16[4,256,128]{2,1,0:T(8,128)(2,1)S(1)}, u32[]{:S(2)}, u32[]{:S(2)}) collective-permute-start(bf16[4,256,128]{2,1,0:T(8,128)(2,1)S(1)} %pad_maximum_fusion.refs_0_), channel_id=1, source_target_pairs={{0,1},{1,0},{2,3},{3,2},{4,5},{5,4},{6,7},{7,6},{8,9},{9,8},{10,11... | collective-permute-start | bytes 786440 | tf_op jit(solution)/shard_map/ppermute | solution.py:288
  64.5 6.1 %collective-permute-start.23 = (bf16[256,128]{1,0:T(8,128)(2,1)S(1)}, bf16[256,128]{1,0:T(8,128)(2,1)S(1)}, u32[]{:S(2)}, u32[]{:S(2)}) collective-permute-start(bf16[256,128]{1,0:T(8,128)(2,1)S(1)} %get-tuple-element.38), channel_id=1, source_target_pairs={{0,32},{32,64},{64,96},{96,0},{1,33},{33,65},{65,97},{97,1},{2,34}... | collective-permute-start | bytes 196616 | tf_op jit(solution)/shard_map/ppermute | solution.py:292
  64.5 6.0 %collective-permute-start.24 = (bf16[256,128]{1,0:T(8,128)(2,1)S(1)}, bf16[256,128]{1,0:T(8,128)(2,1)S(1)}, u32[]{:S(2)}, u32[]{:S(2)}) collective-permute-start(bf16[256,128]{1,0:T(8,128)(2,1)S(1)} %get-tuple-element.39), channel_id=1, source_target_pairs={{0,96},{32,0},{64,32},{96,64},{1,97},{33,1},{65,33},{97,65},{2,98}... | collective-permute-start | bytes 196616 | tf_op jit(solution)/shard_map/ppermute | solution.py:292
  67.8 5.9 %collective-permute-start.25 = (bf16[256,128]{1,0:T(8,128)(2,1)S(1)}, bf16[256,128]{1,0:T(8,128)(2,1)S(1)}, u32[]{:S(2)}, u32[]{:S(2)}) collective-permute-start(bf16[256,128]{1,0:T(8,128)(2,1)S(1)} %get-tuple-element.40), channel_id=1, source_target_pairs={{0,64},{32,96},{64,0},{96,32},{1,65},{33,97},{65,1},{97,33},{2,66}... | collective-permute-start | bytes 196616 | tf_op jit(solution)/shard_map/ppermute | solution.py:292
  74.7 5.8 %collective-permute-start.28 = (bf16[256,128]{1,0:T(8,128)(2,1)S(1)}, bf16[256,128]{1,0:T(8,128)(2,1)S(1)}, u32[]{:S(2)}, u32[]{:S(2)}) collective-permute-start(bf16[256,128]{1,0:T(8,128)(2,1)S(1)} %solve.9), channel_id=1, source_target_pairs={{0,4},{1,17},{2,6},{3,19},{4,0},{5,21},{6,2},{7,23},{8,12},{9,25},... | collective-permute-start | bytes 196616 | tf_op jit(solution)/shard_map/ppermute | solution.py:285
  82.0 8.0 %collective-permute-start.31 = (bf16[4,256,128]{2,1,0:T(8,128)(2,1)S(1)}, bf16[4,256,128]{2,1,0:T(8,128)(2,1)S(1)}, u32[]{:S(2)}, u32[]{:S(2)}) collective-permute-start(bf16[4,256,128]{2,1,0:T(8,128)(2,1)S(1)} %pad_maximum_fusion.1.refs_0_), channel_id=1, source_target_pairs={{0,16},{1,5},{2,18},{3,7},{4,20},{5,1},{6,22},{7,3},{8,24},{9,13},... | collective-permute-start | bytes 786440 | tf_op jit(solution)/shard_map/ppermute | solution.py:287
  83.9 8.5 %collective-permute-start.30 = (bf16[4,256,128]{2,1,0:T(8,128)(2,1)S(1)}, bf16[4,256,128]{2,1,0:T(8,128)(2,1)S(1)}, u32[]{:S(2)}, u32[]{:S(2)}) collective-permute-start(bf16[4,256,128]{2,1,0:T(8,128)(2,1)S(1)} %pad_maximum_fusion.1.refs_0_), channel_id=1, source_target_pairs={{0,24},{1,7},{2,26},{3,1},{4,28},{5,3},{6,30},{7,5},{8,0},{9,15},{... | collective-permute-start | bytes 786440 | tf_op jit(solution)/shard_map/ppermute | solution.py:287
  84.9 7.9 %collective-permute-start.29 = (bf16[4,256,128]{2,1,0:T(8,128)(2,1)S(1)}, bf16[4,256,128]{2,1,0:T(8,128)(2,1)S(1)}, u32[]{:S(2)}, u32[]{:S(2)}) collective-permute-start(bf16[4,256,128]{2,1,0:T(8,128)(2,1)S(1)} %pad_maximum_fusion.1.refs_0_), channel_id=1, source_target_pairs={{0,8},{1,3},{2,10},{3,5},{4,12},{5,7},{6,14},{7,1},{8,16},{9,11},{... | collective-permute-start | bytes 786440 | tf_op jit(solution)/shard_map/ppermute | solution.py:287
  85.9 7.0 %collective-permute-start.32 = (bf16[4,256,128]{2,1,0:T(8,128)(2,1)S(1)}, bf16[4,256,128]{2,1,0:T(8,128)(2,1)S(1)}, u32[]{:S(2)}, u32[]{:S(2)}) collective-permute-start(bf16[4,256,128]{2,1,0:T(8,128)(2,1)S(1)} %pad_maximum_fusion.1.refs_0_), channel_id=1, source_target_pairs={{0,1},{1,0},{2,3},{3,2},{4,5},{5,4},{6,7},{7,6},{8,9},{9,8},{10,11... | collective-permute-start | bytes 786440 | tf_op jit(solution)/shard_map/ppermute | solution.py:288
  95.2 5.5 %collective-permute-start.36 = (bf16[256,128]{1,0:T(8,128)(2,1)S(1)}, bf16[256,128]{1,0:T(8,128)(2,1)S(1)}, u32[]{:S(2)}, u32[]{:S(2)}) collective-permute-start(bf16[256,128]{1,0:T(8,128)(2,1)S(1)} %get-tuple-element.43), channel_id=1, source_target_pairs={{0,32},{32,64},{64,96},{96,0},{1,33},{33,65},{65,97},{97,1},{2,34}... | collective-permute-start | bytes 196616 | tf_op jit(solution)/shard_map/ppermute | solution.py:292
  95.3 6.0 %collective-permute-start.37 = (bf16[256,128]{1,0:T(8,128)(2,1)S(1)}, bf16[256,128]{1,0:T(8,128)(2,1)S(1)}, u32[]{:S(2)}, u32[]{:S(2)}) collective-permute-start(bf16[256,128]{1,0:T(8,128)(2,1)S(1)} %get-tuple-element.44), channel_id=1, source_target_pairs={{0,96},{32,0},{64,32},{96,64},{1,97},{33,1},{65,33},{97,65},{2,98}... | collective-permute-start | bytes 196616 | tf_op jit(solution)/shard_map/ppermute | solution.py:292
  98.5 5.8 %collective-permute-start.38 = (bf16[256,128]{1,0:T(8,128)(2,1)S(1)}, bf16[256,128]{1,0:T(8,128)(2,1)S(1)}, u32[]{:S(2)}, u32[]{:S(2)}) collective-permute-start(bf16[256,128]{1,0:T(8,128)(2,1)S(1)} %get-tuple-element.45), channel_id=1, source_target_pairs={{0,64},{32,96},{64,0},{96,32},{1,65},{33,97},{65,1},{97,33},{2,66}... | collective-permute-start | bytes 196616 | tf_op jit(solution)/shard_map/ppermute | solution.py:292
  106.2 5.8 %collective-permute-start.41 = (bf16[256,128]{1,0:T(8,128)(2,1)S(1)}, bf16[256,128]{1,0:T(8,128)(2,1)S(1)}, u32[]{:S(2)}, u32[]{:S(2)}) collective-permute-start(bf16[256,128]{1,0:T(8,128)(2,1)S(1)} %get-tuple-element.47), channel_id=1, source_target_pairs={{0,4},{1,17},{2,6},{3,19},{4,0},{5,21},{6,2},{7,23},{8,12},{9,25},... | collective-permute-start | bytes 196616 | tf_op jit(solution)/shard_map/ppermute | solution.py:285
  115.0 8.0 %collective-permute-start.44 = (bf16[4,256,128]{2,1,0:T(8,128)(2,1)S(1)}, bf16[4,256,128]{2,1,0:T(8,128)(2,1)S(1)}, u32[]{:S(2)}, u32[]{:S(2)}) collective-permute-start(bf16[4,256,128]{2,1,0:T(8,128)(2,1)S(1)} %pad_maximum_fusion.2.refs_0_), channel_id=1, source_target_pairs={{0,16},{1,5},{2,18},{3,7},{4,20},{5,1},{6,22},{7,3},{8,24},{9,13},... | collective-permute-start | bytes 786440 | tf_op jit(solution)/shard_map/ppermute | solution.py:287
  116.5 9.0 %collective-permute-start.43 = (bf16[4,256,128]{2,1,0:T(8,128)(2,1)S(1)}, bf16[4,256,128]{2,1,0:T(8,128)(2,1)S(1)}, u32[]{:S(2)}, u32[]{:S(2)}) collective-permute-start(bf16[4,256,128]{2,1,0:T(8,128)(2,1)S(1)} %pad_maximum_fusion.2.refs_0_), channel_id=1, source_target_pairs={{0,24},{1,7},{2,26},{3,1},{4,28},{5,3},{6,30},{7,5},{8,0},{9,15},{... | collective-permute-start | bytes 786440 | tf_op jit(solution)/shard_map/ppermute | solution.py:287
  118.8 7.6 %collective-permute-start.42 = (bf16[4,256,128]{2,1,0:T(8,128)(2,1)S(1)}, bf16[4,256,128]{2,1,0:T(8,128)(2,1)S(1)}, u32[]{:S(2)}, u32[]{:S(2)}) collective-permute-start(bf16[4,256,128]{2,1,0:T(8,128)(2,1)S(1)} %pad_maximum_fusion.2.refs_0_), channel_id=1, source_target_pairs={{0,8},{1,3},{2,10},{3,5},{4,12},{5,7},{6,14},{7,1},{8,16},{9,11},{... | collective-permute-start | bytes 786440 | tf_op jit(solution)/shard_map/ppermute | solution.py:287
  118.8 7.6 %collective-permute-start.45 = (bf16[4,256,128]{2,1,0:T(8,128)(2,1)S(1)}, bf16[4,256,128]{2,1,0:T(8,128)(2,1)S(1)}, u32[]{:S(2)}, u32[]{:S(2)}) collective-permute-start(bf16[4,256,128]{2,1,0:T(8,128)(2,1)S(1)} %pad_maximum_fusion.2.refs_0_), channel_id=1, source_target_pairs={{0,1},{1,0},{2,3},{3,2},{4,5},{5,4},{6,7},{7,6},{8,9},{9,8},{10,11... | collective-permute-start | bytes 786440 | tf_op jit(solution)/shard_map/ppermute | solution.py:288
  128.9 5.5 %collective-permute-start.49 = (bf16[256,128]{1,0:T(8,128)(2,1)S(1)}, bf16[256,128]{1,0:T(8,128)(2,1)S(1)}, u32[]{:S(2)}, u32[]{:S(2)}) collective-permute-start(bf16[256,128]{1,0:T(8,128)(2,1)S(1)} %get-tuple-element.49), channel_id=1, source_target_pairs={{0,32},{32,64},{64,96},{96,0},{1,33},{33,65},{65,97},{97,1},{2,34}... | collective-permute-start | bytes 196616 | tf_op jit(solution)/shard_map/ppermute | solution.py:292
  132.2 5.8 %collective-permute-start.51 = (bf16[256,128]{1,0:T(8,128)(2,1)S(1)}, bf16[256,128]{1,0:T(8,128)(2,1)S(1)}, u32[]{:S(2)}, u32[]{:S(2)}) collective-permute-start(bf16[256,128]{1,0:T(8,128)(2,1)S(1)} %get-tuple-element.51), channel_id=1, source_target_pairs={{0,64},{32,96},{64,0},{96,32},{1,65},{33,97},{65,1},{97,33},{2,66}... | collective-permute-start | bytes 196616 | tf_op jit(solution)/shard_map/ppermute | solution.py:292
  139.0 5.8 %collective-permute-start.54 = (bf16[256,128]{1,0:T(8,128)(2,1)S(1)}, bf16[256,128]{1,0:T(8,128)(2,1)S(1)}, u32[]{:S(2)}, u32[]{:S(2)}) collective-permute-start(bf16[256,128]{1,0:T(8,128)(2,1)S(1)} %solve.11), channel_id=1, source_target_pairs={{0,4},{1,17},{2,6},{3,19},{4,0},{5,21},{6,2},{7,23},{8,12},{9,25},... | collective-permute-start | bytes 196616 | tf_op jit(solution)/shard_map/ppermute | solution.py:285
  139.2 5.7 %collective-permute-start.53 = (bf16[256,128]{1,0:T(8,128)(2,1)S(1)}, bf16[256,128]{1,0:T(8,128)(2,1)S(1)}, u32[]{:S(2)}, u32[]{:S(2)}) collective-permute-start(bf16[256,128]{1,0:T(8,128)(2,1)S(1)} %solve.11), channel_id=1, source_target_pairs={{0,6},{1,25},{2,0},{3,27},{4,2},{5,29},{6,4},{7,31},{8,14},{9,1},{... | collective-permute-start | bytes 196616 | tf_op jit(solution)/shard_map/ppermute | solution.py:285
  146.4 8.0 %collective-permute-start.57 = (bf16[4,256,128]{2,1,0:T(8,128)(2,1)S(1)}, bf16[4,256,128]{2,1,0:T(8,128)(2,1)S(1)}, u32[]{:S(2)}, u32[]{:S(2)}) collective-permute-start(bf16[4,256,128]{2,1,0:T(8,128)(2,1)S(1)} %pad_maximum_fusion.3.refs_0_), channel_id=1, source_target_pairs={{0,16},{1,5},{2,18},{3,7},{4,20},{5,1},{6,22},{7,3},{8,24},{9,13},... | collective-permute-start | bytes 786440 | tf_op jit(solution)/shard_map/ppermute | solution.py:287
  148.1 9.0 %collective-permute-start.56 = (bf16[4,256,128]{2,1,0:T(8,128)(2,1)S(1)}, bf16[4,256,128]{2,1,0:T(8,128)(2,1)S(1)}, u32[]{:S(2)}, u32[]{:S(2)}) collective-permute-start(bf16[4,256,128]{2,1,0:T(8,128)(2,1)S(1)} %pad_maximum_fusion.3.refs_0_), channel_id=1, source_target_pairs={{0,24},{1,7},{2,26},{3,1},{4,28},{5,3},{6,30},{7,5},{8,0},{9,15},{... | collective-permute-start | bytes 786440 | tf_op jit(solution)/shard_map/ppermute | solution.py:287
  149.7 7.6 %collective-permute-start.55 = (bf16[4,256,128]{2,1,0:T(8,128)(2,1)S(1)}, bf16[4,256,128]{2,1,0:T(8,128)(2,1)S(1)}, u32[]{:S(2)}, u32[]{:S(2)}) collective-permute-start(bf16[4,256,128]{2,1,0:T(8,128)(2,1)S(1)} %pad_maximum_fusion.3.refs_0_), channel_id=1, source_target_pairs={{0,8},{1,3},{2,10},{3,5},{4,12},{5,7},{6,14},{7,1},{8,16},{9,11},{... | collective-permute-start | bytes 786440 | tf_op jit(solution)/shard_map/ppermute | solution.py:287
  150.1 7.5 %collective-permute-start.58 = (bf16[4,256,128]{2,1,0:T(8,128)(2,1)S(1)}, bf16[4,256,128]{2,1,0:T(8,128)(2,1)S(1)}, u32[]{:S(2)}, u32[]{:S(2)}) collective-permute-start(bf16[4,256,128]{2,1,0:T(8,128)(2,1)S(1)} %pad_maximum_fusion.3.refs_0_), channel_id=1, source_target_pairs={{0,1},{1,0},{2,3},{3,2},{4,5},{5,4},{6,7},{7,6},{8,9},{9,8},{10,11... | collective-permute-start | bytes 786440 | tf_op jit(solution)/shard_map/ppermute | solution.py:288
  160.0 5.5 %collective-permute-start.62 = (bf16[256,128]{1,0:T(8,128)(2,1)S(1)}, bf16[256,128]{1,0:T(8,128)(2,1)S(1)}, u32[]{:S(2)}, u32[]{:S(2)}) collective-permute-start(bf16[256,128]{1,0:T(8,128)(2,1)S(1)} %get-tuple-element.54), channel_id=1, source_target_pairs={{0,32},{32,64},{64,96},{96,0},{1,33},{33,65},{65,97},{97,1},{2,34}... | collective-permute-start | bytes 196616 | tf_op jit(solution)/shard_map/ppermute | solution.py:292
  163.3 5.8 %collective-permute-start.64 = (bf16[256,128]{1,0:T(8,128)(2,1)S(1)}, bf16[256,128]{1,0:T(8,128)(2,1)S(1)}, u32[]{:S(2)}, u32[]{:S(2)}) collective-permute-start(bf16[256,128]{1,0:T(8,128)(2,1)S(1)} %get-tuple-element.56), channel_id=1, source_target_pairs={{0,64},{32,96},{64,0},{96,32},{1,65},{33,97},{65,1},{97,33},{2,66}... | collective-permute-start | bytes 196616 | tf_op jit(solution)/shard_map/ppermute | solution.py:292
  170.1 5.8 %collective-permute-start.67 = (bf16[256,128]{1,0:T(8,128)(2,1)S(1)}, bf16[256,128]{1,0:T(8,128)(2,1)S(1)}, u32[]{:S(2)}, u32[]{:S(2)}) collective-permute-start(bf16[256,128]{1,0:T(8,128)(2,1)S(1)} %solve.12), channel_id=1, source_target_pairs={{0,4},{1,17},{2,6},{3,19},{4,0},{5,21},{6,2},{7,23},{8,12},{9,25},... | collective-permute-start | bytes 196616 | tf_op jit(solution)/shard_map/ppermute | solution.py:285
  177.6 8.0 %collective-permute-start.70 = (bf16[4,256,128]{2,1,0:T(8,128)(2,1)S(1)}, bf16[4,256,128]{2,1,0:T(8,128)(2,1)S(1)}, u32[]{:S(2)}, u32[]{:S(2)}) collective-permute-start(bf16[4,256,128]{2,1,0:T(8,128)(2,1)S(1)} %pad_maximum_fusion.4.refs_0_), channel_id=1, source_target_pairs={{0,16},{1,5},{2,18},{3,7},{4,20},{5,1},{6,22},{7,3},{8,24},{9,13},... | collective-permute-start | bytes 786440 | tf_op jit(solution)/shard_map/ppermute | solution.py:287
  180.0 8.4 %collective-permute-start.69 = (bf16[4,256,128]{2,1,0:T(8,128)(2,1)S(1)}, bf16[4,256,128]{2,1,0:T(8,128)(2,1)S(1)}, u32[]{:S(2)}, u32[]{:S(2)}) collective-permute-start(bf16[4,256,128]{2,1,0:T(8,128)(2,1)S(1)} %pad_maximum_fusion.4.refs_0_), channel_id=1, source_target_pairs={{0,24},{1,7},{2,26},{3,1},{4,28},{5,3},{6,30},{7,5},{8,0},{9,15},{... | collective-permute-start | bytes 786440 | tf_op jit(solution)/shard_map/ppermute | solution.py:287
  181.5 7.6 %collective-permute-start.68 = (bf16[4,256,128]{2,1,0:T(8,128)(2,1)S(1)}, bf16[4,256,128]{2,1,0:T(8,128)(2,1)S(1)}, u32[]{:S(2)}, u32[]{:S(2)}) collective-permute-start(bf16[4,256,128]{2,1,0:T(8,128)(2,1)S(1)} %pad_maximum_fusion.4.refs_0_), channel_id=1, source_target_pairs={{0,8},{1,3},{2,10},{3,5},{4,12},{5,7},{6,14},{7,1},{8,16},{9,11},{... | collective-permute-start | bytes 786440 | tf_op jit(solution)/shard_map/ppermute | solution.py:287
  182.0 7.0 %collective-permute-start.71 = (bf16[4,256,128]{2,1,0:T(8,128)(2,1)S(1)}, bf16[4,256,128]{2,1,0:T(8,128)(2,1)S(1)}, u32[]{:S(2)}, u32[]{:S(2)}) collective-permute-start(bf16[4,256,128]{2,1,0:T(8,128)(2,1)S(1)} %pad_maximum_fusion.4.refs_0_), channel_id=1, source_target_pairs={{0,1},{1,0},{2,3},{3,2},{4,5},{5,4},{6,7},{7,6},{8,9},{9,8},{10,11... | collective-permute-start | bytes 786440 | tf_op jit(solution)/shard_map/ppermute | solution.py:288
  191.5 5.5 %collective-permute-start.75 = (bf16[256,128]{1,0:T(8,128)(2,1)S(1)}, bf16[256,128]{1,0:T(8,128)(2,1)S(1)}, u32[]{:S(2)}, u32[]{:S(2)}) collective-permute-start(bf16[256,128]{1,0:T(8,128)(2,1)S(1)} %get-tuple-element.59), channel_id=1, source_target_pairs={{0,32},{32,64},{64,96},{96,0},{1,33},{33,65},{65,97},{97,1},{2,34}... | collective-permute-start | bytes 196616 | tf_op jit(solution)/shard_map/ppermute | solution.py:292
  191.6 6.0 %collective-permute-start.76 = (bf16[256,128]{1,0:T(8,128)(2,1)S(1)}, bf16[256,128]{1,0:T(8,128)(2,1)S(1)}, u32[]{:S(2)}, u32[]{:S(2)}) collective-permute-start(bf16[256,128]{1,0:T(8,128)(2,1)S(1)} %get-tuple-element.60), channel_id=1, source_target_pairs={{0,96},{32,0},{64,32},{96,64},{1,97},{33,1},{65,33},{97,65},{2,98}... | collective-permute-start | bytes 196616 | tf_op jit(solution)/shard_map/ppermute | solution.py:292
  194.8 5.8 %collective-permute-start.77 = (bf16[256,128]{1,0:T(8,128)(2,1)S(1)}, bf16[256,128]{1,0:T(8,128)(2,1)S(1)}, u32[]{:S(2)}, u32[]{:S(2)}) collective-permute-start(bf16[256,128]{1,0:T(8,128)(2,1)S(1)} %get-tuple-element.61), channel_id=1, source_target_pairs={{0,64},{32,96},{64,0},{96,32},{1,65},{33,97},{65,1},{97,33},{2,66}... | collective-permute-start | bytes 196616 | tf_op jit(solution)/shard_map/ppermute | solution.py:292
  (39 other events, 228.6 us)

commit v3 on v2

--- a/solution.py
+++ b/solution.py
@@ -10,13 +10,14 @@
 B = 256
 R = 128
 SLOTS = 8
-SHIFTS = (0, 1, 3, 2)
+NEAR = (0, 3, 1, 2)
+FAR = (0, 1, 3, 2)
+ACROSS = (0, 2, 1, 3)
 ANY = pl.BlockSpec(memory_space=pl.ANY)
 SMEM = pl.BlockSpec(memory_space=pltpu.SMEM)
 VMEM = pl.BlockSpec(memory_space=pltpu.VMEM)
 HBM = pl.BlockSpec(memory_space=pltpu.HBM)
 LIMIT = 50 * 2**20
-READY = 24
 
 
 def near_pairs(k):
@@ -83,29 +84,6 @@
     )(place, parent, pattern)
 
 
-def ready_kernel(plan, tiles, out, sems):
-    count = jnp.minimum(plan[1, 6], READY)
-    for act in (lambda copy: copy.start(), lambda copy: copy.wait()):
-        for n in range(READY):
-            @pl.when(n < count)
-            def _():
-                code = plan[0, n]
-                act(pltpu.make_async_copy(tiles.at[code >> 5, code & 31], out.at[n], sems.at[n]))
-
-
-def ready_tiles(plan, tiles):
-    return pl.pallas_call(
-        ready_kernel,
-        out_shape=jax.ShapeDtypeStruct((READY, B, B), jnp.bfloat16),
-        in_specs=[SMEM, ANY],
-        out_specs=ANY,
-        scratch_shapes=[pltpu.SemaphoreType.DMA((READY,))],
-        compiler_params=pltpu.CompilerParams(vmem_limit_bytes=LIMIT),
-        cost_estimate=pl.CostEstimate(flops=0, bytes_accessed=2 * READY * B * B * 2, transcendentals=0),
-        name="ready_tiles",
-    )(plan, tiles)
-
-
 def fetch(sources, buffers, sems):
     fetched = [pltpu.make_async_copy(src, buf, sems.at[n]) for n, (src, buf) in enumerate(zip(sources, buffers))]
     for copy in fetched:
@@ -118,7 +96,7 @@
     y_back = ((pcol_at >> 1) - (col >> 1)) & 3
     far = jnp.where((col & 1) == 0, x_back, y_back)
     near = jnp.where((col & 1) == 0, y_back, x_back)
-    near_slot = jnp.where(near == 2, 3, jnp.where(near == 3, 2, near))
+    near_slot = sum(jnp.where(near == shift, n, 0) for n, shift in enumerate(NEAR))
     return (col ^ pcol_at) & 1, far, near_slot
 
 
@@ -126,13 +104,13 @@
     other, far, near_slot = panel_place(pcol_at, col)
     for e in range(2):
         for k in range(4):
-            @pl.when((other == e) & (far == SHIFTS[k]))
+            @pl.when((other == e) & (far == FAR[k]))
             def _():
                 pltpu.make_async_copy(pieces[e * 4 + k].at[near_slot], buffer, sem).start()
 
 
 def tile_kernel(step, plan, scales, place, *refs):
-    pieces, tiles, ready, refs = refs[:8], refs[8], refs[9], refs[10:]
+    pieces, tiles, refs = refs[:8], refs[8], refs[9:]
     before, refs = (refs[0], refs[1:]) if step % 3 > 0 else (None, refs)
     outs, refs = refs[:4], refs[4:]
     after, refs = (refs[0], refs[1:]) if step % 3 < 2 else (None, refs)
@@ -144,23 +122,17 @@
         code = plan[0, n]
         row, col = code >> 5, code & 31
 
-        @pl.when(n < READY)
-        def _():
-            pltpu.make_async_copy(ready.at[n], tile_buf.at[slot], tile_sem.at[slot]).start()
-
-        @pl.when(n >= READY)
-        def _():
-            pltpu.make_async_copy(tiles.at[row, col], tile_buf.at[slot], tile_sem.at[slot]).start()
-
+        pltpu.make_async_copy(tiles.at[row, col], tile_buf.at[slot], tile_sem.at[slot]).start()
         start_panel(pieces, pcol_at, col, panel_buf.at[slot], panel_sem.at[slot])
 
     if step % 3 > 0:
         previous = pltpu.make_async_copy(before, acc, before_sem)
         previous.start()
-    for n in range(SLOTS):
-        @pl.when(first + n < last)
-        def _():
-            start(first + n, n)
+    def begin(n, carry):
+        start(n, n - first)
+        return carry
+
+    lax.fori_loop(first, jnp.minimum(last, first + SLOTS), begin, 0)
 
     if step % 3 > 0:
         previous.wait()
@@ -186,17 +158,17 @@
         after[...] = acc[...]
     outs[0][...] = acc[prow_at]
     for k in range(1, 4):
-        outs[k][...] = acc[(prow_at + SHIFTS[k]) & 3].astype(jnp.bfloat16)
-
-
-def tile_products(step, plan, scales, place, pieces, tiles, ready, before):
+        outs[k][...] = acc[(prow_at + ACROSS[k]) & 3].astype(jnp.bfloat16)
+
+
+def tile_products(step, plan, scales, place, pieces, tiles, before):
     out_shape = [jax.ShapeDtypeStruct((B, R), jnp.float32)] + [jax.ShapeDtypeStruct((B, R), jnp.bfloat16)] * 3
     if step % 3 < 2:
         out_shape = out_shape + [jax.ShapeDtypeStruct((4, B, R), jnp.float32)]
     return pl.pallas_call(
         functools.partial(tile_kernel, step),
         out_shape=out_shape,
-        in_specs=[SMEM] * 3 + [ANY] * (10 + len(before)),
+        in_specs=[SMEM] * 3 + [ANY] * (9 + len(before)),
         out_specs=[VMEM] * len(out_shape),
         scratch_shapes=[
             pltpu.VMEM((4, B, R), jnp.float32),
@@ -209,7 +181,7 @@
         compiler_params=pltpu.CompilerParams(vmem_limit_bytes=LIMIT),
         cost_estimate=pl.CostEstimate(flops=2 * 4 * B * B * R, bytes_accessed=4 * (B * B + B * R) * 2, transcendentals=0),
         name="tile_products",
-    )(plan, scales, place, *pieces, tiles, ready, *before)
+    )(plan, scales, place, *pieces, tiles, *before)
 
 
 def split(vectors):
@@ -257,19 +229,19 @@
         in_specs=[ANY] * (2 + len(sums)),
         out_specs=[VMEM] * len(out_shape),
         scratch_shapes=buffers + [pltpu.VMEM((len(uses), B, B), jnp.bfloat16), pltpu.SemaphoreType.DMA((7,))],
-        compiler_params=pltpu.CompilerParams(vmem_limit_bytes=LIMIT),
+        compiler_params=pltpu.CompilerParams(vmem_limit_bytes=LIMIT if sums else 60 * 2**20),
         cost_estimate=pl.CostEstimate(flops=4 * B * B * R, bytes_accessed=B * R * 20, transcendentals=0),
         name="solve",
     )(target, inverses, *sums)
 
 
-def stack_kernel(ready, *refs):
+def stack_kernel(plan, *refs):
     panels, out, sems = refs[:4], refs[4], refs[5]
     for copy in fetch(panels, [out.at[k] for k in range(4)], sems):
         copy.wait()
 
 
-def stack_after(ready, panels):
+def stack_after(plan, panels):
     return pl.pallas_call(
         stack_kernel,
         out_shape=jax.ShapeDtypeStruct((4, B, R), jnp.bfloat16),
@@ -278,18 +250,18 @@
         scratch_shapes=[pltpu.SemaphoreType.DMA((4,))],
         compiler_params=pltpu.CompilerParams(vmem_limit_bytes=LIMIT),
         name="stack_after",
-    )(ready, *panels)
-
-
-def gather_panels(panel, ready=None):
-    near = [panel] + [lax.ppermute(panel, "pcol", near_pairs(k)) for k in SHIFTS[1:]]
-    near = jnp.stack(near) if ready is None else stack_after(ready, near)
-    far = [near] + [lax.ppermute(near, "pcol", far_pairs(k)) for k in SHIFTS[1:]]
+    )(plan, *panels)
+
+
+def gather_panels(panel, plan=None):
+    near = [panel] + [lax.ppermute(panel, "pcol", near_pairs(k)) for k in NEAR[1:]]
+    near = jnp.stack(near) if plan is None else stack_after(plan, near)
+    far = [near] + [lax.ppermute(near, "pcol", far_pairs(k)) for k in FAR[1:]]
     return far + [lax.ppermute(piece, "pcol", CORE_PAIRS) for piece in far]
 
 
 def across_rows(values):
-    return [lax.ppermute(value, "prow", z_pairs(k)) for value, k in zip(values, SHIFTS[1:])]
+    return [lax.ppermute(value, "prow", z_pairs(k)) for value, k in zip(values, ACROSS[1:])]
 
 
 def shards(right_side, factor_tiles, tile_scales, tile_pattern, parent, inverses):
@@ -300,11 +272,10 @@
     target = right_side[0, 0]
     (rounded,) = solve((0,), target, inverse_pair, ())
     plan = make_plan(place, parent.reshape(1, 128), tile_pattern)
-    ready = ready_tiles(plan, tiles)
     before = ()
     for step in range(6):
-        pieces = gather_panels(rounded, ready if step == 0 else None)
-        parts = tile_products(step, plan, tile_scales, place, pieces, tiles, ready, before)
+        pieces = gather_panels(rounded, plan if step == 0 else None)
+        parts = tile_products(step, plan, tile_scales, place, pieces, tiles, before)
         before = tuple(parts[4:])
         sums = (parts[0], *across_rows(parts[1:4]))
         if step == 2:

time: 204 us -> 195 us (0.956)
  waiting for transfers between devices: 105 us -> 89.8 us
  starting transfers between devices: 75.2 us -> 79 us
  Pallas kernels: 17.9 us -> 20.5 us
    ppermute x18, waiting for transfers between devices: 31.9 us -> 20.3 us  [across_rows(): lax.ppermute(value, 'prow', z_pairs(k))]
    ppermute x18, starting transfers between devices: 22.5 us -> 30.1 us  [gather_panels(): lax.ppermute(panel, 'pcol', near_pairs(k))]
    ppermute x18, waiting for transfers between devices: 22.9 us -> 16.8 us  [gather_panels(): lax.ppermute(panel, 'pcol', near_pairs(k))]
    ppermute x18, starting transfers between devices: 28.3 us -> 22.3 us  [gather_panels(): far = [near] + [lax.ppermute(near, 'pcol', far_pairs(k)) for k in FAR[1:]]]
    ppermute x18, starting transfers between devices: 23.2 us -> 26.6 us  [across_rows(): lax.ppermute(value, 'prow', z_pairs(k))]
    pallas_call x6, Pallas kernels: 6.38 us -> 9.31 us  [tile_products(): pl.pallas_call(functools.partial(tile_kernel, step), out_shape=out_shape,...]
    ppermute x18, waiting for transfers between devices: 41.1 us -> 43.5 us  [gather_panels(): far = [near] + [lax.ppermute(near, 'pcol', far_pairs(k)) for k in FAR[1:]]]
  transfers between devices with their start and end apart: 78 -> 78, of which waited for: 58 -> 59; matrix products, arithmetic and copies ran while one was open for 0% -> 0% of each run, Pallas kernels for 1% -> 1%
where the time goes in v3:
time: 195 us; the launch traced here: 194 us
  waiting for transfers between devices  89.8 us (46%)
  starting transfers between devices  79 us (41%)
  Pallas kernels  20.5 us (11%)
  local copies, waits for them, and re-layouts  2.87 us (1%)
    ppermute x18, waiting for transfers between devices, gather_panels(): far = [near] + [lax.ppermute(near, 'pcol', far_pairs(k)) for k in FAR[1:]]  43.5 us
    ppermute x18, starting transfers between devices, gather_panels(): lax.ppermute(panel, 'pcol', near_pairs(k))  30.1 us
    ppermute x18, starting transfers between devices, across_rows(): lax.ppermute(value, 'prow', z_pairs(k))  26.6 us
    ppermute x18, starting transfers between devices, gather_panels(): far = [near] + [lax.ppermute(near, 'pcol', far_pairs(k)) for k in FAR[1:]]  22.3 us
    ppermute x18, waiting for transfers between devices, across_rows(): lax.ppermute(value, 'prow', z_pairs(k))  20.3 us
    ppermute x18, waiting for transfers between devices, gather_panels(): lax.ppermute(panel, 'pcol', near_pairs(k))  16.8 us
    pallas_call x7, Pallas kernels, solve(): pl.pallas_call(functools.partial(solve_kernel, uses, len(sums), keep, sen...  9.78 us
    pallas_call x6, Pallas kernels, tile_products(): pl.pallas_call(functools.partial(tile_kernel, step), out_shape=out_shape,...  9.31 us
  transfers between devices with their start and end apart: 78, of which 59 were waited for; matrix products, arithmetic and copies ran while one was open for 0% of the time, Pallas kernels for 1%

profile of v3, /device:TPU:0, one launch (start us, length us, event | category | flops | bytes accessed | tf_op | source)
XLA Modules:
  0.0 193.6 jit_solution(6800458669450187309)
XLA Ops:
  0.7 1.9 solve.7.refs_0_
  2.6 3.4 %collective-permute-start.2 = (bf16[256,128]{1,0:T(8,128)(2,1)}, bf16[256,128]{1,0:T(8,128)(2,1)S(1)}, u32[]{:S(2)}, u32[]{:S(2)}) collective-permute-start(bf16[256,128]{1,0:T(8,128)(2,1)} %solve.7.refs_0_), channel_id=1, source_target_pairs={{0,4},{1,17},{2,6},{3,19},{4,0},{5,21},{6,2},{7,23},{8,12},{9,25},... | collective-permute-start | bytes 196616 | tf_op jit(solution)/shard_map/ppermute | solution.py:257
  6.6 2.6 %collective-permute-start = (bf16[256,128]{1,0:T(8,128)(2,1)}, bf16[256,128]{1,0:T(8,128)(2,1)S(1)}, u32[]{:S(2)}, u32[]{:S(2)}) collective-permute-start(bf16[256,128]{1,0:T(8,128)(2,1)} %solve.7.refs_0_), channel_id=1, source_target_pairs={{0,6},{1,25},{2,0},{3,27},{4,2},{5,29},{6,4},{7,31},{8,14},{9,1},{... | collective-permute-start | bytes 196616 | tf_op jit(solution)/shard_map/ppermute | solution.py:257
  12.9 3.1 %collective-permute-start.5 = (bf16[4,256,128]{2,1,0:T(8,128)(2,1)S(1)}, bf16[4,256,128]{2,1,0:T(8,128)(2,1)S(1)}, u32[]{:S(2)}, u32[]{:S(2)}) collective-permute-start(bf16[4,256,128]{2,1,0:T(8,128)(2,1)S(1)} %stack_after.1.refs_0_), channel_id=1, source_target_pairs={{0,16},{1,5},{2,18},{3,7},{4,20},{5,1},{6,22},{7,3},{8,24},{9,13},... | collective-permute-start | bytes 786440 | tf_op jit(solution)/shard_map/ppermute | solution.py:259
  18.1 2.8 %collective-permute-done.5.refs_3_ = bf16[4,256,128]{2,1,0:T(8,128)(2,1)S(1)} collective-permute-done((bf16[4,256,128]{2,1,0:T(8,128)(2,1)S(1)}, bf16[4,256,128]{2,1,0:T(8,128)(2,1)S(1)}, u32[]{:S(2)}, u32[]{:S(2)}) %collective-permute-start.5) | collective-permute-done | bytes 262176 | tf_op jit(solution)/shard_map/ppermute | solution.py:259
  20.9 2.9 %collective-permute-done.4.refs_2_ = bf16[4,256,128]{2,1,0:T(8,128)(2,1)S(1)} collective-permute-done((bf16[4,256,128]{2,1,0:T(8,128)(2,1)S(1)}, bf16[4,256,128]{2,1,0:T(8,128)(2,1)S(1)}, u32[]{:S(2)}, u32[]{:S(2)}) %collective-permute-start.4) | collective-permute-done | bytes 262176 | tf_op jit(solution)/shard_map/ppermute | solution.py:259
  27.0 1.9 tile_products.6
  28.9 2.9 %collective-permute-start.10 = (bf16[256,128]{1,0:T(8,128)(2,1)S(1)}, bf16[256,128]{1,0:T(8,128)(2,1)S(1)}, u32[]{:S(2)}, u32[]{:S(2)}) collective-permute-start(bf16[256,128]{1,0:T(8,128)(2,1)S(1)} %get-tuple-element.33), channel_id=1, source_target_pairs={{0,64},{32,96},{64,0},{96,32},{1,65},{33,97},{65,1},{97,33},{2,66}... | collective-permute-start | bytes 196616 | tf_op jit(solution)/shard_map/ppermute | solution.py:264
  32.8 2.2 %collective-permute-start.12 = (bf16[256,128]{1,0:T(8,128)(2,1)S(1)}, bf16[256,128]{1,0:T(8,128)(2,1)S(1)}, u32[]{:S(2)}, u32[]{:S(2)}) collective-permute-start(bf16[256,128]{1,0:T(8,128)(2,1)S(1)} %get-tuple-element.35), channel_id=1, source_target_pairs={{0,96},{32,0},{64,32},{96,64},{1,97},{33,1},{65,33},{97,65},{2,98}... | collective-permute-start | bytes 196616 | tf_op jit(solution)/shard_map/ppermute | solution.py:264
  35.4 2.4 %collective-permute-done.11.refs_2_ = bf16[256,128]{1,0:T(8,128)(2,1)S(1)} collective-permute-done((bf16[256,128]{1,0:T(8,128)(2,1)S(1)}, bf16[256,128]{1,0:T(8,128)(2,1)S(1)}, u32[]{:S(2)}, u32[]{:S(2)}) %collective-permute-start.11) | collective-permute-done | bytes 65568 | tf_op jit(solution)/shard_map/ppermute | solution.py:264
  40.2 3.8 %collective-permute-start.14 = (bf16[256,128]{1,0:T(8,128)(2,1)S(1)}, bf16[256,128]{1,0:T(8,128)(2,1)S(1)}, u32[]{:S(2)}, u32[]{:S(2)}) collective-permute-start(bf16[256,128]{1,0:T(8,128)(2,1)S(1)} %solve.8), channel_id=1, source_target_pairs={{0,2},{1,9},{2,4},{3,11},{4,6},{5,13},{6,0},{7,15},{8,10},{9,17},{... | collective-permute-start | bytes 196616 | tf_op jit(solution)/shard_map/ppermute | solution.py:257
  46.0 2.4 %collective-permute-done.13 = bf16[256,128]{1,0:T(8,128)(2,1)S(1)} collective-permute-done((bf16[256,128]{1,0:T(8,128)(2,1)S(1)}, bf16[256,128]{1,0:T(8,128)(2,1)S(1)}, u32[]{:S(2)}, u32[]{:S(2)}) %collective-permute-start.13) | collective-permute-done | bytes 65568 | tf_op jit(solution)/shard_map/ppermute | solution.py:257
  51.9 4.5 %collective-permute-done.18.refs_3_ = bf16[4,256,128]{2,1,0:T(8,128)(2,1)S(1)} collective-permute-done((bf16[4,256,128]{2,1,0:T(8,128)(2,1)S(1)}, bf16[4,256,128]{2,1,0:T(8,128)(2,1)S(1)}, u32[]{:S(2)}, u32[]{:S(2)}) %collective-permute-start.18) | collective-permute-done | bytes 262176 | tf_op jit(solution)/shard_map/ppermute | solution.py:259
  56.4 2.2 %collective-permute-done.17.refs_2_ = bf16[4,256,128]{2,1,0:T(8,128)(2,1)S(1)} collective-permute-done((bf16[4,256,128]{2,1,0:T(8,128)(2,1)S(1)}, bf16[4,256,128]{2,1,0:T(8,128)(2,1)S(1)}, u32[]{:S(2)}, u32[]{:S(2)}) %collective-permute-start.17) | collective-permute-done | bytes 262176 | tf_op jit(solution)/shard_map/ppermute | solution.py:259
  60.7 1.9 tile_products.7
  63.1 2.4 %collective-permute-start.24 = (bf16[256,128]{1,0:T(8,128)(2,1)S(1)}, bf16[256,128]{1,0:T(8,128)(2,1)S(1)}, u32[]{:S(2)}, u32[]{:S(2)}) collective-permute-start(bf16[256,128]{1,0:T(8,128)(2,1)S(1)} %get-tuple-element.39), channel_id=1, source_target_pairs={{0,32},{32,64},{64,96},{96,0},{1,33},{33,65},{65,97},{97,1},{2,34}... | collective-permute-start | bytes 196616 | tf_op jit(solution)/shard_map/ppermute | solution.py:264
  66.3 2.6 %collective-permute-done.23.refs_1_ = bf16[256,128]{1,0:T(8,128)(2,1)S(1)} collective-permute-done((bf16[256,128]{1,0:T(8,128)(2,1)S(1)}, bf16[256,128]{1,0:T(8,128)(2,1)S(1)}, u32[]{:S(2)}, u32[]{:S(2)}) %collective-permute-start.23) | collective-permute-done | bytes 65568 | tf_op jit(solution)/shard_map/ppermute | solution.py:264
  71.6 2.6 %collective-permute-start.27 = (bf16[256,128]{1,0:T(8,128)(2,1)S(1)}, bf16[256,128]{1,0:T(8,128)(2,1)S(1)}, u32[]{:S(2)}, u32[]{:S(2)}) collective-permute-start(bf16[256,128]{1,0:T(8,128)(2,1)S(1)} %solve.9), channel_id=1, source_target_pairs={{0,2},{1,9},{2,4},{3,11},{4,6},{5,13},{6,0},{7,15},{8,10},{9,17},{... | collective-permute-start | bytes 196616 | tf_op jit(solution)/shard_map/ppermute | solution.py:257
  74.8 2.3 %collective-permute-done.28 = bf16[256,128]{1,0:T(8,128)(2,1)S(1)} collective-permute-done((bf16[256,128]{1,0:T(8,128)(2,1)S(1)}, bf16[256,128]{1,0:T(8,128)(2,1)S(1)}, u32[]{:S(2)}, u32[]{:S(2)}) %collective-permute-start.28) | collective-permute-done | bytes 65568 | tf_op jit(solution)/shard_map/ppermute | solution.py:257
  82.0 4.5 %collective-permute-done.31.refs_3_ = bf16[4,256,128]{2,1,0:T(8,128)(2,1)S(1)} collective-permute-done((bf16[4,256,128]{2,1,0:T(8,128)(2,1)S(1)}, bf16[4,256,128]{2,1,0:T(8,128)(2,1)S(1)}, u32[]{:S(2)}, u32[]{:S(2)}) %collective-permute-start.31) | collective-permute-done | bytes 262176 | tf_op jit(solution)/shard_map/ppermute | solution.py:259
  86.5 2.1 %collective-permute-done.30.refs_2_ = bf16[4,256,128]{2,1,0:T(8,128)(2,1)S(1)} collective-permute-done((bf16[4,256,128]{2,1,0:T(8,128)(2,1)S(1)}, bf16[4,256,128]{2,1,0:T(8,128)(2,1)S(1)}, u32[]{:S(2)}, u32[]{:S(2)}) %collective-permute-start.30) | collective-permute-done | bytes 262176 | tf_op jit(solution)/shard_map/ppermute | solution.py:259
  92.4 2.4 %collective-permute-start.37 = (bf16[256,128]{1,0:T(8,128)(2,1)S(1)}, bf16[256,128]{1,0:T(8,128)(2,1)S(1)}, u32[]{:S(2)}, u32[]{:S(2)}) collective-permute-start(bf16[256,128]{1,0:T(8,128)(2,1)S(1)} %get-tuple-element.44), channel_id=1, source_target_pairs={{0,32},{32,64},{64,96},{96,0},{1,33},{33,65},{65,97},{97,1},{2,34}... | collective-permute-start | bytes 196616 | tf_op jit(solution)/shard_map/ppermute | solution.py:264
  95.6 2.4 %collective-permute-done.36.refs_1_ = bf16[256,128]{1,0:T(8,128)(2,1)S(1)} collective-permute-done((bf16[256,128]{1,0:T(8,128)(2,1)S(1)}, bf16[256,128]{1,0:T(8,128)(2,1)S(1)}, u32[]{:S(2)}, u32[]{:S(2)}) %collective-permute-start.36) | collective-permute-done | bytes 65568 | tf_op jit(solution)/shard_map/ppermute | solution.py:264
  98.0 1.6 collective-permute-done.37.refs_2_
  99.6 1.9 solve.10
  101.5 1.9 collective-permute-start.41
  103.4 1.6 collective-permute-start.40
  105.0 1.6 collective-permute-start.39
  112.5 4.8 %collective-permute-done.44.refs_3_ = bf16[4,256,128]{2,1,0:T(8,128)(2,1)S(1)} collective-permute-done((bf16[4,256,128]{2,1,0:T(8,128)(2,1)S(1)}, bf16[4,256,128]{2,1,0:T(8,128)(2,1)S(1)}, u32[]{:S(2)}, u32[]{:S(2)}) %collective-permute-start.44) | collective-permute-done | bytes 262176 | tf_op jit(solution)/shard_map/ppermute | solution.py:259
  117.3 2.0 %collective-permute-done.43.refs_2_ = bf16[4,256,128]{2,1,0:T(8,128)(2,1)S(1)} collective-permute-done((bf16[4,256,128]{2,1,0:T(8,128)(2,1)S(1)}, bf16[4,256,128]{2,1,0:T(8,128)(2,1)S(1)}, u32[]{:S(2)}, u32[]{:S(2)}) %collective-permute-start.43) | collective-permute-done | bytes 262176 | tf_op jit(solution)/shard_map/ppermute | solution.py:259
  121.6 1.9 tile_products.9
  123.6 2.4 %collective-permute-start.50 = (bf16[256,128]{1,0:T(8,128)(2,1)S(1)}, bf16[256,128]{1,0:T(8,128)(2,1)S(1)}, u32[]{:S(2)}, u32[]{:S(2)}) collective-permute-start(bf16[256,128]{1,0:T(8,128)(2,1)S(1)} %get-tuple-element.50), channel_id=1, source_target_pairs={{0,32},{32,64},{64,96},{96,0},{1,33},{33,65},{65,97},{97,1},{2,34}... | collective-permute-start | bytes 196616 | tf_op jit(solution)/shard_map/ppermute | solution.py:264
  126.9 3.1 %collective-permute-done.49.refs_1_ = bf16[256,128]{1,0:T(8,128)(2,1)S(1)} collective-permute-done((bf16[256,128]{1,0:T(8,128)(2,1)S(1)}, bf16[256,128]{1,0:T(8,128)(2,1)S(1)}, u32[]{:S(2)}, u32[]{:S(2)}) %collective-permute-start.49) | collective-permute-done | bytes 65568 | tf_op jit(solution)/shard_map/ppermute | solution.py:264
  131.5 2.3 %collective-permute-start.54 = (bf16[256,128]{1,0:T(8,128)(2,1)S(1)}, bf16[256,128]{1,0:T(8,128)(2,1)S(1)}, u32[]{:S(2)}, u32[]{:S(2)}) collective-permute-start(bf16[256,128]{1,0:T(8,128)(2,1)S(1)} %solve.11), channel_id=1, source_target_pairs={{0,4},{1,17},{2,6},{3,19},{4,0},{5,21},{6,2},{7,23},{8,12},{9,25},... | collective-permute-start | bytes 196616 | tf_op jit(solution)/shard_map/ppermute | solution.py:257
  133.8 1.7 collective-permute-start.53
  137.3 2.0 %collective-permute-done.53 = bf16[256,128]{1,0:T(8,128)(2,1)S(1)} collective-permute-done((bf16[256,128]{1,0:T(8,128)(2,1)S(1)}, bf16[256,128]{1,0:T(8,128)(2,1)S(1)}, u32[]{:S(2)}, u32[]{:S(2)}) %collective-permute-start.53) | collective-permute-done | bytes 65568 | tf_op jit(solution)/shard_map/ppermute | solution.py:257
  143.3 4.7 %collective-permute-done.57.refs_3_ = bf16[4,256,128]{2,1,0:T(8,128)(2,1)S(1)} collective-permute-done((bf16[4,256,128]{2,1,0:T(8,128)(2,1)S(1)}, bf16[4,256,128]{2,1,0:T(8,128)(2,1)S(1)}, u32[]{:S(2)}, u32[]{:S(2)}) %collective-permute-start.57) | collective-permute-done | bytes 262176 | tf_op jit(solution)/shard_map/ppermute | solution.py:259
  147.9 1.8 collective-permute-done.56.refs_2_
  152.2 1.9 tile_products.10
  155.4 1.9 collective-permute-start.63
  163.4 2.5 %collective-permute-start.66 = (bf16[256,128]{1,0:T(8,128)(2,1)S(1)}, bf16[256,128]{1,0:T(8,128)(2,1)S(1)}, u32[]{:S(2)}, u32[]{:S(2)}) collective-permute-start(bf16[256,128]{1,0:T(8,128)(2,1)S(1)} %solve.12), channel_id=1, source_target_pairs={{0,2},{1,9},{2,4},{3,11},{4,6},{5,13},{6,0},{7,15},{8,10},{9,17},{... | collective-permute-start | bytes 196616 | tf_op jit(solution)/shard_map/ppermute | solution.py:257
  166.7 1.8 collective-permute-done.67
  171.8 1.8 collective-permute-start.69
  173.8 4.4 %collective-permute-done.70.refs_3_ = bf16[4,256,128]{2,1,0:T(8,128)(2,1)S(1)} collective-permute-done((bf16[4,256,128]{2,1,0:T(8,128)(2,1)S(1)}, bf16[4,256,128]{2,1,0:T(8,128)(2,1)S(1)}, u32[]{:S(2)}, u32[]{:S(2)}) %collective-permute-start.70) | collective-permute-done | bytes 262176 | tf_op jit(solution)/shard_map/ppermute | solution.py:259
  178.2 2.3 %collective-permute-done.69.refs_2_ = bf16[4,256,128]{2,1,0:T(8,128)(2,1)S(1)} collective-permute-done((bf16[4,256,128]{2,1,0:T(8,128)(2,1)S(1)}, bf16[4,256,128]{2,1,0:T(8,128)(2,1)S(1)}, u32[]{:S(2)}, u32[]{:S(2)}) %collective-permute-start.69) | collective-permute-done | bytes 262176 | tf_op jit(solution)/shard_map/ppermute | solution.py:259
  183.5 1.6 collective-permute-start.75
  185.2 2.3 %collective-permute-start.76 = (bf16[256,128]{1,0:T(8,128)(2,1)S(1)}, bf16[256,128]{1,0:T(8,128)(2,1)S(1)}, u32[]{:S(2)}, u32[]{:S(2)}) collective-permute-start(bf16[256,128]{1,0:T(8,128)(2,1)S(1)} %get-tuple-element.60), channel_id=1, source_target_pairs={{0,32},{32,64},{64,96},{96,0},{1,33},{33,65},{65,97},{97,1},{2,34}... | collective-permute-start | bytes 196616 | tf_op jit(solution)/shard_map/ppermute | solution.py:264
  191.7 1.7 solve.13
  (145 shorter events, 72.7 us)
Async XLA Ops:
  2.6 9.1 %collective-permute-start.2 = (bf16[256,128]{1,0:T(8,128)(2,1)}, bf16[256,128]{1,0:T(8,128)(2,1)S(1)}, u32[]{:S(2)}, u32[]{:S(2)}) collective-permute-start(bf16[256,128]{1,0:T(8,128)(2,1)} %solve.7.refs_0_), channel_id=1, source_target_pairs={{0,4},{1,17},{2,6},{3,19},{4,0},{5,21},{6,2},{7,23},{8,12},{9,25},... | collective-permute-start | bytes 196616 | tf_op jit(solution)/shard_map/ppermute | solution.py:257
  6.0 5.8 %collective-permute-start.1 = (bf16[256,128]{1,0:T(8,128)(2,1)}, bf16[256,128]{1,0:T(8,128)(2,1)S(1)}, u32[]{:S(2)}, u32[]{:S(2)}) collective-permute-start(bf16[256,128]{1,0:T(8,128)(2,1)} %solve.7.refs_0_), channel_id=1, source_target_pairs={{0,2},{1,9},{2,4},{3,11},{4,6},{5,13},{6,0},{7,15},{8,10},{9,17},{... | collective-permute-start | bytes 196616 | tf_op jit(solution)/shard_map/ppermute | solution.py:257
  12.9 8.0 %collective-permute-start.5 = (bf16[4,256,128]{2,1,0:T(8,128)(2,1)S(1)}, bf16[4,256,128]{2,1,0:T(8,128)(2,1)S(1)}, u32[]{:S(2)}, u32[]{:S(2)}) collective-permute-start(bf16[4,256,128]{2,1,0:T(8,128)(2,1)S(1)} %stack_after.1.refs_0_), channel_id=1, source_target_pairs={{0,16},{1,5},{2,18},{3,7},{4,20},{5,1},{6,22},{7,3},{8,24},{9,13},... | collective-permute-start | bytes 786440 | tf_op jit(solution)/shard_map/ppermute | solution.py:259
  16.1 7.8 %collective-permute-start.4 = (bf16[4,256,128]{2,1,0:T(8,128)(2,1)S(1)}, bf16[4,256,128]{2,1,0:T(8,128)(2,1)S(1)}, u32[]{:S(2)}, u32[]{:S(2)}) collective-permute-start(bf16[4,256,128]{2,1,0:T(8,128)(2,1)S(1)} %stack_after.1.refs_0_), channel_id=1, source_target_pairs={{0,24},{1,7},{2,26},{3,1},{4,28},{5,3},{6,30},{7,5},{8,0},{9,15},{... | collective-permute-start | bytes 786440 | tf_op jit(solution)/shard_map/ppermute | solution.py:259
  17.2 7.6 %collective-permute-start.3 = (bf16[4,256,128]{2,1,0:T(8,128)(2,1)S(1)}, bf16[4,256,128]{2,1,0:T(8,128)(2,1)S(1)}, u32[]{:S(2)}, u32[]{:S(2)}) collective-permute-start(bf16[4,256,128]{2,1,0:T(8,128)(2,1)S(1)} %stack_after.1.refs_0_), channel_id=1, source_target_pairs={{0,8},{1,3},{2,10},{3,5},{4,12},{5,7},{6,14},{7,1},{8,16},{9,11},{... | collective-permute-start | bytes 786440 | tf_op jit(solution)/shard_map/ppermute | solution.py:259
  18.1 6.7 %collective-permute-start.6 = (bf16[4,256,128]{2,1,0:T(8,128)(2,1)S(1)}, bf16[4,256,128]{2,1,0:T(8,128)(2,1)S(1)}, u32[]{:S(2)}, u32[]{:S(2)}) collective-permute-start(bf16[4,256,128]{2,1,0:T(8,128)(2,1)S(1)} %stack_after.1.refs_0_), channel_id=1, source_target_pairs={{0,1},{1,0},{2,3},{3,2},{4,5},{5,4},{6,7},{7,6},{8,9},{9,8},{10,11... | collective-permute-start | bytes 786440 | tf_op jit(solution)/shard_map/ppermute | solution.py:260
  28.9 6.5 %collective-permute-start.10 = (bf16[256,128]{1,0:T(8,128)(2,1)S(1)}, bf16[256,128]{1,0:T(8,128)(2,1)S(1)}, u32[]{:S(2)}, u32[]{:S(2)}) collective-permute-start(bf16[256,128]{1,0:T(8,128)(2,1)S(1)} %get-tuple-element.33), channel_id=1, source_target_pairs={{0,64},{32,96},{64,0},{96,32},{1,65},{33,97},{65,1},{97,33},{2,66}... | collective-permute-start | bytes 196616 | tf_op jit(solution)/shard_map/ppermute | solution.py:264
  31.8 6.0 %collective-permute-start.11 = (bf16[256,128]{1,0:T(8,128)(2,1)S(1)}, bf16[256,128]{1,0:T(8,128)(2,1)S(1)}, u32[]{:S(2)}, u32[]{:S(2)}) collective-permute-start(bf16[256,128]{1,0:T(8,128)(2,1)S(1)} %get-tuple-element.34), channel_id=1, source_target_pairs={{0,32},{32,64},{64,96},{96,0},{1,33},{33,65},{65,97},{97,1},{2,34}... | collective-permute-start | bytes 196616 | tf_op jit(solution)/shard_map/ppermute | solution.py:264
  38.9 5.8 %collective-permute-start.15 = (bf16[256,128]{1,0:T(8,128)(2,1)S(1)}, bf16[256,128]{1,0:T(8,128)(2,1)S(1)}, u32[]{:S(2)}, u32[]{:S(2)}) collective-permute-start(bf16[256,128]{1,0:T(8,128)(2,1)S(1)} %solve.8), channel_id=1, source_target_pairs={{0,4},{1,17},{2,6},{3,19},{4,0},{5,21},{6,2},{7,23},{8,12},{9,25},... | collective-permute-start | bytes 196616 | tf_op jit(solution)/shard_map/ppermute | solution.py:257
  40.2 5.7 %collective-permute-start.14 = (bf16[256,128]{1,0:T(8,128)(2,1)S(1)}, bf16[256,128]{1,0:T(8,128)(2,1)S(1)}, u32[]{:S(2)}, u32[]{:S(2)}) collective-permute-start(bf16[256,128]{1,0:T(8,128)(2,1)S(1)} %solve.8), channel_id=1, source_target_pairs={{0,2},{1,9},{2,4},{3,11},{4,6},{5,13},{6,0},{7,15},{8,10},{9,17},{... | collective-permute-start | bytes 196616 | tf_op jit(solution)/shard_map/ppermute | solution.py:257
  48.4 8.0 %collective-permute-start.18 = (bf16[4,256,128]{2,1,0:T(8,128)(2,1)S(1)}, bf16[4,256,128]{2,1,0:T(8,128)(2,1)S(1)}, u32[]{:S(2)}, u32[]{:S(2)}) collective-permute-start(bf16[4,256,128]{2,1,0:T(8,128)(2,1)S(1)} %pad_maximum_fusion.refs_0_), channel_id=1, source_target_pairs={{0,16},{1,5},{2,18},{3,7},{4,20},{5,1},{6,22},{7,3},{8,24},{9,13},... | collective-permute-start | bytes 786440 | tf_op jit(solution)/shard_map/ppermute | solution.py:259
  49.8 8.7 %collective-permute-start.17 = (bf16[4,256,128]{2,1,0:T(8,128)(2,1)S(1)}, bf16[4,256,128]{2,1,0:T(8,128)(2,1)S(1)}, u32[]{:S(2)}, u32[]{:S(2)}) collective-permute-start(bf16[4,256,128]{2,1,0:T(8,128)(2,1)S(1)} %pad_maximum_fusion.refs_0_), channel_id=1, source_target_pairs={{0,24},{1,7},{2,26},{3,1},{4,28},{5,3},{6,30},{7,5},{8,0},{9,15},{... | collective-permute-start | bytes 786440 | tf_op jit(solution)/shard_map/ppermute | solution.py:259
  51.0 8.2 %collective-permute-start.16 = (bf16[4,256,128]{2,1,0:T(8,128)(2,1)S(1)}, bf16[4,256,128]{2,1,0:T(8,128)(2,1)S(1)}, u32[]{:S(2)}, u32[]{:S(2)}) collective-permute-start(bf16[4,256,128]{2,1,0:T(8,128)(2,1)S(1)} %pad_maximum_fusion.refs_0_), channel_id=1, source_target_pairs={{0,8},{1,3},{2,10},{3,5},{4,12},{5,7},{6,14},{7,1},{8,16},{9,11},{... | collective-permute-start | bytes 786440 | tf_op jit(solution)/shard_map/ppermute | solution.py:259
  51.9 7.3 %collective-permute-start.19 = (bf16[4,256,128]{2,1,0:T(8,128)(2,1)S(1)}, bf16[4,256,128]{2,1,0:T(8,128)(2,1)S(1)}, u32[]{:S(2)}, u32[]{:S(2)}) collective-permute-start(bf16[4,256,128]{2,1,0:T(8,128)(2,1)S(1)} %pad_maximum_fusion.refs_0_), channel_id=1, source_target_pairs={{0,1},{1,0},{2,3},{3,2},{4,5},{5,4},{6,7},{7,6},{8,9},{9,8},{10,11... | collective-permute-start | bytes 786440 | tf_op jit(solution)/shard_map/ppermute | solution.py:260
  62.6 6.3 %collective-permute-start.23 = (bf16[256,128]{1,0:T(8,128)(2,1)S(1)}, bf16[256,128]{1,0:T(8,128)(2,1)S(1)}, u32[]{:S(2)}, u32[]{:S(2)}) collective-permute-start(bf16[256,128]{1,0:T(8,128)(2,1)S(1)} %get-tuple-element.38), channel_id=1, source_target_pairs={{0,64},{32,96},{64,0},{96,32},{1,65},{33,97},{65,1},{97,33},{2,66}... | collective-permute-start | bytes 196616 | tf_op jit(solution)/shard_map/ppermute | solution.py:264
  63.1 6.8 %collective-permute-start.24 = (bf16[256,128]{1,0:T(8,128)(2,1)S(1)}, bf16[256,128]{1,0:T(8,128)(2,1)S(1)}, u32[]{:S(2)}, u32[]{:S(2)}) collective-permute-start(bf16[256,128]{1,0:T(8,128)(2,1)S(1)} %get-tuple-element.39), channel_id=1, source_target_pairs={{0,32},{32,64},{64,96},{96,0},{1,33},{33,65},{65,97},{97,1},{2,34}... | collective-permute-start | bytes 196616 | tf_op jit(solution)/shard_map/ppermute | solution.py:264
  71.2 5.9 %collective-permute-start.28 = (bf16[256,128]{1,0:T(8,128)(2,1)S(1)}, bf16[256,128]{1,0:T(8,128)(2,1)S(1)}, u32[]{:S(2)}, u32[]{:S(2)}) collective-permute-start(bf16[256,128]{1,0:T(8,128)(2,1)S(1)} %solve.9), channel_id=1, source_target_pairs={{0,4},{1,17},{2,6},{3,19},{4,0},{5,21},{6,2},{7,23},{8,12},{9,25},... | collective-permute-start | bytes 196616 | tf_op jit(solution)/shard_map/ppermute | solution.py:257
  71.6 6.2 %collective-permute-start.27 = (bf16[256,128]{1,0:T(8,128)(2,1)S(1)}, bf16[256,128]{1,0:T(8,128)(2,1)S(1)}, u32[]{:S(2)}, u32[]{:S(2)}) collective-permute-start(bf16[256,128]{1,0:T(8,128)(2,1)S(1)} %solve.9), channel_id=1, source_target_pairs={{0,2},{1,9},{2,4},{3,11},{4,6},{5,13},{6,0},{7,15},{8,10},{9,17},{... | collective-permute-start | bytes 196616 | tf_op jit(solution)/shard_map/ppermute | solution.py:257
  78.5 8.0 %collective-permute-start.31 = (bf16[4,256,128]{2,1,0:T(8,128)(2,1)S(1)}, bf16[4,256,128]{2,1,0:T(8,128)(2,1)S(1)}, u32[]{:S(2)}, u32[]{:S(2)}) collective-permute-start(bf16[4,256,128]{2,1,0:T(8,128)(2,1)S(1)} %pad_maximum_fusion.1.refs_0_), channel_id=1, source_target_pairs={{0,16},{1,5},{2,18},{3,7},{4,20},{5,1},{6,22},{7,3},{8,24},{9,13},... | collective-permute-start | bytes 786440 | tf_op jit(solution)/shard_map/ppermute | solution.py:259
  80.0 8.6 %collective-permute-start.30 = (bf16[4,256,128]{2,1,0:T(8,128)(2,1)S(1)}, bf16[4,256,128]{2,1,0:T(8,128)(2,1)S(1)}, u32[]{:S(2)}, u32[]{:S(2)}) collective-permute-start(bf16[4,256,128]{2,1,0:T(8,128)(2,1)S(1)} %pad_maximum_fusion.1.refs_0_), channel_id=1, source_target_pairs={{0,24},{1,7},{2,26},{3,1},{4,28},{5,3},{6,30},{7,5},{8,0},{9,15},{... | collective-permute-start | bytes 786440 | tf_op jit(solution)/shard_map/ppermute | solution.py:259
  81.1 8.1 %collective-permute-start.29 = (bf16[4,256,128]{2,1,0:T(8,128)(2,1)S(1)}, bf16[4,256,128]{2,1,0:T(8,128)(2,1)S(1)}, u32[]{:S(2)}, u32[]{:S(2)}) collective-permute-start(bf16[4,256,128]{2,1,0:T(8,128)(2,1)S(1)} %pad_maximum_fusion.1.refs_0_), channel_id=1, source_target_pairs={{0,8},{1,3},{2,10},{3,5},{4,12},{5,7},{6,14},{7,1},{8,16},{9,11},{... | collective-permute-start | bytes 786440 | tf_op jit(solution)/shard_map/ppermute | solution.py:259
  82.0 7.3 %collective-permute-start.32 = (bf16[4,256,128]{2,1,0:T(8,128)(2,1)S(1)}, bf16[4,256,128]{2,1,0:T(8,128)(2,1)S(1)}, u32[]{:S(2)}, u32[]{:S(2)}) collective-permute-start(bf16[4,256,128]{2,1,0:T(8,128)(2,1)S(1)} %pad_maximum_fusion.1.refs_0_), channel_id=1, source_target_pairs={{0,1},{1,0},{2,3},{3,2},{4,5},{5,4},{6,7},{7,6},{8,9},{9,8},{10,11... | collective-permute-start | bytes 786440 | tf_op jit(solution)/shard_map/ppermute | solution.py:260
  91.6 6.4 %collective-permute-start.36 = (bf16[256,128]{1,0:T(8,128)(2,1)S(1)}, bf16[256,128]{1,0:T(8,128)(2,1)S(1)}, u32[]{:S(2)}, u32[]{:S(2)}) collective-permute-start(bf16[256,128]{1,0:T(8,128)(2,1)S(1)} %get-tuple-element.43), channel_id=1, source_target_pairs={{0,64},{32,96},{64,0},{96,32},{1,65},{33,97},{65,1},{97,33},{2,66}... | collective-permute-start | bytes 196616 | tf_op jit(solution)/shard_map/ppermute | solution.py:264
  92.4 7.2 %collective-permute-start.37 = (bf16[256,128]{1,0:T(8,128)(2,1)S(1)}, bf16[256,128]{1,0:T(8,128)(2,1)S(1)}, u32[]{:S(2)}, u32[]{:S(2)}) collective-permute-start(bf16[256,128]{1,0:T(8,128)(2,1)S(1)} %get-tuple-element.44), channel_id=1, source_target_pairs={{0,32},{32,64},{64,96},{96,0},{1,33},{33,65},{65,97},{97,1},{2,34}... | collective-permute-start | bytes 196616 | tf_op jit(solution)/shard_map/ppermute | solution.py:264
  101.5 5.8 %collective-permute-start.41 = (bf16[256,128]{1,0:T(8,128)(2,1)S(1)}, bf16[256,128]{1,0:T(8,128)(2,1)S(1)}, u32[]{:S(2)}, u32[]{:S(2)}) collective-permute-start(bf16[256,128]{1,0:T(8,128)(2,1)S(1)} %get-tuple-element.47), channel_id=1, source_target_pairs={{0,4},{1,17},{2,6},{3,19},{4,0},{5,21},{6,2},{7,23},{8,12},{9,25},... | collective-permute-start | bytes 196616 | tf_op jit(solution)/shard_map/ppermute | solution.py:257
  103.4 5.5 %collective-permute-start.40 = (bf16[256,128]{1,0:T(8,128)(2,1)S(1)}, bf16[256,128]{1,0:T(8,128)(2,1)S(1)}, u32[]{:S(2)}, u32[]{:S(2)}) collective-permute-start(bf16[256,128]{1,0:T(8,128)(2,1)S(1)} %get-tuple-element.47), channel_id=1, source_target_pairs={{0,2},{1,9},{2,4},{3,11},{4,6},{5,13},{6,0},{7,15},{8,10},{9,17},{... | collective-permute-start | bytes 196616 | tf_op jit(solution)/shard_map/ppermute | solution.py:257
  109.3 8.0 %collective-permute-start.44 = (bf16[4,256,128]{2,1,0:T(8,128)(2,1)S(1)}, bf16[4,256,128]{2,1,0:T(8,128)(2,1)S(1)}, u32[]{:S(2)}, u32[]{:S(2)}) collective-permute-start(bf16[4,256,128]{2,1,0:T(8,128)(2,1)S(1)} %pad_maximum_fusion.2.refs_0_), channel_id=1, source_target_pairs={{0,16},{1,5},{2,18},{3,7},{4,20},{5,1},{6,22},{7,3},{8,24},{9,13},... | collective-permute-start | bytes 786440 | tf_op jit(solution)/shard_map/ppermute | solution.py:259
  110.5 8.9 %collective-permute-start.43 = (bf16[4,256,128]{2,1,0:T(8,128)(2,1)S(1)}, bf16[4,256,128]{2,1,0:T(8,128)(2,1)S(1)}, u32[]{:S(2)}, u32[]{:S(2)}) collective-permute-start(bf16[4,256,128]{2,1,0:T(8,128)(2,1)S(1)} %pad_maximum_fusion.2.refs_0_), channel_id=1, source_target_pairs={{0,24},{1,7},{2,26},{3,1},{4,28},{5,3},{6,30},{7,5},{8,0},{9,15},{... | collective-permute-start | bytes 786440 | tf_op jit(solution)/shard_map/ppermute | solution.py:259
  111.7 8.4 %collective-permute-start.42 = (bf16[4,256,128]{2,1,0:T(8,128)(2,1)S(1)}, bf16[4,256,128]{2,1,0:T(8,128)(2,1)S(1)}, u32[]{:S(2)}, u32[]{:S(2)}) collective-permute-start(bf16[4,256,128]{2,1,0:T(8,128)(2,1)S(1)} %pad_maximum_fusion.2.refs_0_), channel_id=1, source_target_pairs={{0,8},{1,3},{2,10},{3,5},{4,12},{5,7},{6,14},{7,1},{8,16},{9,11},{... | collective-permute-start | bytes 786440 | tf_op jit(solution)/shard_map/ppermute | solution.py:259
  112.5 7.5 %collective-permute-start.45 = (bf16[4,256,128]{2,1,0:T(8,128)(2,1)S(1)}, bf16[4,256,128]{2,1,0:T(8,128)(2,1)S(1)}, u32[]{:S(2)}, u32[]{:S(2)}) collective-permute-start(bf16[4,256,128]{2,1,0:T(8,128)(2,1)S(1)} %pad_maximum_fusion.2.refs_0_), channel_id=1, source_target_pairs={{0,1},{1,0},{2,3},{3,2},{4,5},{5,4},{6,7},{7,6},{8,9},{9,8},{10,11... | collective-permute-start | bytes 786440 | tf_op jit(solution)/shard_map/ppermute | solution.py:260
  123.5 6.5 %collective-permute-start.49 = (bf16[256,128]{1,0:T(8,128)(2,1)S(1)}, bf16[256,128]{1,0:T(8,128)(2,1)S(1)}, u32[]{:S(2)}, u32[]{:S(2)}) collective-permute-start(bf16[256,128]{1,0:T(8,128)(2,1)S(1)} %get-tuple-element.49), channel_id=1, source_target_pairs={{0,64},{32,96},{64,0},{96,32},{1,65},{33,97},{65,1},{97,33},{2,66}... | collective-permute-start | bytes 196616 | tf_op jit(solution)/shard_map/ppermute | solution.py:264
  123.6 6.8 %collective-permute-start.50 = (bf16[256,128]{1,0:T(8,128)(2,1)S(1)}, bf16[256,128]{1,0:T(8,128)(2,1)S(1)}, u32[]{:S(2)}, u32[]{:S(2)}) collective-permute-start(bf16[256,128]{1,0:T(8,128)(2,1)S(1)} %get-tuple-element.50), channel_id=1, source_target_pairs={{0,32},{32,64},{64,96},{96,0},{1,33},{33,65},{65,97},{97,1},{2,34}... | collective-permute-start | bytes 196616 | tf_op jit(solution)/shard_map/ppermute | solution.py:264
  131.5 5.8 %collective-permute-start.54 = (bf16[256,128]{1,0:T(8,128)(2,1)S(1)}, bf16[256,128]{1,0:T(8,128)(2,1)S(1)}, u32[]{:S(2)}, u32[]{:S(2)}) collective-permute-start(bf16[256,128]{1,0:T(8,128)(2,1)S(1)} %solve.11), channel_id=1, source_target_pairs={{0,4},{1,17},{2,6},{3,19},{4,0},{5,21},{6,2},{7,23},{8,12},{9,25},... | collective-permute-start | bytes 196616 | tf_op jit(solution)/shard_map/ppermute | solution.py:257
  133.8 5.5 %collective-permute-start.53 = (bf16[256,128]{1,0:T(8,128)(2,1)S(1)}, bf16[256,128]{1,0:T(8,128)(2,1)S(1)}, u32[]{:S(2)}, u32[]{:S(2)}) collective-permute-start(bf16[256,128]{1,0:T(8,128)(2,1)S(1)} %solve.11), channel_id=1, source_target_pairs={{0,2},{1,9},{2,4},{3,11},{4,6},{5,13},{6,0},{7,15},{8,10},{9,17},{... | collective-permute-start | bytes 196616 | tf_op jit(solution)/shard_map/ppermute | solution.py:257
  139.9 8.0 %collective-permute-start.57 = (bf16[4,256,128]{2,1,0:T(8,128)(2,1)S(1)}, bf16[4,256,128]{2,1,0:T(8,128)(2,1)S(1)}, u32[]{:S(2)}, u32[]{:S(2)}) collective-permute-start(bf16[4,256,128]{2,1,0:T(8,128)(2,1)S(1)} %pad_maximum_fusion.3.refs_0_), channel_id=1, source_target_pairs={{0,16},{1,5},{2,18},{3,7},{4,20},{5,1},{6,22},{7,3},{8,24},{9,13},... | collective-permute-start | bytes 786440 | tf_op jit(solution)/shard_map/ppermute | solution.py:259
  141.2 8.5 %collective-permute-start.56 = (bf16[4,256,128]{2,1,0:T(8,128)(2,1)S(1)}, bf16[4,256,128]{2,1,0:T(8,128)(2,1)S(1)}, u32[]{:S(2)}, u32[]{:S(2)}) collective-permute-start(bf16[4,256,128]{2,1,0:T(8,128)(2,1)S(1)} %pad_maximum_fusion.3.refs_0_), channel_id=1, source_target_pairs={{0,24},{1,7},{2,26},{3,1},{4,28},{5,3},{6,30},{7,5},{8,0},{9,15},{... | collective-permute-start | bytes 786440 | tf_op jit(solution)/shard_map/ppermute | solution.py:259
  142.2 8.4 %collective-permute-start.55 = (bf16[4,256,128]{2,1,0:T(8,128)(2,1)S(1)}, bf16[4,256,128]{2,1,0:T(8,128)(2,1)S(1)}, u32[]{:S(2)}, u32[]{:S(2)}) collective-permute-start(bf16[4,256,128]{2,1,0:T(8,128)(2,1)S(1)} %pad_maximum_fusion.3.refs_0_), channel_id=1, source_target_pairs={{0,8},{1,3},{2,10},{3,5},{4,12},{5,7},{6,14},{7,1},{8,16},{9,11},{... | collective-permute-start | bytes 786440 | tf_op jit(solution)/shard_map/ppermute | solution.py:259
  143.3 7.4 %collective-permute-start.58 = (bf16[4,256,128]{2,1,0:T(8,128)(2,1)S(1)}, bf16[4,256,128]{2,1,0:T(8,128)(2,1)S(1)}, u32[]{:S(2)}, u32[]{:S(2)}) collective-permute-start(bf16[4,256,128]{2,1,0:T(8,128)(2,1)S(1)} %pad_maximum_fusion.3.refs_0_), channel_id=1, source_target_pairs={{0,1},{1,0},{2,3},{3,2},{4,5},{5,4},{6,7},{7,6},{8,9},{9,8},{10,11... | collective-permute-start | bytes 786440 | tf_op jit(solution)/shard_map/ppermute | solution.py:260
  154.1 5.9 %collective-permute-start.62 = (bf16[256,128]{1,0:T(8,128)(2,1)S(1)}, bf16[256,128]{1,0:T(8,128)(2,1)S(1)}, u32[]{:S(2)}, u32[]{:S(2)}) collective-permute-start(bf16[256,128]{1,0:T(8,128)(2,1)S(1)} %get-tuple-element.54), channel_id=1, source_target_pairs={{0,64},{32,96},{64,0},{96,32},{1,65},{33,97},{65,1},{97,33},{2,66}... | collective-permute-start | bytes 196616 | tf_op jit(solution)/shard_map/ppermute | solution.py:264
  155.4 6.1 %collective-permute-start.63 = (bf16[256,128]{1,0:T(8,128)(2,1)S(1)}, bf16[256,128]{1,0:T(8,128)(2,1)S(1)}, u32[]{:S(2)}, u32[]{:S(2)}) collective-permute-start(bf16[256,128]{1,0:T(8,128)(2,1)S(1)} %get-tuple-element.55), channel_id=1, source_target_pairs={{0,32},{32,64},{64,96},{96,0},{1,33},{33,65},{65,97},{97,1},{2,34}... | collective-permute-start | bytes 196616 | tf_op jit(solution)/shard_map/ppermute | solution.py:264
  162.6 5.9 %collective-permute-start.67 = (bf16[256,128]{1,0:T(8,128)(2,1)S(1)}, bf16[256,128]{1,0:T(8,128)(2,1)S(1)}, u32[]{:S(2)}, u32[]{:S(2)}) collective-permute-start(bf16[256,128]{1,0:T(8,128)(2,1)S(1)} %solve.12), channel_id=1, source_target_pairs={{0,4},{1,17},{2,6},{3,19},{4,0},{5,21},{6,2},{7,23},{8,12},{9,25},... | collective-permute-start | bytes 196616 | tf_op jit(solution)/shard_map/ppermute | solution.py:257
  163.4 5.7 %collective-permute-start.66 = (bf16[256,128]{1,0:T(8,128)(2,1)S(1)}, bf16[256,128]{1,0:T(8,128)(2,1)S(1)}, u32[]{:S(2)}, u32[]{:S(2)}) collective-permute-start(bf16[256,128]{1,0:T(8,128)(2,1)S(1)} %solve.12), channel_id=1, source_target_pairs={{0,2},{1,9},{2,4},{3,11},{4,6},{5,13},{6,0},{7,15},{8,10},{9,17},{... | collective-permute-start | bytes 196616 | tf_op jit(solution)/shard_map/ppermute | solution.py:257
  170.2 8.0 %collective-permute-start.70 = (bf16[4,256,128]{2,1,0:T(8,128)(2,1)S(1)}, bf16[4,256,128]{2,1,0:T(8,128)(2,1)S(1)}, u32[]{:S(2)}, u32[]{:S(2)}) collective-permute-start(bf16[4,256,128]{2,1,0:T(8,128)(2,1)S(1)} %pad_maximum_fusion.4.refs_0_), channel_id=1, source_target_pairs={{0,16},{1,5},{2,18},{3,7},{4,20},{5,1},{6,22},{7,3},{8,24},{9,13},... | collective-permute-start | bytes 786440 | tf_op jit(solution)/shard_map/ppermute | solution.py:259
  171.8 8.8 %collective-permute-start.69 = (bf16[4,256,128]{2,1,0:T(8,128)(2,1)S(1)}, bf16[4,256,128]{2,1,0:T(8,128)(2,1)S(1)}, u32[]{:S(2)}, u32[]{:S(2)}) collective-permute-start(bf16[4,256,128]{2,1,0:T(8,128)(2,1)S(1)} %pad_maximum_fusion.4.refs_0_), channel_id=1, source_target_pairs={{0,24},{1,7},{2,26},{3,1},{4,28},{5,3},{6,30},{7,5},{8,0},{9,15},{... | collective-permute-start | bytes 786440 | tf_op jit(solution)/shard_map/ppermute | solution.py:259
  173.6 7.6 %collective-permute-start.68 = (bf16[4,256,128]{2,1,0:T(8,128)(2,1)S(1)}, bf16[4,256,128]{2,1,0:T(8,128)(2,1)S(1)}, u32[]{:S(2)}, u32[]{:S(2)}) collective-permute-start(bf16[4,256,128]{2,1,0:T(8,128)(2,1)S(1)} %pad_maximum_fusion.4.refs_0_), channel_id=1, source_target_pairs={{0,8},{1,3},{2,10},{3,5},{4,12},{5,7},{6,14},{7,1},{8,16},{9,11},{... | collective-permute-start | bytes 786440 | tf_op jit(solution)/shard_map/ppermute | solution.py:259
  173.8 7.4 %collective-permute-start.71 = (bf16[4,256,128]{2,1,0:T(8,128)(2,1)S(1)}, bf16[4,256,128]{2,1,0:T(8,128)(2,1)S(1)}, u32[]{:S(2)}, u32[]{:S(2)}) collective-permute-start(bf16[4,256,128]{2,1,0:T(8,128)(2,1)S(1)} %pad_maximum_fusion.4.refs_0_), channel_id=1, source_target_pairs={{0,1},{1,0},{2,3},{3,2},{4,5},{5,4},{6,7},{7,6},{8,9},{9,8},{10,11... | collective-permute-start | bytes 786440 | tf_op jit(solution)/shard_map/ppermute | solution.py:260
  183.5 5.9 %collective-permute-start.75 = (bf16[256,128]{1,0:T(8,128)(2,1)S(1)}, bf16[256,128]{1,0:T(8,128)(2,1)S(1)}, u32[]{:S(2)}, u32[]{:S(2)}) collective-permute-start(bf16[256,128]{1,0:T(8,128)(2,1)S(1)} %get-tuple-element.59), channel_id=1, source_target_pairs={{0,64},{32,96},{64,0},{96,32},{1,65},{33,97},{65,1},{97,33},{2,66}... | collective-permute-start | bytes 196616 | tf_op jit(solution)/shard_map/ppermute | solution.py:264
  185.2 5.6 %collective-permute-start.76 = (bf16[256,128]{1,0:T(8,128)(2,1)S(1)}, bf16[256,128]{1,0:T(8,128)(2,1)S(1)}, u32[]{:S(2)}, u32[]{:S(2)}) collective-permute-start(bf16[256,128]{1,0:T(8,128)(2,1)S(1)} %get-tuple-element.60), channel_id=1, source_target_pairs={{0,32},{32,64},{64,96},{96,0},{1,33},{33,65},{65,97},{97,1},{2,34}... | collective-permute-start | bytes 196616 | tf_op jit(solution)/shard_map/ppermute | solution.py:264
  (38 other events, 256.5 us)

commit v4 on v3

--- a/solution.py
+++ b/solution.py
@@ -10,9 +10,9 @@
 B = 256
 R = 128
 SLOTS = 8
-NEAR = (0, 3, 1, 2)
-FAR = (0, 1, 3, 2)
-ACROSS = (0, 2, 1, 3)
+NEAR = ((0, 3, 1, 2), (0, 1, 2, 3))
+FAR = ((0, 1, 3, 2), (0, 1, 3, 2))
+ACROSS = ((0, 2, 1, 3), (0, 2, 1, 3))
 ANY = pl.BlockSpec(memory_space=pl.ANY)
 SMEM = pl.BlockSpec(memory_space=pltpu.SMEM)
 VMEM = pl.BlockSpec(memory_space=pltpu.VMEM)
@@ -20,20 +20,25 @@
 LIMIT = 50 * 2**20
 
 
-def near_pairs(k):
-    return [(i, shifted(i, k, 1 if i & 1 == 0 else 3)) for i in range(32)]
-
-
-def far_pairs(k):
-    return [(i, shifted(i, k, 3 if i & 1 == 0 else 1)) for i in range(32)]
+def near_pairs(n):
+    return [(i, shifted(i, NEAR[i & 1][n], 1 if i & 1 == 0 else 3)) for i in range(32)]
+
+
+def far_pairs(n):
+    return [(i, shifted(i, FAR[i & 1][n], 3 if i & 1 == 0 else 1)) for i in range(32)]
 
 
 def shifted(i, k, bit):
     return (i & ~(3 << bit)) | ((((i >> bit) + k) & 3) << bit)
 
 
-def z_pairs(k):
-    return [(i, (i + k) & 3) for i in range(4)]
+def across_pairs(n):
+    return [(i, (i + 32 * ACROSS[i & 1][n]) & 127) for i in range(128)]
+
+
+def order_at(order, odd, shift):
+    places = [sum(jnp.where(shift == k, n, 0) for n, k in enumerate(one)) for one in order]
+    return jnp.where(odd, places[1], places[0])
 
 
 CORE_PAIRS = [(i, i ^ 1) for i in range(32)]
@@ -96,15 +101,15 @@
     y_back = ((pcol_at >> 1) - (col >> 1)) & 3
     far = jnp.where((col & 1) == 0, x_back, y_back)
     near = jnp.where((col & 1) == 0, y_back, x_back)
-    near_slot = sum(jnp.where(near == shift, n, 0) for n, shift in enumerate(NEAR))
-    return (col ^ pcol_at) & 1, far, near_slot
+    odd = (col & 1) == 1
+    return (col ^ pcol_at) & 1, order_at(FAR, odd, far), order_at(NEAR, odd, near)
 
 
 def start_panel(pieces, pcol_at, col, buffer, sem):
     other, far, near_slot = panel_place(pcol_at, col)
     for e in range(2):
         for k in range(4):
-            @pl.when((other == e) & (far == FAR[k]))
+            @pl.when((other == e) & (far == k))
             def _():
                 pltpu.make_async_copy(pieces[e * 4 + k].at[near_slot], buffer, sem).start()
 
@@ -158,7 +163,7 @@
         after[...] = acc[...]
     outs[0][...] = acc[prow_at]
     for k in range(1, 4):
-        outs[k][...] = acc[(prow_at + ACROSS[k]) & 3].astype(jnp.bfloat16)
+        outs[k][...] = acc[(prow_at + jnp.where((pcol_at & 1) == 0, ACROSS[0][k], ACROSS[1][k])) & 3].astype(jnp.bfloat16)
 
 
 def tile_products(step, plan, scales, place, pieces, tiles, before):
@@ -229,7 +234,7 @@
         in_specs=[ANY] * (2 + len(sums)),
         out_specs=[VMEM] * len(out_shape),
         scratch_shapes=buffers + [pltpu.VMEM((len(uses), B, B), jnp.bfloat16), pltpu.SemaphoreType.DMA((7,))],
-        compiler_params=pltpu.CompilerParams(vmem_limit_bytes=LIMIT if sums else 60 * 2**20),
+        compiler_params=pltpu.CompilerParams(vmem_limit_bytes=LIMIT),
         cost_estimate=pl.CostEstimate(flops=4 * B * B * R, bytes_accessed=B * R * 20, transcendentals=0),
         name="solve",
     )(target, inverses, *sums)
@@ -254,14 +259,14 @@
 
 
 def gather_panels(panel, plan=None):
-    near = [panel] + [lax.ppermute(panel, "pcol", near_pairs(k)) for k in NEAR[1:]]
+    near = [panel] + [lax.ppermute(panel, "pcol", near_pairs(n)) for n in (1, 2, 3)]
     near = jnp.stack(near) if plan is None else stack_after(plan, near)
-    far = [near] + [lax.ppermute(near, "pcol", far_pairs(k)) for k in FAR[1:]]
+    far = [near] + [lax.ppermute(near, "pcol", far_pairs(n)) for n in (1, 2, 3)]
     return far + [lax.ppermute(piece, "pcol", CORE_PAIRS) for piece in far]
 
 
 def across_rows(values):
-    return [lax.ppermute(value, "prow", z_pairs(k)) for value, k in zip(values, ACROSS[1:])]
+    return [lax.ppermute(value, ("prow", "pcol"), across_pairs(n + 1)) for n, value in enumerate(values)]
 
 
 def shards(right_side, factor_tiles, tile_scales, tile_pattern, parent, inverses):

time: 195 us -> 195 us (level)
  starting transfers between devices: 79 us -> 85.5 us
  Pallas kernels: 20.5 us -> 16.3 us
  waiting for transfers between devices: 89.8 us -> 87.5 us
    ppermute x54, starting transfers between devices: 79 us -> 85.2 us  [the longest x18 31.5 us: across_rows(): lax.ppermute(value, ('prow', 'pcol'), across_pairs(n + 1))]
    pallas_call x6, Pallas kernels: 9.31 us -> 6.32 us  [tile_products(): pl.pallas_call(functools.partial(tile_kernel, step), out_shape=out_shape,...]
    ppermute x54, waiting for transfers between devices: 80.6 us -> 78.4 us  [the longest x18 43.3 us: gather_panels(): far = [near] + [lax.ppermute(near, 'pcol', far_pairs(n)) for n in (1, 2, 3)]]
  transfers between devices with their start and end apart: 78 -> 78, of which waited for: 59 -> 57; matrix products, arithmetic and copies ran while one was open for 0% -> 0% of each run, Pallas kernels for 1% -> 1%
where the time goes in v4:
time: 195 us; the launch traced here: 194 us
  waiting for transfers between devices  87.5 us (45%)
  starting transfers between devices  85.5 us (44%)
  Pallas kernels  16.3 us (8%)
  local copies, waits for them, and re-layouts  3.88 us (2%)
    ppermute x18, waiting for transfers between devices, gather_panels(): far = [near] + [lax.ppermute(near, 'pcol', far_pairs(n)) for n in (1, 2, 3)]  43.3 us
    ppermute x18, starting transfers between devices, across_rows(): lax.ppermute(value, ('prow', 'pcol'), across_pairs(n + 1))  31.5 us
    ppermute x18, starting transfers between devices, gather_panels(): far = [near] + [lax.ppermute(near, 'pcol', far_pairs(n)) for n in (1, 2, 3)]  27.1 us
    ppermute x18, starting transfers between devices, gather_panels(): lax.ppermute(panel, 'pcol', near_pairs(n))  26.6 us
    ppermute x18, waiting for transfers between devices, across_rows(): lax.ppermute(value, ('prow', 'pcol'), across_pairs(n + 1))  19.1 us
    ppermute x18, waiting for transfers between devices, gather_panels(): lax.ppermute(panel, 'pcol', near_pairs(n))  16 us
    ppermute x24, waiting for transfers between devices, gather_panels(): return far + [lax.ppermute(piece, 'pcol', CORE_PAIRS) for piece in far]  9.03 us
    pallas_call x7, Pallas kernels, solve(): pl.pallas_call(functools.partial(solve_kernel, uses, len(sums), keep, sen...  8.45 us
  transfers between devices with their start and end apart: 78, of which 57 were waited for; matrix products, arithmetic and copies ran while one was open for 0% of the time, Pallas kernels for 1%

profile of v4, /device:TPU:0, one launch (start us, length us, event | category | flops | bytes accessed | tf_op | source)
XLA Modules:
  0.0 194.4 jit_solution(7800035600832698509)
XLA Ops:
  3.1 3.3 %collective-permute-start.2 = (bf16[256,128]{1,0:T(8,128)(2,1)S(1)}, bf16[256,128]{1,0:T(8,128)(2,1)S(1)}, u32[]{:S(2)}, u32[]{:S(2)}) collective-permute-start(bf16[256,128]{1,0:T(8,128)(2,1)S(1)} %solve.7.refs_0_), channel_id=1, source_target_pairs={{0,4},{1,25},{2,6},{3,27},{4,0},{5,29},{6,2},{7,31},{8,12},{9,1},{... | collective-permute-start | bytes 196616 | tf_op jit(solution)/shard_map/ppermute | solution.py:262
  7.1 2.6 %collective-permute-start = (bf16[256,128]{1,0:T(8,128)(2,1)S(1)}, bf16[256,128]{1,0:T(8,128)(2,1)S(1)}, u32[]{:S(2)}, u32[]{:S(2)}) collective-permute-start(bf16[256,128]{1,0:T(8,128)(2,1)S(1)} %solve.7.refs_0_), channel_id=1, source_target_pairs={{0,6},{1,9},{2,0},{3,11},{4,2},{5,13},{6,4},{7,15},{8,14},{9,17},{... | collective-permute-start | bytes 196616 | tf_op jit(solution)/shard_map/ppermute | solution.py:262
  12.6 3.1 %collective-permute-start.5 = (bf16[4,256,128]{2,1,0:T(8,128)(2,1)S(1)}, bf16[4,256,128]{2,1,0:T(8,128)(2,1)S(1)}, u32[]{:S(2)}, u32[]{:S(2)}) collective-permute-start(bf16[4,256,128]{2,1,0:T(8,128)(2,1)S(1)} %stack_after.1.refs_0_), channel_id=1, source_target_pairs={{0,16},{1,5},{2,18},{3,7},{4,20},{5,1},{6,22},{7,3},{8,24},{9,13},... | collective-permute-start | bytes 786440 | tf_op jit(solution)/shard_map/ppermute | solution.py:264
  17.8 2.8 %collective-permute-done.5.refs_3_ = bf16[4,256,128]{2,1,0:T(8,128)(2,1)S(1)} collective-permute-done((bf16[4,256,128]{2,1,0:T(8,128)(2,1)S(1)}, bf16[4,256,128]{2,1,0:T(8,128)(2,1)S(1)}, u32[]{:S(2)}, u32[]{:S(2)}) %collective-permute-start.5) | collective-permute-done | bytes 262176 | tf_op jit(solution)/shard_map/ppermute | solution.py:264
  20.6 2.9 %collective-permute-done.4.refs_2_ = bf16[4,256,128]{2,1,0:T(8,128)(2,1)S(1)} collective-permute-done((bf16[4,256,128]{2,1,0:T(8,128)(2,1)S(1)}, bf16[4,256,128]{2,1,0:T(8,128)(2,1)S(1)}, u32[]{:S(2)}, u32[]{:S(2)}) %collective-permute-start.4) | collective-permute-done | bytes 262176 | tf_op jit(solution)/shard_map/ppermute | solution.py:264
  27.5 5.0 %collective-permute-start.10 = (bf16[256,128]{1,0:T(8,128)(2,1)S(1)}, bf16[256,128]{1,0:T(8,128)(2,1)S(1)}, u32[]{:S(2)}, u32[]{:S(2)}) collective-permute-start(bf16[256,128]{1,0:T(8,128)(2,1)S(1)} %get-tuple-element.33), channel_id=1, source_target_pairs={{0,64},{1,65},{2,66},{3,67},{4,68},{5,69},{6,70},{7,71},{8,72},{9,... | collective-permute-start | bytes 196616 | tf_op jit(solution)/shard_map/ppermute | solution.py:269
  33.6 2.2 %collective-permute-start.12 = (bf16[256,128]{1,0:T(8,128)(2,1)S(1)}, bf16[256,128]{1,0:T(8,128)(2,1)S(1)}, u32[]{:S(2)}, u32[]{:S(2)}) collective-permute-start(bf16[256,128]{1,0:T(8,128)(2,1)S(1)} %get-tuple-element.35), channel_id=1, source_target_pairs={{0,96},{1,97},{2,98},{3,99},{4,100},{5,101},{6,102},{7,103},{8,104... | collective-permute-start | bytes 196616 | tf_op jit(solution)/shard_map/ppermute | solution.py:269
  35.8 2.2 %collective-permute-done.11.refs_2_ = bf16[256,128]{1,0:T(8,128)(2,1)S(1)} collective-permute-done((bf16[256,128]{1,0:T(8,128)(2,1)S(1)}, bf16[256,128]{1,0:T(8,128)(2,1)S(1)}, u32[]{:S(2)}, u32[]{:S(2)}) %collective-permute-start.11) | collective-permute-done | bytes 65568 | tf_op jit(solution)/shard_map/ppermute | solution.py:269
  40.3 3.0 %collective-permute-start.14 = (bf16[256,128]{1,0:T(8,128)(2,1)S(1)}, bf16[256,128]{1,0:T(8,128)(2,1)S(1)}, u32[]{:S(2)}, u32[]{:S(2)}) collective-permute-start(bf16[256,128]{1,0:T(8,128)(2,1)S(1)} %solve.8), channel_id=1, source_target_pairs={{0,2},{1,17},{2,4},{3,19},{4,6},{5,21},{6,0},{7,23},{8,10},{9,25},... | collective-permute-start | bytes 196616 | tf_op jit(solution)/shard_map/ppermute | solution.py:262
  45.8 1.8 collective-permute-done.13
  49.2 2.4 %collective-permute-start.17 = (bf16[4,256,128]{2,1,0:T(8,128)(2,1)S(1)}, bf16[4,256,128]{2,1,0:T(8,128)(2,1)S(1)}, u32[]{:S(2)}, u32[]{:S(2)}) collective-permute-start(bf16[4,256,128]{2,1,0:T(8,128)(2,1)S(1)} %pad_maximum_fusion.refs_0_), channel_id=1, source_target_pairs={{0,24},{1,7},{2,26},{3,1},{4,28},{5,3},{6,30},{7,5},{8,0},{9,15},{... | collective-permute-start | bytes 786440 | tf_op jit(solution)/shard_map/ppermute | solution.py:264
  51.6 4.0 %collective-permute-done.18.refs_3_ = bf16[4,256,128]{2,1,0:T(8,128)(2,1)S(1)} collective-permute-done((bf16[4,256,128]{2,1,0:T(8,128)(2,1)S(1)}, bf16[4,256,128]{2,1,0:T(8,128)(2,1)S(1)}, u32[]{:S(2)}, u32[]{:S(2)}) %collective-permute-start.18) | collective-permute-done | bytes 262176 | tf_op jit(solution)/shard_map/ppermute | solution.py:264
  55.6 2.2 %collective-permute-done.17.refs_2_ = bf16[4,256,128]{2,1,0:T(8,128)(2,1)S(1)} collective-permute-done((bf16[4,256,128]{2,1,0:T(8,128)(2,1)S(1)}, bf16[4,256,128]{2,1,0:T(8,128)(2,1)S(1)}, u32[]{:S(2)}, u32[]{:S(2)}) %collective-permute-start.17) | collective-permute-done | bytes 262176 | tf_op jit(solution)/shard_map/ppermute | solution.py:264
  62.4 2.6 %collective-permute-start.24 = (bf16[256,128]{1,0:T(8,128)(2,1)S(1)}, bf16[256,128]{1,0:T(8,128)(2,1)S(1)}, u32[]{:S(2)}, u32[]{:S(2)}) collective-permute-start(bf16[256,128]{1,0:T(8,128)(2,1)S(1)} %get-tuple-element.39), channel_id=1, source_target_pairs={{0,32},{1,33},{2,34},{3,35},{4,36},{5,37},{6,38},{7,39},{8,40},{9,... | collective-permute-start | bytes 196616 | tf_op jit(solution)/shard_map/ppermute | solution.py:269
  65.6 2.4 %collective-permute-done.23.refs_1_ = bf16[256,128]{1,0:T(8,128)(2,1)S(1)} collective-permute-done((bf16[256,128]{1,0:T(8,128)(2,1)S(1)}, bf16[256,128]{1,0:T(8,128)(2,1)S(1)}, u32[]{:S(2)}, u32[]{:S(2)}) %collective-permute-start.23) | collective-permute-done | bytes 65568 | tf_op jit(solution)/shard_map/ppermute | solution.py:269
  71.0 1.8 collective-permute-start.27
  74.2 1.9 collective-permute-done.28
  77.1 3.4 %collective-permute-start.31 = (bf16[4,256,128]{2,1,0:T(8,128)(2,1)S(1)}, bf16[4,256,128]{2,1,0:T(8,128)(2,1)S(1)}, u32[]{:S(2)}, u32[]{:S(2)}) collective-permute-start(bf16[4,256,128]{2,1,0:T(8,128)(2,1)S(1)} %pad_maximum_fusion.1.refs_0_), channel_id=1, source_target_pairs={{0,16},{1,5},{2,18},{3,7},{4,20},{5,1},{6,22},{7,3},{8,24},{9,13},... | collective-permute-start | bytes 786440 | tf_op jit(solution)/shard_map/ppermute | solution.py:264
  80.5 2.3 %collective-permute-start.30 = (bf16[4,256,128]{2,1,0:T(8,128)(2,1)S(1)}, bf16[4,256,128]{2,1,0:T(8,128)(2,1)S(1)}, u32[]{:S(2)}, u32[]{:S(2)}) collective-permute-start(bf16[4,256,128]{2,1,0:T(8,128)(2,1)S(1)} %pad_maximum_fusion.1.refs_0_), channel_id=1, source_target_pairs={{0,24},{1,7},{2,26},{3,1},{4,28},{5,3},{6,30},{7,5},{8,0},{9,15},{... | collective-permute-start | bytes 786440 | tf_op jit(solution)/shard_map/ppermute | solution.py:264
  82.8 2.3 %collective-permute-done.31.refs_3_ = bf16[4,256,128]{2,1,0:T(8,128)(2,1)S(1)} collective-permute-done((bf16[4,256,128]{2,1,0:T(8,128)(2,1)S(1)}, bf16[4,256,128]{2,1,0:T(8,128)(2,1)S(1)}, u32[]{:S(2)}, u32[]{:S(2)}) %collective-permute-start.31) | collective-permute-done | bytes 262176 | tf_op jit(solution)/shard_map/ppermute | solution.py:264
  85.1 3.4 %collective-permute-done.30.refs_2_ = bf16[4,256,128]{2,1,0:T(8,128)(2,1)S(1)} collective-permute-done((bf16[4,256,128]{2,1,0:T(8,128)(2,1)S(1)}, bf16[4,256,128]{2,1,0:T(8,128)(2,1)S(1)}, u32[]{:S(2)}, u32[]{:S(2)}) %collective-permute-start.30) | collective-permute-done | bytes 262176 | tf_op jit(solution)/shard_map/ppermute | solution.py:264
  88.5 1.9 collective-permute-done.29.refs_1_
  93.5 1.9 collective-permute-start.37
  96.7 2.4 %collective-permute-done.36.refs_1_ = bf16[256,128]{1,0:T(8,128)(2,1)S(1)} collective-permute-done((bf16[256,128]{1,0:T(8,128)(2,1)S(1)}, bf16[256,128]{1,0:T(8,128)(2,1)S(1)}, u32[]{:S(2)}, u32[]{:S(2)}) %collective-permute-start.36) | collective-permute-done | bytes 65568 | tf_op jit(solution)/shard_map/ppermute | solution.py:269
  99.9 1.9 solve.10
  104.0 1.8 collective-permute-start.39
  105.8 1.8 collective-permute-done.41
  108.4 2.8 %collective-permute-start.44 = (bf16[4,256,128]{2,1,0:T(8,128)(2,1)S(1)}, bf16[4,256,128]{2,1,0:T(8,128)(2,1)S(1)}, u32[]{:S(2)}, u32[]{:S(2)}) collective-permute-start(bf16[4,256,128]{2,1,0:T(8,128)(2,1)S(1)} %pad_maximum_fusion.2.refs_0_), channel_id=1, source_target_pairs={{0,16},{1,5},{2,18},{3,7},{4,20},{5,1},{6,22},{7,3},{8,24},{9,13},... | collective-permute-start | bytes 786440 | tf_op jit(solution)/shard_map/ppermute | solution.py:264
  113.2 3.1 %collective-permute-done.44.refs_3_ = bf16[4,256,128]{2,1,0:T(8,128)(2,1)S(1)} collective-permute-done((bf16[4,256,128]{2,1,0:T(8,128)(2,1)S(1)}, bf16[4,256,128]{2,1,0:T(8,128)(2,1)S(1)}, u32[]{:S(2)}, u32[]{:S(2)}) %collective-permute-start.44) | collective-permute-done | bytes 262176 | tf_op jit(solution)/shard_map/ppermute | solution.py:264
  116.3 3.2 %collective-permute-done.43.refs_2_ = bf16[4,256,128]{2,1,0:T(8,128)(2,1)S(1)} collective-permute-done((bf16[4,256,128]{2,1,0:T(8,128)(2,1)S(1)}, bf16[4,256,128]{2,1,0:T(8,128)(2,1)S(1)}, u32[]{:S(2)}, u32[]{:S(2)}) %collective-permute-start.43) | collective-permute-done | bytes 262176 | tf_op jit(solution)/shard_map/ppermute | solution.py:264
  121.7 1.9 tile_products.9
  124.9 2.9 %collective-permute-start.50 = (bf16[256,128]{1,0:T(8,128)(2,1)S(1)}, bf16[256,128]{1,0:T(8,128)(2,1)S(1)}, u32[]{:S(2)}, u32[]{:S(2)}) collective-permute-start(bf16[256,128]{1,0:T(8,128)(2,1)S(1)} %get-tuple-element.50), channel_id=1, source_target_pairs={{0,32},{1,33},{2,34},{3,35},{4,36},{5,37},{6,38},{7,39},{8,40},{9,... | collective-permute-start | bytes 196616 | tf_op jit(solution)/shard_map/ppermute | solution.py:269
  133.3 2.5 %collective-permute-start.53 = (bf16[256,128]{1,0:T(8,128)(2,1)S(1)}, bf16[256,128]{1,0:T(8,128)(2,1)S(1)}, u32[]{:S(2)}, u32[]{:S(2)}) collective-permute-start(bf16[256,128]{1,0:T(8,128)(2,1)S(1)} %solve.11), channel_id=1, source_target_pairs={{0,2},{1,17},{2,4},{3,19},{4,6},{5,21},{6,0},{7,23},{8,10},{9,25},... | collective-permute-start | bytes 196616 | tf_op jit(solution)/shard_map/ppermute | solution.py:262
  136.5 2.5 %collective-permute-done.54 = bf16[256,128]{1,0:T(8,128)(2,1)S(1)} collective-permute-done((bf16[256,128]{1,0:T(8,128)(2,1)S(1)}, bf16[256,128]{1,0:T(8,128)(2,1)S(1)}, u32[]{:S(2)}, u32[]{:S(2)}) %collective-permute-start.54) | collective-permute-done | bytes 65568 | tf_op jit(solution)/shard_map/ppermute | solution.py:262
  140.1 1.9 collective-permute-start.57
  144.0 4.0 %collective-permute-done.57.refs_3_ = bf16[4,256,128]{2,1,0:T(8,128)(2,1)S(1)} collective-permute-done((bf16[4,256,128]{2,1,0:T(8,128)(2,1)S(1)}, bf16[4,256,128]{2,1,0:T(8,128)(2,1)S(1)}, u32[]{:S(2)}, u32[]{:S(2)}) %collective-permute-start.57) | collective-permute-done | bytes 262176 | tf_op jit(solution)/shard_map/ppermute | solution.py:264
  148.1 2.6 %collective-permute-done.56.refs_2_ = bf16[4,256,128]{2,1,0:T(8,128)(2,1)S(1)} collective-permute-done((bf16[4,256,128]{2,1,0:T(8,128)(2,1)S(1)}, bf16[4,256,128]{2,1,0:T(8,128)(2,1)S(1)}, u32[]{:S(2)}, u32[]{:S(2)}) %collective-permute-start.56) | collective-permute-done | bytes 262176 | tf_op jit(solution)/shard_map/ppermute | solution.py:264
  153.7 2.4 %collective-permute-start.62 = (bf16[256,128]{1,0:T(8,128)(2,1)S(1)}, bf16[256,128]{1,0:T(8,128)(2,1)S(1)}, u32[]{:S(2)}, u32[]{:S(2)}) collective-permute-start(bf16[256,128]{1,0:T(8,128)(2,1)S(1)} %get-tuple-element.54), channel_id=1, source_target_pairs={{0,64},{1,65},{2,66},{3,67},{4,68},{5,69},{6,70},{7,71},{8,72},{9,... | collective-permute-start | bytes 196616 | tf_op jit(solution)/shard_map/ppermute | solution.py:269
  156.1 2.8 %collective-permute-start.63 = (bf16[256,128]{1,0:T(8,128)(2,1)S(1)}, bf16[256,128]{1,0:T(8,128)(2,1)S(1)}, u32[]{:S(2)}, u32[]{:S(2)}) collective-permute-start(bf16[256,128]{1,0:T(8,128)(2,1)S(1)} %get-tuple-element.55), channel_id=1, source_target_pairs={{0,32},{1,33},{2,34},{3,35},{4,36},{5,37},{6,38},{7,39},{8,40},{9,... | collective-permute-start | bytes 196616 | tf_op jit(solution)/shard_map/ppermute | solution.py:269
  160.0 1.6 collective-permute-done.63.refs_2_
  165.2 2.1 %collective-permute-start.66 = (bf16[256,128]{1,0:T(8,128)(2,1)S(1)}, bf16[256,128]{1,0:T(8,128)(2,1)S(1)}, u32[]{:S(2)}, u32[]{:S(2)}) collective-permute-start(bf16[256,128]{1,0:T(8,128)(2,1)S(1)} %solve.12), channel_id=1, source_target_pairs={{0,2},{1,17},{2,4},{3,19},{4,6},{5,21},{6,0},{7,23},{8,10},{9,25},... | collective-permute-start | bytes 196616 | tf_op jit(solution)/shard_map/ppermute | solution.py:262
  168.4 1.6 collective-permute-done.67
  173.1 2.0 %collective-permute-start.69 = (bf16[4,256,128]{2,1,0:T(8,128)(2,1)S(1)}, bf16[4,256,128]{2,1,0:T(8,128)(2,1)S(1)}, u32[]{:S(2)}, u32[]{:S(2)}) collective-permute-start(bf16[4,256,128]{2,1,0:T(8,128)(2,1)S(1)} %pad_maximum_fusion.4.refs_0_), channel_id=1, source_target_pairs={{0,24},{1,7},{2,26},{3,1},{4,28},{5,3},{6,30},{7,5},{8,0},{9,15},{... | collective-permute-start | bytes 786440 | tf_op jit(solution)/shard_map/ppermute | solution.py:264
  175.2 4.4 %collective-permute-done.70.refs_3_ = bf16[4,256,128]{2,1,0:T(8,128)(2,1)S(1)} collective-permute-done((bf16[4,256,128]{2,1,0:T(8,128)(2,1)S(1)}, bf16[4,256,128]{2,1,0:T(8,128)(2,1)S(1)}, u32[]{:S(2)}, u32[]{:S(2)}) %collective-permute-start.70) | collective-permute-done | bytes 262176 | tf_op jit(solution)/shard_map/ppermute | solution.py:264
  179.6 2.0 %collective-permute-done.69.refs_2_ = bf16[4,256,128]{2,1,0:T(8,128)(2,1)S(1)} collective-permute-done((bf16[4,256,128]{2,1,0:T(8,128)(2,1)S(1)}, bf16[4,256,128]{2,1,0:T(8,128)(2,1)S(1)}, u32[]{:S(2)}, u32[]{:S(2)}) %collective-permute-start.69) | collective-permute-done | bytes 262176 | tf_op jit(solution)/shard_map/ppermute | solution.py:264
  185.1 1.8 collective-permute-start.75
  188.1 2.1 %collective-permute-start.77 = (bf16[256,128]{1,0:T(8,128)(2,1)S(1)}, bf16[256,128]{1,0:T(8,128)(2,1)S(1)}, u32[]{:S(2)}, u32[]{:S(2)}) collective-permute-start(bf16[256,128]{1,0:T(8,128)(2,1)S(1)} %get-tuple-element.61), channel_id=1, source_target_pairs={{0,96},{1,97},{2,98},{3,99},{4,100},{5,101},{6,102},{7,103},{8,104... | collective-permute-start | bytes 196616 | tf_op jit(solution)/shard_map/ppermute | solution.py:269
  192.5 1.7 solve.13
  (147 shorter events, 72.0 us)
Async XLA Ops:
  3.1 9.1 %collective-permute-start.2 = (bf16[256,128]{1,0:T(8,128)(2,1)S(1)}, bf16[256,128]{1,0:T(8,128)(2,1)S(1)}, u32[]{:S(2)}, u32[]{:S(2)}) collective-permute-start(bf16[256,128]{1,0:T(8,128)(2,1)S(1)} %solve.7.refs_0_), channel_id=1, source_target_pairs={{0,4},{1,25},{2,6},{3,27},{4,0},{5,29},{6,2},{7,31},{8,12},{9,1},{... | collective-permute-start | bytes 196616 | tf_op jit(solution)/shard_map/ppermute | solution.py:262
  6.4 5.8 %collective-permute-start.1 = (bf16[256,128]{1,0:T(8,128)(2,1)S(1)}, bf16[256,128]{1,0:T(8,128)(2,1)S(1)}, u32[]{:S(2)}, u32[]{:S(2)}) collective-permute-start(bf16[256,128]{1,0:T(8,128)(2,1)S(1)} %solve.7.refs_0_), channel_id=1, source_target_pairs={{0,2},{1,17},{2,4},{3,19},{4,6},{5,21},{6,0},{7,23},{8,10},{9,25},... | collective-permute-start | bytes 196616 | tf_op jit(solution)/shard_map/ppermute | solution.py:262
  12.6 8.0 %collective-permute-start.5 = (bf16[4,256,128]{2,1,0:T(8,128)(2,1)S(1)}, bf16[4,256,128]{2,1,0:T(8,128)(2,1)S(1)}, u32[]{:S(2)}, u32[]{:S(2)}) collective-permute-start(bf16[4,256,128]{2,1,0:T(8,128)(2,1)S(1)} %stack_after.1.refs_0_), channel_id=1, source_target_pairs={{0,16},{1,5},{2,18},{3,7},{4,20},{5,1},{6,22},{7,3},{8,24},{9,13},... | collective-permute-start | bytes 786440 | tf_op jit(solution)/shard_map/ppermute | solution.py:264
  15.7 7.8 %collective-permute-start.4 = (bf16[4,256,128]{2,1,0:T(8,128)(2,1)S(1)}, bf16[4,256,128]{2,1,0:T(8,128)(2,1)S(1)}, u32[]{:S(2)}, u32[]{:S(2)}) collective-permute-start(bf16[4,256,128]{2,1,0:T(8,128)(2,1)S(1)} %stack_after.1.refs_0_), channel_id=1, source_target_pairs={{0,24},{1,7},{2,26},{3,1},{4,28},{5,3},{6,30},{7,5},{8,0},{9,15},{... | collective-permute-start | bytes 786440 | tf_op jit(solution)/shard_map/ppermute | solution.py:264
  16.9 7.6 %collective-permute-start.3 = (bf16[4,256,128]{2,1,0:T(8,128)(2,1)S(1)}, bf16[4,256,128]{2,1,0:T(8,128)(2,1)S(1)}, u32[]{:S(2)}, u32[]{:S(2)}) collective-permute-start(bf16[4,256,128]{2,1,0:T(8,128)(2,1)S(1)} %stack_after.1.refs_0_), channel_id=1, source_target_pairs={{0,8},{1,3},{2,10},{3,5},{4,12},{5,7},{6,14},{7,1},{8,16},{9,11},{... | collective-permute-start | bytes 786440 | tf_op jit(solution)/shard_map/ppermute | solution.py:264
  17.8 6.7 %collective-permute-start.6 = (bf16[4,256,128]{2,1,0:T(8,128)(2,1)S(1)}, bf16[4,256,128]{2,1,0:T(8,128)(2,1)S(1)}, u32[]{:S(2)}, u32[]{:S(2)}) collective-permute-start(bf16[4,256,128]{2,1,0:T(8,128)(2,1)S(1)} %stack_after.1.refs_0_), channel_id=1, source_target_pairs={{0,1},{1,0},{2,3},{3,2},{4,5},{5,4},{6,7},{7,6},{8,9},{9,8},{10,11... | collective-permute-start | bytes 786440 | tf_op jit(solution)/shard_map/ppermute | solution.py:265
  27.5 8.3 %collective-permute-start.10 = (bf16[256,128]{1,0:T(8,128)(2,1)S(1)}, bf16[256,128]{1,0:T(8,128)(2,1)S(1)}, u32[]{:S(2)}, u32[]{:S(2)}) collective-permute-start(bf16[256,128]{1,0:T(8,128)(2,1)S(1)} %get-tuple-element.33), channel_id=1, source_target_pairs={{0,64},{1,65},{2,66},{3,67},{4,68},{5,69},{6,70},{7,71},{8,72},{9,... | collective-permute-start | bytes 196616 | tf_op jit(solution)/shard_map/ppermute | solution.py:269
  32.5 5.5 %collective-permute-start.11 = (bf16[256,128]{1,0:T(8,128)(2,1)S(1)}, bf16[256,128]{1,0:T(8,128)(2,1)S(1)}, u32[]{:S(2)}, u32[]{:S(2)}) collective-permute-start(bf16[256,128]{1,0:T(8,128)(2,1)S(1)} %get-tuple-element.34), channel_id=1, source_target_pairs={{0,32},{1,33},{2,34},{3,35},{4,36},{5,37},{6,38},{7,39},{8,40},{9,... | collective-permute-start | bytes 196616 | tf_op jit(solution)/shard_map/ppermute | solution.py:269
  39.1 5.8 %collective-permute-start.15 = (bf16[256,128]{1,0:T(8,128)(2,1)S(1)}, bf16[256,128]{1,0:T(8,128)(2,1)S(1)}, u32[]{:S(2)}, u32[]{:S(2)}) collective-permute-start(bf16[256,128]{1,0:T(8,128)(2,1)S(1)} %solve.8), channel_id=1, source_target_pairs={{0,4},{1,25},{2,6},{3,27},{4,0},{5,29},{6,2},{7,31},{8,12},{9,1},{... | collective-permute-start | bytes 196616 | tf_op jit(solution)/shard_map/ppermute | solution.py:262
  40.3 5.5 %collective-permute-start.14 = (bf16[256,128]{1,0:T(8,128)(2,1)S(1)}, bf16[256,128]{1,0:T(8,128)(2,1)S(1)}, u32[]{:S(2)}, u32[]{:S(2)}) collective-permute-start(bf16[256,128]{1,0:T(8,128)(2,1)S(1)} %solve.8), channel_id=1, source_target_pairs={{0,2},{1,17},{2,4},{3,19},{4,6},{5,21},{6,0},{7,23},{8,10},{9,25},... | collective-permute-start | bytes 196616 | tf_op jit(solution)/shard_map/ppermute | solution.py:262
  47.6 8.0 %collective-permute-start.18 = (bf16[4,256,128]{2,1,0:T(8,128)(2,1)S(1)}, bf16[4,256,128]{2,1,0:T(8,128)(2,1)S(1)}, u32[]{:S(2)}, u32[]{:S(2)}) collective-permute-start(bf16[4,256,128]{2,1,0:T(8,128)(2,1)S(1)} %pad_maximum_fusion.refs_0_), channel_id=1, source_target_pairs={{0,16},{1,5},{2,18},{3,7},{4,20},{5,1},{6,22},{7,3},{8,24},{9,13},... | collective-permute-start | bytes 786440 | tf_op jit(solution)/shard_map/ppermute | solution.py:264
  49.2 8.6 %collective-permute-start.17 = (bf16[4,256,128]{2,1,0:T(8,128)(2,1)S(1)}, bf16[4,256,128]{2,1,0:T(8,128)(2,1)S(1)}, u32[]{:S(2)}, u32[]{:S(2)}) collective-permute-start(bf16[4,256,128]{2,1,0:T(8,128)(2,1)S(1)} %pad_maximum_fusion.refs_0_), channel_id=1, source_target_pairs={{0,24},{1,7},{2,26},{3,1},{4,28},{5,3},{6,30},{7,5},{8,0},{9,15},{... | collective-permute-start | bytes 786440 | tf_op jit(solution)/shard_map/ppermute | solution.py:264
  51.6 7.6 %collective-permute-start.16 = (bf16[4,256,128]{2,1,0:T(8,128)(2,1)S(1)}, bf16[4,256,128]{2,1,0:T(8,128)(2,1)S(1)}, u32[]{:S(2)}, u32[]{:S(2)}) collective-permute-start(bf16[4,256,128]{2,1,0:T(8,128)(2,1)S(1)} %pad_maximum_fusion.refs_0_), channel_id=1, source_target_pairs={{0,8},{1,3},{2,10},{3,5},{4,12},{5,7},{6,14},{7,1},{8,16},{9,11},{... | collective-permute-start | bytes 786440 | tf_op jit(solution)/shard_map/ppermute | solution.py:264
  51.6 7.6 %collective-permute-start.19 = (bf16[4,256,128]{2,1,0:T(8,128)(2,1)S(1)}, bf16[4,256,128]{2,1,0:T(8,128)(2,1)S(1)}, u32[]{:S(2)}, u32[]{:S(2)}) collective-permute-start(bf16[4,256,128]{2,1,0:T(8,128)(2,1)S(1)} %pad_maximum_fusion.refs_0_), channel_id=1, source_target_pairs={{0,1},{1,0},{2,3},{3,2},{4,5},{5,4},{6,7},{7,6},{8,9},{9,8},{10,11... | collective-permute-start | bytes 786440 | tf_op jit(solution)/shard_map/ppermute | solution.py:265
  61.6 6.4 %collective-permute-start.23 = (bf16[256,128]{1,0:T(8,128)(2,1)S(1)}, bf16[256,128]{1,0:T(8,128)(2,1)S(1)}, u32[]{:S(2)}, u32[]{:S(2)}) collective-permute-start(bf16[256,128]{1,0:T(8,128)(2,1)S(1)} %get-tuple-element.38), channel_id=1, source_target_pairs={{0,64},{1,65},{2,66},{3,67},{4,68},{5,69},{6,70},{7,71},{8,72},{9,... | collective-permute-start | bytes 196616 | tf_op jit(solution)/shard_map/ppermute | solution.py:269
  62.4 6.3 %collective-permute-start.24 = (bf16[256,128]{1,0:T(8,128)(2,1)S(1)}, bf16[256,128]{1,0:T(8,128)(2,1)S(1)}, u32[]{:S(2)}, u32[]{:S(2)}) collective-permute-start(bf16[256,128]{1,0:T(8,128)(2,1)S(1)} %get-tuple-element.39), channel_id=1, source_target_pairs={{0,32},{1,33},{2,34},{3,35},{4,36},{5,37},{6,38},{7,39},{8,40},{9,... | collective-permute-start | bytes 196616 | tf_op jit(solution)/shard_map/ppermute | solution.py:269
  70.3 5.9 %collective-permute-start.28 = (bf16[256,128]{1,0:T(8,128)(2,1)S(1)}, bf16[256,128]{1,0:T(8,128)(2,1)S(1)}, u32[]{:S(2)}, u32[]{:S(2)}) collective-permute-start(bf16[256,128]{1,0:T(8,128)(2,1)S(1)} %solve.9), channel_id=1, source_target_pairs={{0,4},{1,25},{2,6},{3,27},{4,0},{5,29},{6,2},{7,31},{8,12},{9,1},{... | collective-permute-start | bytes 196616 | tf_op jit(solution)/shard_map/ppermute | solution.py:262
  71.0 5.8 %collective-permute-start.27 = (bf16[256,128]{1,0:T(8,128)(2,1)S(1)}, bf16[256,128]{1,0:T(8,128)(2,1)S(1)}, u32[]{:S(2)}, u32[]{:S(2)}) collective-permute-start(bf16[256,128]{1,0:T(8,128)(2,1)S(1)} %solve.9), channel_id=1, source_target_pairs={{0,2},{1,17},{2,4},{3,19},{4,6},{5,21},{6,0},{7,23},{8,10},{9,25},... | collective-permute-start | bytes 196616 | tf_op jit(solution)/shard_map/ppermute | solution.py:262
  77.1 8.0 %collective-permute-start.31 = (bf16[4,256,128]{2,1,0:T(8,128)(2,1)S(1)}, bf16[4,256,128]{2,1,0:T(8,128)(2,1)S(1)}, u32[]{:S(2)}, u32[]{:S(2)}) collective-permute-start(bf16[4,256,128]{2,1,0:T(8,128)(2,1)S(1)} %pad_maximum_fusion.1.refs_0_), channel_id=1, source_target_pairs={{0,16},{1,5},{2,18},{3,7},{4,20},{5,1},{6,22},{7,3},{8,24},{9,13},... | collective-permute-start | bytes 786440 | tf_op jit(solution)/shard_map/ppermute | solution.py:264
  80.5 7.9 %collective-permute-start.30 = (bf16[4,256,128]{2,1,0:T(8,128)(2,1)S(1)}, bf16[4,256,128]{2,1,0:T(8,128)(2,1)S(1)}, u32[]{:S(2)}, u32[]{:S(2)}) collective-permute-start(bf16[4,256,128]{2,1,0:T(8,128)(2,1)S(1)} %pad_maximum_fusion.1.refs_0_), channel_id=1, source_target_pairs={{0,24},{1,7},{2,26},{3,1},{4,28},{5,3},{6,30},{7,5},{8,0},{9,15},{... | collective-permute-start | bytes 786440 | tf_op jit(solution)/shard_map/ppermute | solution.py:264
  82.8 7.6 %collective-permute-start.29 = (bf16[4,256,128]{2,1,0:T(8,128)(2,1)S(1)}, bf16[4,256,128]{2,1,0:T(8,128)(2,1)S(1)}, u32[]{:S(2)}, u32[]{:S(2)}) collective-permute-start(bf16[4,256,128]{2,1,0:T(8,128)(2,1)S(1)} %pad_maximum_fusion.1.refs_0_), channel_id=1, source_target_pairs={{0,8},{1,3},{2,10},{3,5},{4,12},{5,7},{6,14},{7,1},{8,16},{9,11},{... | collective-permute-start | bytes 786440 | tf_op jit(solution)/shard_map/ppermute | solution.py:264
  82.8 7.6 %collective-permute-start.32 = (bf16[4,256,128]{2,1,0:T(8,128)(2,1)S(1)}, bf16[4,256,128]{2,1,0:T(8,128)(2,1)S(1)}, u32[]{:S(2)}, u32[]{:S(2)}) collective-permute-start(bf16[4,256,128]{2,1,0:T(8,128)(2,1)S(1)} %pad_maximum_fusion.1.refs_0_), channel_id=1, source_target_pairs={{0,1},{1,0},{2,3},{3,2},{4,5},{5,4},{6,7},{7,6},{8,9},{9,8},{10,11... | collective-permute-start | bytes 786440 | tf_op jit(solution)/shard_map/ppermute | solution.py:265
  92.7 6.4 %collective-permute-start.36 = (bf16[256,128]{1,0:T(8,128)(2,1)S(1)}, bf16[256,128]{1,0:T(8,128)(2,1)S(1)}, u32[]{:S(2)}, u32[]{:S(2)}) collective-permute-start(bf16[256,128]{1,0:T(8,128)(2,1)S(1)} %get-tuple-element.43), channel_id=1, source_target_pairs={{0,64},{1,65},{2,66},{3,67},{4,68},{5,69},{6,70},{7,71},{8,72},{9,... | collective-permute-start | bytes 196616 | tf_op jit(solution)/shard_map/ppermute | solution.py:269
  93.5 6.4 %collective-permute-start.37 = (bf16[256,128]{1,0:T(8,128)(2,1)S(1)}, bf16[256,128]{1,0:T(8,128)(2,1)S(1)}, u32[]{:S(2)}, u32[]{:S(2)}) collective-permute-start(bf16[256,128]{1,0:T(8,128)(2,1)S(1)} %get-tuple-element.44), channel_id=1, source_target_pairs={{0,32},{1,33},{2,34},{3,35},{4,36},{5,37},{6,38},{7,39},{8,40},{9,... | collective-permute-start | bytes 196616 | tf_op jit(solution)/shard_map/ppermute | solution.py:269
  101.8 5.9 %collective-permute-start.41 = (bf16[256,128]{1,0:T(8,128)(2,1)S(1)}, bf16[256,128]{1,0:T(8,128)(2,1)S(1)}, u32[]{:S(2)}, u32[]{:S(2)}) collective-permute-start(bf16[256,128]{1,0:T(8,128)(2,1)S(1)} %get-tuple-element.47), channel_id=1, source_target_pairs={{0,4},{1,25},{2,6},{3,27},{4,0},{5,29},{6,2},{7,31},{8,12},{9,1},{... | collective-permute-start | bytes 196616 | tf_op jit(solution)/shard_map/ppermute | solution.py:262
  102.6 5.7 %collective-permute-start.40 = (bf16[256,128]{1,0:T(8,128)(2,1)S(1)}, bf16[256,128]{1,0:T(8,128)(2,1)S(1)}, u32[]{:S(2)}, u32[]{:S(2)}) collective-permute-start(bf16[256,128]{1,0:T(8,128)(2,1)S(1)} %get-tuple-element.47), channel_id=1, source_target_pairs={{0,2},{1,17},{2,4},{3,19},{4,6},{5,21},{6,0},{7,23},{8,10},{9,25},... | collective-permute-start | bytes 196616 | tf_op jit(solution)/shard_map/ppermute | solution.py:262
  108.4 8.0 %collective-permute-start.44 = (bf16[4,256,128]{2,1,0:T(8,128)(2,1)S(1)}, bf16[4,256,128]{2,1,0:T(8,128)(2,1)S(1)}, u32[]{:S(2)}, u32[]{:S(2)}) collective-permute-start(bf16[4,256,128]{2,1,0:T(8,128)(2,1)S(1)} %pad_maximum_fusion.2.refs_0_), channel_id=1, source_target_pairs={{0,16},{1,5},{2,18},{3,7},{4,20},{5,1},{6,22},{7,3},{8,24},{9,13},... | collective-permute-start | bytes 786440 | tf_op jit(solution)/shard_map/ppermute | solution.py:264
  111.2 8.3 %collective-permute-start.43 = (bf16[4,256,128]{2,1,0:T(8,128)(2,1)S(1)}, bf16[4,256,128]{2,1,0:T(8,128)(2,1)S(1)}, u32[]{:S(2)}, u32[]{:S(2)}) collective-permute-start(bf16[4,256,128]{2,1,0:T(8,128)(2,1)S(1)} %pad_maximum_fusion.2.refs_0_), channel_id=1, source_target_pairs={{0,24},{1,7},{2,26},{3,1},{4,28},{5,3},{6,30},{7,5},{8,0},{9,15},{... | collective-permute-start | bytes 786440 | tf_op jit(solution)/shard_map/ppermute | solution.py:264
  112.6 7.6 %collective-permute-start.42 = (bf16[4,256,128]{2,1,0:T(8,128)(2,1)S(1)}, bf16[4,256,128]{2,1,0:T(8,128)(2,1)S(1)}, u32[]{:S(2)}, u32[]{:S(2)}) collective-permute-start(bf16[4,256,128]{2,1,0:T(8,128)(2,1)S(1)} %pad_maximum_fusion.2.refs_0_), channel_id=1, source_target_pairs={{0,8},{1,3},{2,10},{3,5},{4,12},{5,7},{6,14},{7,1},{8,16},{9,11},{... | collective-permute-start | bytes 786440 | tf_op jit(solution)/shard_map/ppermute | solution.py:264
  113.2 7.0 %collective-permute-start.45 = (bf16[4,256,128]{2,1,0:T(8,128)(2,1)S(1)}, bf16[4,256,128]{2,1,0:T(8,128)(2,1)S(1)}, u32[]{:S(2)}, u32[]{:S(2)}) collective-permute-start(bf16[4,256,128]{2,1,0:T(8,128)(2,1)S(1)} %pad_maximum_fusion.2.refs_0_), channel_id=1, source_target_pairs={{0,1},{1,0},{2,3},{3,2},{4,5},{5,4},{6,7},{7,6},{8,9},{9,8},{10,11... | collective-permute-start | bytes 786440 | tf_op jit(solution)/shard_map/ppermute | solution.py:265
  123.6 6.0 %collective-permute-start.49 = (bf16[256,128]{1,0:T(8,128)(2,1)S(1)}, bf16[256,128]{1,0:T(8,128)(2,1)S(1)}, u32[]{:S(2)}, u32[]{:S(2)}) collective-permute-start(bf16[256,128]{1,0:T(8,128)(2,1)S(1)} %get-tuple-element.49), channel_id=1, source_target_pairs={{0,64},{1,65},{2,66},{3,67},{4,68},{5,69},{6,70},{7,71},{8,72},{9,... | collective-permute-start | bytes 196616 | tf_op jit(solution)/shard_map/ppermute | solution.py:269
  124.9 6.1 %collective-permute-start.50 = (bf16[256,128]{1,0:T(8,128)(2,1)S(1)}, bf16[256,128]{1,0:T(8,128)(2,1)S(1)}, u32[]{:S(2)}, u32[]{:S(2)}) collective-permute-start(bf16[256,128]{1,0:T(8,128)(2,1)S(1)} %get-tuple-element.50), channel_id=1, source_target_pairs={{0,32},{1,33},{2,34},{3,35},{4,36},{5,37},{6,38},{7,39},{8,40},{9,... | collective-permute-start | bytes 196616 | tf_op jit(solution)/shard_map/ppermute | solution.py:269
  133.1 5.9 %collective-permute-start.54 = (bf16[256,128]{1,0:T(8,128)(2,1)S(1)}, bf16[256,128]{1,0:T(8,128)(2,1)S(1)}, u32[]{:S(2)}, u32[]{:S(2)}) collective-permute-start(bf16[256,128]{1,0:T(8,128)(2,1)S(1)} %solve.11), channel_id=1, source_target_pairs={{0,4},{1,25},{2,6},{3,27},{4,0},{5,29},{6,2},{7,31},{8,12},{9,1},{... | collective-permute-start | bytes 196616 | tf_op jit(solution)/shard_map/ppermute | solution.py:262
  133.3 6.2 %collective-permute-start.53 = (bf16[256,128]{1,0:T(8,128)(2,1)S(1)}, bf16[256,128]{1,0:T(8,128)(2,1)S(1)}, u32[]{:S(2)}, u32[]{:S(2)}) collective-permute-start(bf16[256,128]{1,0:T(8,128)(2,1)S(1)} %solve.11), channel_id=1, source_target_pairs={{0,2},{1,17},{2,4},{3,19},{4,6},{5,21},{6,0},{7,23},{8,10},{9,25},... | collective-permute-start | bytes 196616 | tf_op jit(solution)/shard_map/ppermute | solution.py:262
  140.1 8.0 %collective-permute-start.57 = (bf16[4,256,128]{2,1,0:T(8,128)(2,1)S(1)}, bf16[4,256,128]{2,1,0:T(8,128)(2,1)S(1)}, u32[]{:S(2)}, u32[]{:S(2)}) collective-permute-start(bf16[4,256,128]{2,1,0:T(8,128)(2,1)S(1)} %pad_maximum_fusion.3.refs_0_), channel_id=1, source_target_pairs={{0,16},{1,5},{2,18},{3,7},{4,20},{5,1},{6,22},{7,3},{8,24},{9,13},... | collective-permute-start | bytes 786440 | tf_op jit(solution)/shard_map/ppermute | solution.py:264
  142.0 8.7 %collective-permute-start.56 = (bf16[4,256,128]{2,1,0:T(8,128)(2,1)S(1)}, bf16[4,256,128]{2,1,0:T(8,128)(2,1)S(1)}, u32[]{:S(2)}, u32[]{:S(2)}) collective-permute-start(bf16[4,256,128]{2,1,0:T(8,128)(2,1)S(1)} %pad_maximum_fusion.3.refs_0_), channel_id=1, source_target_pairs={{0,24},{1,7},{2,26},{3,1},{4,28},{5,3},{6,30},{7,5},{8,0},{9,15},{... | collective-permute-start | bytes 786440 | tf_op jit(solution)/shard_map/ppermute | solution.py:264
  143.4 7.6 %collective-permute-start.55 = (bf16[4,256,128]{2,1,0:T(8,128)(2,1)S(1)}, bf16[4,256,128]{2,1,0:T(8,128)(2,1)S(1)}, u32[]{:S(2)}, u32[]{:S(2)}) collective-permute-start(bf16[4,256,128]{2,1,0:T(8,128)(2,1)S(1)} %pad_maximum_fusion.3.refs_0_), channel_id=1, source_target_pairs={{0,8},{1,3},{2,10},{3,5},{4,12},{5,7},{6,14},{7,1},{8,16},{9,11},{... | collective-permute-start | bytes 786440 | tf_op jit(solution)/shard_map/ppermute | solution.py:264
  144.0 7.2 %collective-permute-start.58 = (bf16[4,256,128]{2,1,0:T(8,128)(2,1)S(1)}, bf16[4,256,128]{2,1,0:T(8,128)(2,1)S(1)}, u32[]{:S(2)}, u32[]{:S(2)}) collective-permute-start(bf16[4,256,128]{2,1,0:T(8,128)(2,1)S(1)} %pad_maximum_fusion.3.refs_0_), channel_id=1, source_target_pairs={{0,1},{1,0},{2,3},{3,2},{4,5},{5,4},{6,7},{7,6},{8,9},{9,8},{10,11... | collective-permute-start | bytes 786440 | tf_op jit(solution)/shard_map/ppermute | solution.py:265
  153.7 6.3 %collective-permute-start.62 = (bf16[256,128]{1,0:T(8,128)(2,1)S(1)}, bf16[256,128]{1,0:T(8,128)(2,1)S(1)}, u32[]{:S(2)}, u32[]{:S(2)}) collective-permute-start(bf16[256,128]{1,0:T(8,128)(2,1)S(1)} %get-tuple-element.54), channel_id=1, source_target_pairs={{0,64},{1,65},{2,66},{3,67},{4,68},{5,69},{6,70},{7,71},{8,72},{9,... | collective-permute-start | bytes 196616 | tf_op jit(solution)/shard_map/ppermute | solution.py:269
  156.1 5.6 %collective-permute-start.63 = (bf16[256,128]{1,0:T(8,128)(2,1)S(1)}, bf16[256,128]{1,0:T(8,128)(2,1)S(1)}, u32[]{:S(2)}, u32[]{:S(2)}) collective-permute-start(bf16[256,128]{1,0:T(8,128)(2,1)S(1)} %get-tuple-element.55), channel_id=1, source_target_pairs={{0,32},{1,33},{2,34},{3,35},{4,36},{5,37},{6,38},{7,39},{8,40},{9,... | collective-permute-start | bytes 196616 | tf_op jit(solution)/shard_map/ppermute | solution.py:269
  164.2 5.8 %collective-permute-start.67 = (bf16[256,128]{1,0:T(8,128)(2,1)S(1)}, bf16[256,128]{1,0:T(8,128)(2,1)S(1)}, u32[]{:S(2)}, u32[]{:S(2)}) collective-permute-start(bf16[256,128]{1,0:T(8,128)(2,1)S(1)} %solve.12), channel_id=1, source_target_pairs={{0,4},{1,25},{2,6},{3,27},{4,0},{5,29},{6,2},{7,31},{8,12},{9,1},{... | collective-permute-start | bytes 196616 | tf_op jit(solution)/shard_map/ppermute | solution.py:262
  165.2 5.6 %collective-permute-start.66 = (bf16[256,128]{1,0:T(8,128)(2,1)S(1)}, bf16[256,128]{1,0:T(8,128)(2,1)S(1)}, u32[]{:S(2)}, u32[]{:S(2)}) collective-permute-start(bf16[256,128]{1,0:T(8,128)(2,1)S(1)} %solve.12), channel_id=1, source_target_pairs={{0,2},{1,17},{2,4},{3,19},{4,6},{5,21},{6,0},{7,23},{8,10},{9,25},... | collective-permute-start | bytes 196616 | tf_op jit(solution)/shard_map/ppermute | solution.py:262
  171.6 8.0 %collective-permute-start.70 = (bf16[4,256,128]{2,1,0:T(8,128)(2,1)S(1)}, bf16[4,256,128]{2,1,0:T(8,128)(2,1)S(1)}, u32[]{:S(2)}, u32[]{:S(2)}) collective-permute-start(bf16[4,256,128]{2,1,0:T(8,128)(2,1)S(1)} %pad_maximum_fusion.4.refs_0_), channel_id=1, source_target_pairs={{0,16},{1,5},{2,18},{3,7},{4,20},{5,1},{6,22},{7,3},{8,24},{9,13},... | collective-permute-start | bytes 786440 | tf_op jit(solution)/shard_map/ppermute | solution.py:264
  173.1 8.4 %collective-permute-start.69 = (bf16[4,256,128]{2,1,0:T(8,128)(2,1)S(1)}, bf16[4,256,128]{2,1,0:T(8,128)(2,1)S(1)}, u32[]{:S(2)}, u32[]{:S(2)}) collective-permute-start(bf16[4,256,128]{2,1,0:T(8,128)(2,1)S(1)} %pad_maximum_fusion.4.refs_0_), channel_id=1, source_target_pairs={{0,24},{1,7},{2,26},{3,1},{4,28},{5,3},{6,30},{7,5},{8,0},{9,15},{... | collective-permute-start | bytes 786440 | tf_op jit(solution)/shard_map/ppermute | solution.py:264
  175.2 7.6 %collective-permute-start.68 = (bf16[4,256,128]{2,1,0:T(8,128)(2,1)S(1)}, bf16[4,256,128]{2,1,0:T(8,128)(2,1)S(1)}, u32[]{:S(2)}, u32[]{:S(2)}) collective-permute-start(bf16[4,256,128]{2,1,0:T(8,128)(2,1)S(1)} %pad_maximum_fusion.4.refs_0_), channel_id=1, source_target_pairs={{0,8},{1,3},{2,10},{3,5},{4,12},{5,7},{6,14},{7,1},{8,16},{9,11},{... | collective-permute-start | bytes 786440 | tf_op jit(solution)/shard_map/ppermute | solution.py:264
  175.2 7.6 %collective-permute-start.71 = (bf16[4,256,128]{2,1,0:T(8,128)(2,1)S(1)}, bf16[4,256,128]{2,1,0:T(8,128)(2,1)S(1)}, u32[]{:S(2)}, u32[]{:S(2)}) collective-permute-start(bf16[4,256,128]{2,1,0:T(8,128)(2,1)S(1)} %pad_maximum_fusion.4.refs_0_), channel_id=1, source_target_pairs={{0,1},{1,0},{2,3},{3,2},{4,5},{5,4},{6,7},{7,6},{8,9},{9,8},{10,11... | collective-permute-start | bytes 786440 | tf_op jit(solution)/shard_map/ppermute | solution.py:265
  185.1 6.5 %collective-permute-start.75 = (bf16[256,128]{1,0:T(8,128)(2,1)S(1)}, bf16[256,128]{1,0:T(8,128)(2,1)S(1)}, u32[]{:S(2)}, u32[]{:S(2)}) collective-permute-start(bf16[256,128]{1,0:T(8,128)(2,1)S(1)} %get-tuple-element.59), channel_id=1, source_target_pairs={{0,64},{1,65},{2,66},{3,67},{4,68},{5,69},{6,70},{7,71},{8,72},{9,... | collective-permute-start | bytes 196616 | tf_op jit(solution)/shard_map/ppermute | solution.py:269
  186.9 5.6 %collective-permute-start.76 = (bf16[256,128]{1,0:T(8,128)(2,1)S(1)}, bf16[256,128]{1,0:T(8,128)(2,1)S(1)}, u32[]{:S(2)}, u32[]{:S(2)}) collective-permute-start(bf16[256,128]{1,0:T(8,128)(2,1)S(1)} %get-tuple-element.60), channel_id=1, source_target_pairs={{0,32},{1,33},{2,34},{3,35},{4,36},{5,37},{6,38},{7,39},{8,40},{9,... | collective-permute-start | bytes 196616 | tf_op jit(solution)/shard_map/ppermute | solution.py:269
  (39 other events, 264.9 us)
